TPU v7x, 32 devices: a whole 2x2x4 slice. The times are simulated.
32 devices in a mesh: wide: 8 (over z, y), narrow: 4 (over x, core).
Axes of the slice: x: 2, y: 2, z: 4, core: 2. Of those that a mesh axis runs over, the one named last changes fastest.
Arguments:
- features: bfloat16 [768, 65536], P('narrow', 'wide'), may hold values from -6 to 6
- owner_of: int32 [4096, 16, 1], P('wide'), may hold values from 0 to 7; in each aligned block of 8192 rows (0 to 8191, 8192 to 16383, ..., all dimensions but the last counted through in order) at most 1536 rows name the same one
- row_of: int32 [4096, 16], P('wide'), may hold values from 0 to 8191
- w_self: bfloat16 [768, 256], P('narrow'), may hold values from -0.15625 to 0.15625
- w_neighbor: bfloat16 [768, 256], P('narrow'), may hold values from -0.15625 to 0.15625
- cotangent: bfloat16 [4096, 256], P(('wide', 'narrow')), may hold values from -0.09375 to 0.09375
Outputs:
- hidden: bfloat16 [4096, 256], P(('wide', 'narrow'))
- grad_self: float32 [768, 256], P('narrow')
- grad_neighbor: float32 [768, 256], P('narrow')
Inputs may be any that keep to these rules, and one draw needn't show every extreme that they name: `owner_of`: among the 8192 rows read by the targets of one index of wide, no owner is named more than 1536 times, and in every draw some owner is named exactly 1536 times by some index.
All inputs are finite; a program needn't handle non-finite values.
Results may differ from a plain program's by a relative error of at most 0.0054.
Values may be sent and summed in bfloat16 or wider, within the bound.
No kernel may reach another device: no remote copies, remote signals or barrier semaphores. Data moves between devices by JAX's collectives and lax.ppermute only.
A program may use at most 64 MiB of HBM per device.

v0:
```python
import jax
import jax.numpy as jnp
from jax import lax
from jax.sharding import PartitionSpec as P

FANOUT = 15


def activation(value):
    return jax.nn.gelu(value, approximate=True)


def contract_rows(left, right):
    return lax.dot_general(
        left, right, (((0,), (0,)), ((), ())), preferred_element_type=jnp.float32
    )


def slot_numbers(owners, wide_count, total):
    block_rows = 128
    block_count = total // block_rows
    onehot = (owners[:, None] == jnp.arange(wide_count, dtype=jnp.int32)[None, :]).astype(
        jnp.float32
    )
    blocked = onehot.reshape(block_count, block_rows, wide_count)
    lower = (jnp.arange(block_rows)[:, None] > jnp.arange(block_rows)[None, :]).astype(jnp.float32)
    within = jnp.einsum("ij,bjw->biw", lower, blocked, precision=lax.Precision.HIGHEST)
    block_sums = jnp.sum(blocked, axis=1)
    offsets = jnp.cumsum(block_sums, axis=0) - block_sums
    prefix = within + offsets[:, None, :]
    return jnp.sum(prefix * blocked, axis=2).reshape(total).astype(jnp.int32)


def on_device(features, owner_of, row_of, w_self, w_neighbor, cotangent):
    wide_count = lax.axis_size("wide")
    tgt_rows, request_count = row_of.shape
    feat_cols = features.shape[0]
    total = tgt_rows * request_count
    capacity = max(2, 3 * total // (2 * wide_count))
    owners = owner_of.reshape(total)
    wanted = row_of.reshape(total)
    slot_of = slot_numbers(owners, wide_count, total)
    flat_slot = owners * capacity + slot_of
    buffer = (
        jnp.zeros((wide_count * capacity,), jnp.int32)
        .at[flat_slot]
        .set(wanted)
        .reshape(wide_count, capacity)
    )
    table = jnp.transpose(features)
    found = jnp.take(
        table, lax.all_to_all(buffer, "wide", split_axis=0, concat_axis=0, tiled=True), axis=0
    )
    fetched = lax.all_to_all(found, "wide", split_axis=0, concat_axis=0, tiled=True)
    flat_fetched = fetched.reshape(wide_count * capacity, feat_cols)
    gathered = jnp.take(flat_fetched, flat_slot, axis=0).reshape(tgt_rows, request_count, feat_cols)
    self_rows = gathered[:, 0]
    pooled = (jnp.sum(gathered[:, 1:], axis=1, dtype=jnp.float32) / FANOUT).astype(jnp.bfloat16)
    preact = lax.psum_scatter(
        jnp.dot(self_rows, w_self, preferred_element_type=jnp.float32)
        + jnp.dot(pooled, w_neighbor, preferred_element_type=jnp.float32),
        "narrow",
        scatter_dimension=0,
        tiled=True,
    )
    value, pullback = jax.vjp(activation, preact)
    hidden = value.astype(jnp.bfloat16)
    slope_share = pullback(cotangent.astype(jnp.float32))[0].astype(jnp.bfloat16)
    slope = lax.all_gather(slope_share, "narrow", axis=0, tiled=True)
    grad_self, grad_neighbor = lax.psum(
        (contract_rows(self_rows, slope), contract_rows(pooled, slope)), "wide"
    )
    return (hidden, grad_self, grad_neighbor)


def solution(mesh):
    return jax.shard_map(
        on_device,
        mesh=mesh,
        in_specs=(
            P("narrow", "wide"),
            P("wide", None, None),
            P("wide", None),
            P("narrow", None),
            P("narrow", None),
            P(("wide", "narrow"), None),
        ),
        out_specs=(P(("wide", "narrow"), None), P("narrow", None), P("narrow", None)),
        check_vma=False,
    )
```

profile of v0, /device:TPU:0, one launch (start us, length us, event | category | flops | bytes accessed | tf_op | source)
XLA Modules:
  0.0 394.3 jit_solution(16413855901795440808)
XLA Ops:
  7.2 0.0 copy-start
  7.2 0.8 copy_multiply_fusion
  8.0 0.9 copy.26
  8.9 0.1 copy.28
  9.0 0.2 mul.73
  9.2 0.9 copy.29
  10.0 0.1 reshape.155
  10.2 0.1 eq.17
  10.3 0.1 convert_reduce_fusion.1
  10.5 0.1 reduce_window_sum.11
  10.6 0.3 fusion.2
  10.8 0.1 compare_select_fusion.1
  10.9 31.1 %scatter_custom_fusion = s32[12288]{0:T(1024)} fusion(s32[8192]{0:T(1024)S(1)} %bitcast.48, s32[8192]{0:T(1024)S(1)} %reshape.155, s32[]{:T(128)} %constant.26.clone.1), kind=kCustom, calls=%fused_computation.45 | custom fusion | bytes 49156 | tf_op jit(solution)/shard_map/scatter | solution.py:47
  42.0 7.3 %all-to-all-start = ((s32[8,1,1536]{2,1,0:T(1,128)}), s32[8,1,1536]{2,1,0:T(1,128)S(1)}, u32[]{:S(2)}, u32[]{:S(2)}) async-start(s32[8,1,1536]{2,1,0:T(1,128)} %bitcast.5), calls=%async_computation | async-start | bytes 98304 | tf_op jit(solution)/shard_map/all_to_all | solution.py:52
  49.2 5.9 %copy.30 = bf16[192,8192]{0,1:T(8,128)(2,1)} copy(bf16[192,8192]{1,0:T(8,128)(2,1)} %param.6) | data formatting | bytes 6291456 | tf_op args[0]
  55.2 0.9 all-to-all-done
  56.0 0.1 compare_select_fusion
  56.1 48.5 %gather_fusion = bf16[12288,192]{1,0:T(8,128)(2,1)} fusion(bf16[8192,192]{1,0:T(8,128)(2,1)} %bitcast.42, s32[12288]{0:T(1024)S(1)} %broadcast_clamp_fusion), kind=kCustom, calls=%fused_computation | custom fusion | bytes 9486336 | tf_op jit(solution)/shard_map/jit(_take)/gather | solution.py:51
  104.6 8.0 %copy.31 = bf16[8,1536,192]{1,2,0:T(8,128)(2,1)} copy(bf16[8,1536,192]{2,1,0:T(8,128)(2,1)} %bitcast.44) | data formatting | bytes 9437184 | tf_op jit(solution)/shard_map/jit(_take)/gather | solution.py:51
  112.6 4.9 %broadcast_select_fusion = bf16[8,1536,192]{1,2,0:T(8,128)(2,1)} fusion(bf16[8,1536,192]{1,2,0:T(8,128)(2,1)} %copy.31, pred[8,1536]{1,0:T(8,128)(4,1)S(1)} %compare_and_fusion), kind=kLoop, calls=%fused_computation.4 | loop fusion | flops 2359296 | bytes 9449472 | tf_op jit(solution)/shard_map/jit(_take)/select_n | solution.py:51
  117.6 5.3 %all-to-all-start.1 = ((bf16[8,1536,192]{1,2,0:T(8,128)(2,1)}), bf16[8,1536,192]{1,2,0:T(8,128)(2,1)}, u32[]{:S(2)}, u32[]{:S(2)}) async-start(bf16[8,1536,192]{1,2,0:T(8,128)(2,1)} %broadcast_select_fusion), calls=%async_computation.1 | async-start | bytes 9437184 | tf_op jit(solution)/shard_map/all_to_all | solution.py:54
  122.8 0.0 reduce-scatter.2.cloned.1.call-start
  122.9 0.1 convert_element_type.41
  123.0 0.1 copy.27
  123.1 0.0 copy-done.2
  123.2 103.6 %all-to-all-done.1 = bf16[8,1536,192]{1,2,0:T(8,128)(2,1)} async-done(((bf16[8,1536,192]{1,2,0:T(8,128)(2,1)}), bf16[8,1536,192]{1,2,0:T(8,128)(2,1)}, u32[]{:S(2)}, u32[]{:S(2)}) %all-to-all-start.1) | async-done | bytes 4718624 | tf_op jit(solution)/shard_map/all_to_all | solution.py:54
  226.8 7.9 %copy.32 = bf16[8,1536,192]{2,1,0:T(8,128)(2,1)} copy(bf16[8,1536,192]{1,2,0:T(8,128)(2,1)} %all-to-all-done.1) | data formatting | bytes 9437184 | tf_op jit(solution)/shard_map/all_to_all | solution.py:54
  234.7 34.5 %gather_fusion.1 = bf16[8192,192]{1,0:T(8,128)(2,1)} fusion(bf16[12288,192]{1,0:T(8,128)(2,1)} %bitcast.43, s32[8192]{0:T(1024)S(1)} %broadcast_clamp_fusion.1), kind=kCustom, calls=%fused_computation.1 | custom fusion | bytes 6324224 | tf_op jit(solution)/shard_map/jit(_take)/gather | solution.py:56
  269.2 7.7 %copy.33 = bf16[512,16,192]{0,2,1:T(8,128)(2,1)} copy(bf16[512,16,192]{2,1,0:T(8,128)(2,1)} %bitcast.45) | data formatting | bytes 6291456 | tf_op jit(solution)/shard_map/jit(_take)/gather | solution.py:56
  277.0 2.2 broadcast_select_fusion.1
  279.2 0.0 copy-start.4
  279.2 0.4 convert_reduce_fusion
  279.6 0.0 copy-done
  279.6 0.0 copy-start.1
  279.6 0.3 fusion.4
  279.9 0.5 copy-done.1
  280.4 1.1 convolution_add_fusion
  281.4 0.0 reduce-scatter.2.cloned.1.call-update
  281.5 0.0 all-reduce.3.cloned.1.call-start
  281.5 20.8 %reduce-scatter.2.cloned.1.call-done = f32[128,256]{1,0:T(8,128)} async-done(((f32[512,256]{1,0:T(8,128)}), f32[128,256]{1,0:T(8,128)}) %reduce-scatter.2.cloned.1.call-update) | async-done | bytes 131088 | tf_op jit(solution)/shard_map/reduce_scatter | solution.py:59
  302.3 1.6 fusion.7
  304.0 5.8 %all_gather.3 = bf16[512,256]{1,0:T(8,128)(2,1)S(1)} all-gather(bf16[128,256]{1,0:T(8,128)(2,1)S(1)} %get-tuple-element.5), channel_id=1, replica_groups=mesh['wide'=8,'narrow'=4] {'narrow'}, dimensions={0}, use_global_device_ids=true | all-gather | bytes 327680 | tf_op jit(solution)/shard_map/all_gather | solution.py:69
  309.7 0.9 fusion.3
  310.6 1.9 fusion.16
  312.5 0.0 all-reduce.3.cloned.1.call-update
  312.5 71.7 %all-reduce.3.cloned.1.call-done = (f32[192,256]{1,0:T(8,128)}, f32[192,256]{1,0:T(8,128)}) async-done(((f32[192,256]{1,0:T(8,128)}, f32[192,256]{1,0:T(8,128)}), (f32[192,256]{1,0:T(8,128)}, f32[192,256]{1,0:T(8,128)})) %all-reduce.3.cloned.1.call-update) | async-done | bytes 393232 | tf_op jit(solution)/shard_map/psum | solution.py:70
  384.2 1.6 copy.43
  385.8 1.6 copy.44
  (10 shorter events, 0.1 us)
Async XLA Ops:
  7.2 272.5 %copy-start = (bf16[192,256]{1,0:T(8,128)(2,1)S(1)}, bf16[192,256]{1,0:T(8,128)(2,1)}, u32[]{:S(2)}) copy-start(bf16[192,256]{1,0:T(8,128)(2,1)} %param.9) | copy-start | bytes 294916
  42.0 14.1 %all-to-all-start = ((s32[8,1,1536]{2,1,0:T(1,128)}), s32[8,1,1536]{2,1,0:T(1,128)S(1)}, u32[]{:S(2)}, u32[]{:S(2)}) async-start(s32[8,1,1536]{2,1,0:T(1,128)} %bitcast.5), calls=%async_computation | async-start | bytes 98304 | tf_op jit(solution)/shard_map/all_to_all | solution.py:52
  117.6 5.5 %copy-start.2 = (s32[512,16,1]{0,2,1:T(1,128)S(1)}, s32[512,16,1]{0,2,1:T(1,128)}, u32[]{:S(2)}) copy-start(s32[512,16,1]{0,2,1:T(1,128)} %param.7) | copy-start | bytes 98308
  117.6 109.2 %all-to-all-start.1 = ((bf16[8,1536,192]{1,2,0:T(8,128)(2,1)}), bf16[8,1536,192]{1,2,0:T(8,128)(2,1)}, u32[]{:S(2)}, u32[]{:S(2)}) async-start(bf16[8,1536,192]{1,2,0:T(8,128)(2,1)} %broadcast_select_fusion), calls=%async_computation.1 | async-start | bytes 9437184 | tf_op jit(solution)/shard_map/all_to_all | solution.py:54
  122.8 179.5 %reduce-scatter.2.cloned.1.call-start = ((), (), s32[]{:S(2)}) async-start(), calls=%async_computation.3 | async-start | bytes 655360 | tf_op jit(solution)/shard_map/reduce_scatter | solution.py:59
  277.0 3.4 copy-start.3
  279.2 23.2 %copy-start.4 = (bf16[128,256]{1,0:T(8,128)(2,1)S(1)}, bf16[128,256]{1,0:T(8,128)(2,1)}, u32[]{:S(2)}) copy-start(bf16[128,256]{1,0:T(8,128)(2,1)} %param.11) | copy-start | bytes 196612
  279.6 0.7 copy-start.1
  281.5 102.7 %all-reduce.3.cloned.1.call-start = ((), (), s32[]{:S(2)}) async-start(), calls=%async_computation.4 | async-start | bytes 786432 | tf_op jit(solution)/shard_map/psum | solution.py:70
Sparse Core Ops, SparseCore 0:
  281.6 20.7 reduce-scatter.1
  312.7 71.4 all-reduce.2
where the time goes:
time: 396 us; the launch traced here: 394 us
  waiting for transfers between devices  197 us (50%)
  local copies, waits for them, and re-layouts  150 us (38%)
  between operations  14.2 us (4%)
  starting transfers between devices  12.6 us (3%)
  other arithmetic  10.4 us (3%)
  blocking collectives  5.77 us (1%)
  matrix products  4.36 us (1%)
    all_to_all x1, waiting for transfers between devices, on_device(): lax.all_to_all(found, 'wide', split_axis=0, concat_axis=0, tiled=True)  104 us
    psum x1, waiting for transfers between devices, on_device(): lax.psum((contract_rows(self_rows, slope), contract_rows(pooled, slope)),...  71.7 us
    gather x2, local copies, waits for them, and re-layouts, on_device(): jnp.take(table, lax.all_to_all(buffer, 'wide', split_axis=0, concat_axis=...  56.5 us
    gather x2, local copies, waits for them, and re-layouts, on_device(): jnp.take(flat_fetched, flat_slot, axis=0)  42.2 us
    scatter x1, local copies, waits for them, and re-layouts, on_device(): buffer = jnp.zeros((wide_count * capacity,), jnp.int32).at[flat_slot].set...  31.1 us
    reduce_scatter x1, waiting for transfers between devices, on_device(): lax.psum_scatter(jnp.dot(self_rows, w_self, preferred_element_type=jnp.fl...  20.8 us
    unnamed x15, local copies, waits for them, and re-layouts  11.4 us
    all_to_all x1, local copies, waits for them, and re-layouts, on_device(): lax.all_to_all(found, 'wide', split_axis=0, concat_axis=0, tiled=True)  7.95 us
  transfers between devices with their start and end apart: 4, of which 4 were waited for; matrix products, arithmetic and copies ran while one was open for 2% of the time, Pallas kernels for 0%

commit v1 on v0

v1 whole, which is shorter than its diff:
```python
import functools

import jax
import jax.numpy as jnp
from jax import lax
from jax.experimental import pallas as pl
from jax.experimental.pallas import tpu as pltpu
from jax.sharding import PartitionSpec as P

FANOUT = 15
BF16 = jnp.bfloat16
F32 = jnp.float32
VMEM_BYTES = 56 * 1024 * 1024


def activation(value):
    return jax.nn.gelu(value, approximate=True)


def contract_rows(left, right):
    return lax.dot_general(
        left, right, (((0,), (0,)), ((), ())), preferred_element_type=F32
    )


def list_kernel(wide_count, capacity, row_bits, tgt_bits, owner_ref, row_ref, out_ref):
    requests, targets = owner_ref.shape
    hi_count = out_ref.shape[0]
    owners = owner_ref[...]
    masks = jnp.concatenate(
        [jnp.where(owners == w, 1.0, 0.0).astype(BF16) for w in range(wide_count)], axis=0
    )
    lanes = lax.broadcasted_iota(jnp.int32, (targets, targets), 1)
    upper = jnp.where(lax.broadcasted_iota(jnp.int32, (targets, targets), 0) < lanes, 1.0, 0.0)
    within = jnp.dot(masks, upper.astype(BF16), preferred_element_type=F32)
    total = wide_count * requests
    first = lax.broadcasted_iota(jnp.int32, (total, total), 0)
    second = lax.broadcasted_iota(jnp.int32, (total, total), 1)
    lower = jnp.where((second < first) & (second >= first - first % requests), 1.0, 0.0)
    before = jnp.dot(lower.astype(BF16), masks, preferred_element_type=F32)
    offset = jnp.sum(before, axis=1, keepdims=True)
    ranked = masks.astype(F32) * (within + offset)
    slot = jnp.zeros(owners.shape, F32)
    for w in range(wide_count):
        slot = slot + ranked[w * requests : (w + 1) * requests]
    position = owners * capacity + slot.astype(jnp.int32)
    high = position >> 7
    low = position & 127
    target = lax.broadcasted_iota(jnp.int32, owners.shape, 1)
    kind = jnp.where(lax.broadcasted_iota(jnp.int32, owners.shape, 0) == 0, 0, 1)
    code = row_ref[...] | ((target | ((kind | 2) << tgt_bits)) << row_bits)
    parts = [(code & 255).astype(F32), ((code >> 8) & 255).astype(F32), (code >> 16).astype(F32)]
    high_iota = lax.broadcasted_iota(jnp.int32, (hi_count, targets), 0)
    low_iota = lax.broadcasted_iota(jnp.int32, (128, targets), 0)
    sums = jnp.zeros((hi_count, 384), F32)
    for j in range(requests):
        left = jnp.where(high_iota == high[j : j + 1], 1.0, 0.0).astype(BF16)
        hit = low_iota == low[j : j + 1]
        right = jnp.concatenate(
            [jnp.where(hit, part[j : j + 1], 0.0).astype(BF16) for part in parts], axis=0
        )
        sums = sums + lax.dot_general(
            left, right, (((1,), (1,)), ((), ())), preferred_element_type=F32
        )
    out_ref[...] = (sums[:, :128] + sums[:, 128:256] * 256.0 + sums[:, 256:] * 65536.0).astype(
        jnp.int32
    )


def table_kernel(feature_ref, out_ref):
    block = feature_ref[...].astype(F32)
    rest = block[128:]
    out_ref[0] = jnp.transpose(block[:128])
    out_ref[1] = jnp.transpose(jnp.concatenate([rest, rest], axis=0))


def owner_kernel(unroll, rows_ref, place_ref, key_ref, table_ref, weight_ref,
                 keep_ref, send_ref, sums_ref, held, dense):
    source = pl.program_id(0)
    capacity = held.shape[1]
    targets = 128
    quarters = 4
    table = table_ref.reshape(2, table_ref.shape[1], 1, 128)
    base = source * capacity

    def fetch(step, carry):
        for u in range(unroll):
            i = step * unroll + u
            r = rows_ref[base + i]
            held[0, i] = table[0, r]
            held[1, i] = table[1, r]
        return carry

    lax.fori_loop(0, capacity // unroll, fetch, 0)
    flat = held.reshape(2, capacity, 128)
    dense[:, :128] = flat[0].astype(BF16)
    dense[:, 128:] = flat[1].astype(BF16)
    lane = lax.broadcasted_iota(jnp.int32, (targets, 128), 1)
    narrow = place_ref[0]

    def quarter(q, carry):
        row = lax.broadcasted_iota(jnp.int32, (2 * targets, capacity), 0)
        wanted = jnp.where(row < targets, row, row + (quarters - 1) * targets) + q * targets
        onehot = jnp.where(wanted == key_ref[0], 1.0, 0.0).astype(BF16)
        both = jnp.dot(onehot, dense[...], preferred_element_type=F32)
        own = both[:targets]
        mean = both[targets:] / FANOUT
        mid = jnp.where(lane < 64, own[:, 128:], mean[:, 128:])
        summed = jnp.concatenate([own[:, :128], mid, mean[:, :128]], axis=1).astype(BF16)
        preact = jnp.dot(summed, weight_ref[...], preferred_element_type=F32).astype(BF16)
        other = q ^ narrow
        core = other & 1
        chip = other >> 1
        sums_ref[2 * core + chip, 0] = summed

        @pl.when(core == 0)
        def _():
            keep_ref[chip, 0] = preact

        @pl.when(core == 1)
        def _():
            send_ref[chip, 0] = preact

        return carry

    lax.fori_loop(0, quarters, quarter, 0)


def swap(value, axis, bit):
    count = lax.axis_size(axis)
    return lax.ppermute(value, axis, [(i, i ^ bit) for i in range(count)])


def on_device(features, owner_of, row_of, w_self, w_neighbor, cotangent):
    wide_count = lax.axis_size("wide")
    targets, requests = row_of.shape
    columns, nodes = features.shape
    hidden_units = w_self.shape[1]
    total = targets * requests
    capacity = max(2, 3 * total // (2 * wide_count))
    row_bits = (nodes - 1).bit_length()
    tgt_bits = (targets - 1).bit_length()
    share = targets // 4

    lists = pl.pallas_call(
        functools.partial(list_kernel, wide_count, capacity, row_bits, tgt_bits),
        out_shape=jax.ShapeDtypeStruct((wide_count * capacity // 128, 128), jnp.int32),
        compiler_params=pltpu.CompilerParams(vmem_limit_bytes=VMEM_BYTES),
        name="lists",
    )(jnp.transpose(owner_of.reshape(targets, requests)), jnp.transpose(row_of))
    asked = lax.all_to_all(
        lists.reshape(wide_count, capacity), "wide", split_axis=0, concat_axis=0, tiled=True
    )

    block = 1024
    table = pl.pallas_call(
        table_kernel,
        grid=(nodes // block,),
        in_specs=[pl.BlockSpec((columns, block), lambda i: (0, i))],
        out_specs=pl.BlockSpec((2, block, 128), lambda i: (0, i, 0)),
        out_shape=jax.ShapeDtypeStruct((2, nodes, 128), F32),
        cost_estimate=pl.CostEstimate(flops=0, bytes_accessed=24 * 1024 * 1024, transcendentals=0),
        name="table",
    )(features)

    rows = (asked & (nodes - 1)).reshape(wide_count * capacity)
    tail = asked >> row_bits
    keys = jnp.where(tail >= 2 * targets, tail - 2 * targets, -1).reshape(wide_count, 1, capacity)
    weights = jnp.concatenate(
        [w_self[:128], w_self[128:], w_neighbor[128:], w_neighbor[:128]], axis=0
    )
    unroll = next(u for u in (64, 32, 16, 8, 4, 2, 1) if capacity % u == 0)
    place = lax.axis_index("narrow").astype(jnp.int32).reshape(1)
    halves = jax.ShapeDtypeStruct((2, wide_count, share, hidden_units), BF16)
    keep, send, sums = pl.pallas_call(
        functools.partial(owner_kernel, unroll),
        grid_spec=pltpu.PrefetchScalarGridSpec(
            num_scalar_prefetch=2,
            grid=(wide_count,),
            in_specs=[
                pl.BlockSpec((1, 1, capacity), lambda s, *_: (s, 0, 0)),
                pl.BlockSpec((2, nodes, 128), lambda s, *_: (0, 0, 0)),
                pl.BlockSpec((2 * columns, hidden_units), lambda s, *_: (0, 0)),
            ],
            out_specs=[
                pl.BlockSpec((2, 1, share, hidden_units), lambda s, *_: (0, s, 0, 0)),
                pl.BlockSpec((2, 1, share, hidden_units), lambda s, *_: (0, s, 0, 0)),
                pl.BlockSpec((4, 1, share, 2 * columns), lambda s, *_: (0, s, 0, 0)),
            ],
            scratch_shapes=[
                pltpu.VMEM((2, capacity, 1, 128), F32),
                pltpu.VMEM((capacity, 256), BF16),
            ],
        ),
        out_shape=[
            halves,
            halves,
            jax.ShapeDtypeStruct((4, wide_count, share, 2 * columns), BF16),
        ],
        compiler_params=pltpu.CompilerParams(vmem_limit_bytes=VMEM_BYTES),
        name="owner",
    )(rows, place, keys, table, weights)

    paired = keep.astype(F32) + swap(send, "narrow", 1).astype(F32)
    quartet = paired[0] + swap(paired[1].astype(BF16), "narrow", 2).astype(F32)
    pieces = lax.all_to_all(
        quartet.astype(BF16), "wide", split_axis=0, concat_axis=0, tiled=True
    )
    preact = jnp.sum(pieces.astype(F32), axis=0)
    value, pullback = jax.vjp(activation, preact)
    hidden = value.astype(BF16)
    slope = pullback(cotangent.astype(F32))[0].astype(BF16)

    slopes = lax.all_to_all(
        jnp.broadcast_to(slope[None], (wide_count, share, hidden_units)),
        "wide", split_axis=0, concat_axis=0, tiled=True,
    )
    across = swap(slopes, "narrow", 2)
    both = jnp.stack([slopes, across])
    beside = swap(both, "narrow", 1)
    rows_per = wide_count * share
    grads = contract_rows(
        sums[:2].reshape(2 * rows_per, 2 * columns), both.reshape(2 * rows_per, hidden_units)
    ) + contract_rows(
        sums[2:].reshape(2 * rows_per, 2 * columns), beside.reshape(2 * rows_per, hidden_units)
    )
    slices = grads.astype(BF16).reshape(wide_count, 2 * columns // wide_count, hidden_units)
    own = jnp.sum(
        lax.all_to_all(slices, "wide", split_axis=0, concat_axis=0, tiled=True).astype(F32), axis=0
    ).astype(BF16)
    full = lax.all_to_all(
        jnp.broadcast_to(own[None], slices.shape), "wide", split_axis=0, concat_axis=0, tiled=True
    ).reshape(2 * columns, hidden_units).astype(F32)
    grad_self = full[:columns]
    grad_neighbor = jnp.concatenate([full[columns + 64 :], full[columns : columns + 64]], axis=0)
    return (hidden, grad_self, grad_neighbor)


def solution(mesh):
    return jax.shard_map(
        on_device,
        mesh=mesh,
        in_specs=(
            P("narrow", "wide"),
            P("wide", None, None),
            P("wide", None),
            P("narrow", None),
            P("narrow", None),
            P(("wide", "narrow"), None),
        ),
        out_specs=(P(("wide", "narrow"), None), P("narrow", None), P("narrow", None)),
        check_vma=False,
    )
```

time: 396 us -> 160 us (0.40)
  waiting for transfers between devices: 197 us -> 28.8 us
  local copies, waits for them, and re-layouts: 150 us -> 2.21 us
  blocking collectives: 5.77 us -> 60.7 us
  Pallas kernels: 0 us -> 50.6 us
  between operations: 14.2 us -> 0.77 us
  other arithmetic: 10.4 us -> 4.71 us
    all_to_all x2 -> x1, waiting for transfers between devices: 105 us -> 0.01 us  [on_device(): lax.all_to_all(lists.reshape(wide_count, capacity), 'wide', split_axis=0,...]
    gather x4 -> x0, local copies, waits for them, and re-layouts: 98.7 us -> none  [the longest x2 56.5 us: on_device(): jnp.take(table, lax.all_to_all(buffer, 'wide', split_axis=0, concat_axis=...]
    psum x1 -> x0, waiting for transfers between devices: 71.7 us -> none  [on_device(): lax.psum((contract_rows(self_rows, slope), contract_rows(pooled, slope)),...]
    all_to_all x0 -> x4, blocking collectives: none -> 60.7 us  [the longest x1 20 us: on_device(): lax.all_to_all(quartet.astype(BF16), 'wide', split_axis=0, concat_axis=0,...]
    pallas_call x0 -> x3, Pallas kernels: none -> 50.6 us  [the longest x1 39.1 us: on_device(): pl.pallas_call(functools.partial(owner_kernel, unroll), grid_spec=pltpu.P...]
    scatter x1 -> x0, local copies, waits for them, and re-layouts: 31.1 us -> none  [on_device(): buffer = jnp.zeros((wide_count * capacity,), jnp.int32).at[flat_slot].set...]
    ppermute x0 -> x4, waiting for transfers between devices: none -> 28.8 us  [swap(): return lax.ppermute(value, axis, [(i, i ^ bit) for i in range(count)])]
    reduce_scatter x1 -> x0, waiting for transfers between devices: 20.8 us -> none  [on_device(): lax.psum_scatter(jnp.dot(self_rows, w_self, preferred_element_type=jnp.fl...]
  transfers between devices with their start and end apart: 4 -> 5, of which waited for: 4 -> 4; matrix products, arithmetic and copies ran while one was open for 2% -> 0% of each run, Pallas kernels for 0% -> 5%
where the time goes in v1:
time: 160 us; the launch traced here: 159 us
  blocking collectives  60.7 us (38%)
  Pallas kernels  50.6 us (32%)
  waiting for transfers between devices  28.8 us (18%)
  starting transfers between devices  10.4 us (6%)
  other arithmetic  4.71 us (3%)
  local copies, waits for them, and re-layouts  2.21 us (1%)
    pallas_call x1, Pallas kernels, on_device(): pl.pallas_call(functools.partial(owner_kernel, unroll), grid_spec=pltpu.P...  39.1 us
    ppermute x4, waiting for transfers between devices, swap(): return lax.ppermute(value, axis, [(i, i ^ bit) for i in range(count)])  28.8 us
    all_to_all x1, blocking collectives, on_device(): lax.all_to_all(quartet.astype(BF16), 'wide', split_axis=0, concat_axis=0,...  20 us
    all_to_all x1, blocking collectives, on_device(): lax.all_to_all(jnp.broadcast_to(slope[None], (wide_count, share, hidden_u...  17.4 us
    all_to_all x1, blocking collectives, on_device(): lax.all_to_all(slices, 'wide', split_axis=0, concat_axis=0, tiled=True)  12.5 us
    all_to_all x1, blocking collectives, on_device(): lax.all_to_all(jnp.broadcast_to(own[None], slices.shape), 'wide', split_a...  10.7 us
    pallas_call x1, Pallas kernels, on_device(): pl.pallas_call(table_kernel, grid=(nodes // block,), in_specs=[pl.BlockSp...  7.69 us
    all_to_all x1, starting transfers between devices, on_device(): lax.all_to_all(lists.reshape(wide_count, capacity), 'wide', split_axis=0,...  7.27 us
  transfers between devices with their start and end apart: 5, of which 4 were waited for; matrix products, arithmetic and copies ran while one was open for 0% of the time, Pallas kernels for 5%

profile of v1, /device:TPU:0, one launch (start us, length us, event | category | flops | bytes accessed | tf_op | source)
XLA Modules:
  0.0 159.4 jit_solution(9579737816698962906)
XLA Ops:
  0.6 1.4 copy.17
  2.0 3.8 %lists.1 = s32[96,128]{1,0:T(8,128)} custom-call(s32[16,512]{1,0:T(8,128)} %bitcast.47, s32[16,512]{1,0:T(8,128)} %bitcast.48), custom_call_target="tpu_custom_call" | custom-call | tf_op jit(solution)/shard_map/lists/pallas_call | solution.py:145
  5.8 7.3 %all-to-all-start = ((s32[8,1,1536]{2,1,0:T(1,128)}), s32[8,1,1536]{2,1,0:T(1,128)S(1)}, u32[]{:S(2)}, u32[]{:S(2)}) async-start(s32[8,1,1536]{2,1,0:T(1,128)} %bitcast.44), calls=%async_computation | async-start | bytes 98304 | tf_op jit(solution)/shard_map/all_to_all | solution.py:151
  13.1 0.0 slice-start
  13.1 0.0 slice-start.1
  13.1 0.0 copy-start.1
  13.1 7.7 %table.1.table_ref = f32[2,8192,128]{2,1,0:T(8,128)} custom-call(bf16[192,8192]{1,0:T(8,128)(2,1)} %feature_ref.1), custom_call_target="tpu_custom_call" | custom-call | bytes 25165824 | tf_op jit(solution)/shard_map/table/pallas_call | solution.py:156
  20.8 0.0 slice-done
  20.8 0.0 slice-done.1
  20.8 0.0 copy-done.1
  20.8 0.7 pad_maximum_fusion.1.weight_ref
  21.5 0.0 all-to-all-done
  21.5 0.7 compare_select_fusion
  22.2 39.1 %owner.1 = (bf16[2,8,128,256]{3,2,1,0:T(8,128)(2,1)}, bf16[2,8,128,256]{3,2,1,0:T(8,128)(2,1)}, bf16[4,8,128,384]{3,2,1,0:T(8,128)(2,1)}) custom-call(s32[12288]{0:T(1024)} %bitcast.43, s32[1]{0:T(128)} %bitcast.4.place_ref, s32[8,1,1536]{2,1,0:T(1,128)} %get-tuple-element.11.key_ref, f32[2,8192,128]{2,1,0:T(8,128)} %table.1.table_ref, ...), custom_call_target="tpu_custom_call" | custom-call | tf_op jit(solution)/shard_map/owner/pallas_call | solution.py:175
  61.3 0.0 collective-permute-start
  61.3 2.9 %collective-permute-done = bf16[2,8,128,256]{3,2,1,0:T(8,128)(2,1)S(1)} collective-permute-done((bf16[2,8,128,256]{3,2,1,0:T(8,128)(2,1)}, bf16[2,8,128,256]{3,2,1,0:T(8,128)(2,1)S(1)}, u32[]{:S(2)}, u32[]{:S(2)}) %collective-permute-start) | collective-permute-done | bytes 1048608 | tf_op jit(solution)/shard_map/ppermute | solution.py:131
  64.2 1.5 convert_add_fusion
  65.7 0.0 copy-start.2
  65.7 0.1 fusion.4
  65.8 1.6 collective-permute-start.1
  67.3 12.5 %collective-permute-done.1 = bf16[8,128,256]{2,1,0:T(8,128)(2,1)S(1)} collective-permute-done((bf16[8,128,256]{2,1,0:T(8,128)(2,1)S(1)}, bf16[8,128,256]{2,1,0:T(8,128)(2,1)S(1)}, u32[]{:S(2)}, u32[]{:S(2)}) %collective-permute-start.1) | collective-permute-done | bytes 524320 | tf_op jit(solution)/shard_map/ppermute | solution.py:131
  79.8 0.2 fusion.3
  80.0 0.0 copy-start
  80.0 20.0 %all_to_all.29 = bf16[8,128,256]{2,1,0:T(8,128)(2,1)S(1)} all-to-all(bf16[8,128,256]{2,1,0:T(8,128)(2,1)S(1)} %fusion.3), channel_id=1, replica_groups=mesh['wide'=8,'narrow'=4] {'wide'}, dimensions={0} | all-to-all | bytes 1048576 | tf_op jit(solution)/shard_map/all_to_all | solution.py:206
  100.0 0.1 convert_reduce_fusion
  100.0 0.0 copy-done.2
  100.0 0.7 fusion.7
  100.8 17.4 %all_to_all.30 = bf16[8,128,256]{2,1,0:T(8,128)(2,1)S(1)} all-to-all(bf16[8,128,256]{2,1,0:T(8,128)(2,1)S(1)} %broadcast_in_dim.9), channel_id=1, replica_groups=mesh['wide'=8,'narrow'=4] {'wide'}, dimensions={0} | all-to-all | bytes 1048576 | tf_op jit(solution)/shard_map/all_to_all | solution.py:214
  118.2 1.5 collective-permute-start.2
  119.7 10.8 %collective-permute-done.2 = bf16[8,128,256]{2,1,0:T(8,128)(2,1)S(1)} collective-permute-done((bf16[8,128,256]{2,1,0:T(8,128)(2,1)S(1)}, bf16[8,128,256]{2,1,0:T(8,128)(2,1)S(1)}, u32[]{:S(2)}, u32[]{:S(2)}) %collective-permute-start.2) | collective-permute-done | bytes 524320 | tf_op jit(solution)/shard_map/ppermute | solution.py:131
  130.6 0.1 pad_maximum_fusion
  130.7 0.1 collective-permute-start.3
  130.7 2.6 %collective-permute-done.3 = bf16[2,8,128,256]{3,2,1,0:T(8,128)(2,1)S(1)} collective-permute-done((bf16[2,8,128,256]{3,2,1,0:T(8,128)(2,1)S(1)}, bf16[2,8,128,256]{3,2,1,0:T(8,128)(2,1)S(1)}, u32[]{:S(2)}, u32[]{:S(2)}) %collective-permute-start.3) | collective-permute-done | bytes 1048608 | tf_op jit(solution)/shard_map/ppermute | solution.py:131
  133.4 0.0 copy-done
  133.4 0.6 convolution_bitcast_fusion
  134.0 0.6 fusion.1
  134.6 12.5 %all_to_all.31 = bf16[8,48,256]{2,1,0:T(8,128)(2,1)S(1)} all-to-all(bf16[8,48,256]{2,1,0:T(8,128)(2,1)S(1)} %bitcast.46), channel_id=1, replica_groups=mesh['wide'=8,'narrow'=4] {'wide'}, dimensions={0} | all-to-all | bytes 393216 | tf_op jit(solution)/shard_map/all_to_all | solution.py:229
  147.2 10.7 %all_to_all.32 = bf16[8,48,256]{2,1,0:T(8,128)(2,1)S(1)} all-to-all(bf16[8,48,256]{2,1,0:T(8,128)(2,1)S(1)} %broadcast_in_dim.18), channel_id=1, replica_groups=mesh['wide'=8,'narrow'=4] {'wide'}, dimensions={0} | all-to-all | bytes 393216 | tf_op jit(solution)/shard_map/all_to_all | solution.py:231
  158.0 0.7 pad_maximum_fusion.2
  158.7 0.7 slice.46
  (6 shorter events, 0.1 us)
Async XLA Ops:
  5.8 15.7 %all-to-all-start = ((s32[8,1,1536]{2,1,0:T(1,128)}), s32[8,1,1536]{2,1,0:T(1,128)S(1)}, u32[]{:S(2)}, u32[]{:S(2)}) async-start(s32[8,1,1536]{2,1,0:T(1,128)} %bitcast.44), calls=%async_computation | async-start | bytes 98304 | tf_op jit(solution)/shard_map/all_to_all | solution.py:151
  13.1 7.7 %slice-start = ((bf16[192,256]{1,0:T(8,128)(2,1)}), bf16[64,256]{1,0:T(8,128)(2,1)S(1)}, s32[]{:S(2)}) async-start(bf16[192,256]{1,0:T(8,128)(2,1)} %param.10), calls=%async_computation.5 | async-start | bytes 65536 | tf_op jit(solution)/shard_map/slice | solution.py:170
  13.1 7.7 %slice-start.1 = ((bf16[192,256]{1,0:T(8,128)(2,1)}), bf16[128,256]{1,0:T(8,128)(2,1)S(1)}, s32[]{:S(2)}) async-start(bf16[192,256]{1,0:T(8,128)(2,1)} %param.10), calls=%async_computation.6 | async-start | bytes 131072 | tf_op jit(solution)/shard_map/slice | solution.py:170
  13.1 7.7 %copy-start.1 = (bf16[192,256]{1,0:T(8,128)(2,1)S(1)}, bf16[192,256]{1,0:T(8,128)(2,1)}, u32[]{:S(2)}) copy-start(bf16[192,256]{1,0:T(8,128)(2,1)} %param.9) | copy-start | bytes 294916
  61.3 2.9 %collective-permute-start = (bf16[2,8,128,256]{3,2,1,0:T(8,128)(2,1)}, bf16[2,8,128,256]{3,2,1,0:T(8,128)(2,1)S(1)}, u32[]{:S(2)}, u32[]{:S(2)}) collective-permute-start(bf16[2,8,128,256]{3,2,1,0:T(8,128)(2,1)} %get-tuple-element.7), channel_id=1, source_target_pairs={{0,1},{1,0},{2,3},{3,2},{4,5},{5,4},{6,7},{7,6},{8,9},{9,8},{10,11... | collective-permute-start | bytes 3145736 | tf_op jit(solution)/shard_map/ppermute | solution.py:131
  65.7 34.3 %copy-start.2 = (bf16[128,256]{1,0:T(8,128)(2,1)S(1)}, bf16[128,256]{1,0:T(8,128)(2,1)}, u32[]{:S(2)}) copy-start(bf16[128,256]{1,0:T(8,128)(2,1)} %param.11) | copy-start | bytes 196612
  65.8 14.0 %collective-permute-start.1 = (bf16[8,128,256]{2,1,0:T(8,128)(2,1)S(1)}, bf16[8,128,256]{2,1,0:T(8,128)(2,1)S(1)}, u32[]{:S(2)}, u32[]{:S(2)}) collective-permute-start(bf16[8,128,256]{2,1,0:T(8,128)(2,1)S(1)} %fusion.4), channel_id=1, source_target_pairs={{0,2},{1,3},{2,0},{3,1},{4,6},{5,7},{6,4},{7,5},{8,10},{9,11},{10,... | collective-permute-start | bytes 1572872 | tf_op jit(solution)/shard_map/ppermute | solution.py:131
  80.0 53.4 %copy-start = (bf16[4,8,128,384]{3,2,1,0:T(8,128)(2,1)S(1)}, bf16[4,8,128,384]{3,2,1,0:T(8,128)(2,1)}, u32[]{:S(2)}) copy-start(bf16[4,8,128,384]{3,2,1,0:T(8,128)(2,1)} %get-tuple-element.8) | copy-start | bytes 9437188
  118.2 12.3 %collective-permute-start.2 = (bf16[8,128,256]{2,1,0:T(8,128)(2,1)S(1)}, bf16[8,128,256]{2,1,0:T(8,128)(2,1)S(1)}, u32[]{:S(2)}, u32[]{:S(2)}) collective-permute-start(bf16[8,128,256]{2,1,0:T(8,128)(2,1)S(1)} %all_to_all.30), channel_id=1, source_target_pairs={{0,2},{1,3},{2,0},{3,1},{4,6},{5,7},{6,4},{7,5},{8,10},{9,11},{10,... | collective-permute-start | bytes 1572872 | tf_op jit(solution)/shard_map/ppermute | solution.py:131
  130.7 2.7 %collective-permute-start.3 = (bf16[2,8,128,256]{3,2,1,0:T(8,128)(2,1)S(1)}, bf16[2,8,128,256]{3,2,1,0:T(8,128)(2,1)S(1)}, u32[]{:S(2)}, u32[]{:S(2)}) collective-permute-start(bf16[2,8,128,256]{3,2,1,0:T(8,128)(2,1)S(1)} %pad_maximum_fusion), channel_id=1, source_target_pairs={{0,1},{1,0},{2,3},{3,2},{4,5},{5,4},{6,7},{7,6},{8,9},{9,8},{10,11... | collective-permute-start | bytes 3145736 | tf_op jit(solution)/shard_map/ppermute | solution.py:131

commit v2 on v1

--- a/solution.py
+++ b/solution.py
@@ -24,9 +24,9 @@
 
 
 def list_kernel(wide_count, capacity, row_bits, tgt_bits, owner_ref, row_ref, out_ref):
-    requests, targets = owner_ref.shape
+    requests, targets = row_ref.shape
     hi_count = out_ref.shape[0]
-    owners = owner_ref[...]
+    owners = owner_ref[...].reshape(requests, targets)
     masks = jnp.concatenate(
         [jnp.where(owners == w, 1.0, 0.0).astype(BF16) for w in range(wide_count)], axis=0
     )
@@ -70,60 +70,60 @@
 def table_kernel(feature_ref, out_ref):
     block = feature_ref[...].astype(F32)
     rest = block[128:]
-    out_ref[0] = jnp.transpose(block[:128])
-    out_ref[1] = jnp.transpose(jnp.concatenate([rest, rest], axis=0))
-
-
-def owner_kernel(unroll, rows_ref, place_ref, key_ref, table_ref, weight_ref,
+    count = out_ref.shape[0]
+    flat = out_ref.reshape(2 * count, 128)
+    flat[pl.ds(0, count, stride=2), :] = jnp.transpose(block[:128])
+    flat[pl.ds(1, count, stride=2), :] = jnp.transpose(jnp.concatenate([rest, rest], axis=0))
+
+
+def owner_kernel(tgt_bits, unroll, rows_ref, place_ref, key_ref, table_ref, weight_ref,
                  keep_ref, send_ref, sums_ref, held, dense):
     source = pl.program_id(0)
-    capacity = held.shape[1]
-    targets = 128
-    quarters = 4
-    table = table_ref.reshape(2, table_ref.shape[1], 1, 128)
-    base = source * capacity
-
-    def fetch(step, carry):
-        for u in range(unroll):
-            i = step * unroll + u
-            r = rows_ref[base + i]
-            held[0, i] = table[0, r]
-            held[1, i] = table[1, r]
-        return carry
-
-    lax.fori_loop(0, capacity // unroll, fetch, 0)
-    flat = held.reshape(2, capacity, 128)
-    dense[:, :128] = flat[0].astype(BF16)
-    dense[:, 128:] = flat[1].astype(BF16)
+    count = pl.num_programs(0)
+    capacity = held.shape[0]
+    targets = 1 << tgt_bits
+    share = targets // 4
+    now = source & 1
+    flat = held.reshape(2 * capacity, 128)
+
+    def settle(slot):
+        dense[slot, :, :128] = flat[pl.ds(0, capacity, stride=2), :].astype(BF16)
+        dense[slot, :, 128:] = flat[pl.ds(1, capacity, stride=2), :].astype(BF16)
+
+    @pl.when(source == 0)
+    def _():
+        def fetch(step, carry):
+            for u in range(unroll):
+                i = step * unroll + u
+                held[i] = table_ref[rows_ref[i]]
+            return carry
+
+        lax.fori_loop(0, capacity // unroll, fetch, 0)
+        settle(0)
+
+    key = key_ref[0]
+    target = key & (targets - 1)
+    other = (target // share) ^ place_ref[0]
+    piece = 2 * (other & 1) + (other >> 1)
+    place = (target & (share - 1)) + piece * share + (key >> tgt_bits) * targets
+    place = jnp.where(key >= 0, place, -1)
+    row = lax.broadcasted_iota(jnp.int32, (2 * targets, capacity), 0)
+    onehot = jnp.where(row == place, 1.0, 0.0).astype(BF16)
+    both = jnp.dot(onehot, dense[now], preferred_element_type=F32)
+    own = both[:targets]
+    mean = both[targets:] / FANOUT
     lane = lax.broadcasted_iota(jnp.int32, (targets, 128), 1)
-    narrow = place_ref[0]
-
-    def quarter(q, carry):
-        row = lax.broadcasted_iota(jnp.int32, (2 * targets, capacity), 0)
-        wanted = jnp.where(row < targets, row, row + (quarters - 1) * targets) + q * targets
-        onehot = jnp.where(wanted == key_ref[0], 1.0, 0.0).astype(BF16)
-        both = jnp.dot(onehot, dense[...], preferred_element_type=F32)
-        own = both[:targets]
-        mean = both[targets:] / FANOUT
-        mid = jnp.where(lane < 64, own[:, 128:], mean[:, 128:])
-        summed = jnp.concatenate([own[:, :128], mid, mean[:, :128]], axis=1).astype(BF16)
-        preact = jnp.dot(summed, weight_ref[...], preferred_element_type=F32).astype(BF16)
-        other = q ^ narrow
-        core = other & 1
-        chip = other >> 1
-        sums_ref[2 * core + chip, 0] = summed
-
-        @pl.when(core == 0)
-        def _():
-            keep_ref[chip, 0] = preact
-
-        @pl.when(core == 1)
-        def _():
-            send_ref[chip, 0] = preact
-
-        return carry
-
-    lax.fori_loop(0, quarters, quarter, 0)
+    mid = jnp.where(lane < 64, own[:, 128:], mean[:, 128:])
+    summed = jnp.concatenate([own[:, :128], mid, mean[:, :128]], axis=1).astype(BF16)
+    preact = jnp.dot(summed, weight_ref[...], preferred_element_type=F32).astype(BF16)
+    sums_ref[:, 0] = summed.reshape(4, share, summed.shape[1])
+    keep_ref[:, 0] = preact[: 2 * share].reshape(2, share, preact.shape[1])
+    send_ref[:, 0] = preact[2 * share :].reshape(2, share, preact.shape[1])
+
+    ahead = jnp.where(source + 1 < count, source + 1, 0) * capacity
+    for i in range(capacity):
+        held[i] = table_ref[rows_ref[ahead + i]]
+    settle(1 - now)
 
 
 def swap(value, axis, bit):
@@ -147,18 +147,19 @@
         out_shape=jax.ShapeDtypeStruct((wide_count * capacity // 128, 128), jnp.int32),
         compiler_params=pltpu.CompilerParams(vmem_limit_bytes=VMEM_BYTES),
         name="lists",
-    )(jnp.transpose(owner_of.reshape(targets, requests)), jnp.transpose(row_of))
+    )(jnp.transpose(owner_of, (1, 2, 0)), jnp.transpose(row_of))
     asked = lax.all_to_all(
         lists.reshape(wide_count, capacity), "wide", split_axis=0, concat_axis=0, tiled=True
     )
 
-    block = 1024
+    block = nodes // 4
     table = pl.pallas_call(
         table_kernel,
         grid=(nodes // block,),
         in_specs=[pl.BlockSpec((columns, block), lambda i: (0, i))],
-        out_specs=pl.BlockSpec((2, block, 128), lambda i: (0, i, 0)),
-        out_shape=jax.ShapeDtypeStruct((2, nodes, 128), F32),
+        out_specs=pl.BlockSpec((block, 2, 128), lambda i: (i, 0, 0)),
+        out_shape=jax.ShapeDtypeStruct((nodes, 2, 128), F32),
+        compiler_params=pltpu.CompilerParams(vmem_limit_bytes=VMEM_BYTES),
         cost_estimate=pl.CostEstimate(flops=0, bytes_accessed=24 * 1024 * 1024, transcendentals=0),
         name="table",
     )(features)
@@ -173,13 +174,13 @@
     place = lax.axis_index("narrow").astype(jnp.int32).reshape(1)
     halves = jax.ShapeDtypeStruct((2, wide_count, share, hidden_units), BF16)
     keep, send, sums = pl.pallas_call(
-        functools.partial(owner_kernel, unroll),
+        functools.partial(owner_kernel, tgt_bits, unroll),
         grid_spec=pltpu.PrefetchScalarGridSpec(
             num_scalar_prefetch=2,
             grid=(wide_count,),
             in_specs=[
                 pl.BlockSpec((1, 1, capacity), lambda s, *_: (s, 0, 0)),
-                pl.BlockSpec((2, nodes, 128), lambda s, *_: (0, 0, 0)),
+                pl.BlockSpec((nodes, 2, 128), lambda s, *_: (0, 0, 0)),
                 pl.BlockSpec((2 * columns, hidden_units), lambda s, *_: (0, 0)),
             ],
             out_specs=[
@@ -188,8 +189,8 @@
                 pl.BlockSpec((4, 1, share, 2 * columns), lambda s, *_: (0, s, 0, 0)),
             ],
             scratch_shapes=[
-                pltpu.VMEM((2, capacity, 1, 128), F32),
-                pltpu.VMEM((capacity, 256), BF16),
+                pltpu.VMEM((capacity, 2, 128), F32),
+                pltpu.VMEM((2, capacity, 256), BF16),
             ],
         ),
         out_shape=[

time: 160 us -> 145 us (0.906)
  Pallas kernels: 50.6 us -> 36.5 us
    pallas_call x1, Pallas kernels: 39.1 us -> 26.2 us  [on_device(): pl.pallas_call(functools.partial(owner_kernel, tgt_bits, unroll), grid_sp...]
  transfers between devices with their start and end apart: 5 -> 5, of which waited for: 4 -> 4; matrix products, arithmetic and copies ran while one was open for 0% -> 0% of each run, Pallas kernels for 5% -> 4%
where the time goes in v2:
time: 145 us; the launch traced here: 144 us
  blocking collectives  60.7 us (42%)
  Pallas kernels  36.5 us (25%)
  waiting for transfers between devices  28.8 us (20%)
  starting transfers between devices  10.4 us (7%)
  other arithmetic  4.71 us (3%)
    ppermute x4, waiting for transfers between devices, swap(): return lax.ppermute(value, axis, [(i, i ^ bit) for i in range(count)])  28.8 us
    pallas_call x1, Pallas kernels, on_device(): pl.pallas_call(functools.partial(owner_kernel, tgt_bits, unroll), grid_sp...  26.2 us
    all_to_all x1, blocking collectives, on_device(): lax.all_to_all(quartet.astype(BF16), 'wide', split_axis=0, concat_axis=0,...  20 us
    all_to_all x1, blocking collectives, on_device(): lax.all_to_all(jnp.broadcast_to(slope[None], (wide_count, share, hidden_u...  17.4 us
    all_to_all x1, blocking collectives, on_device(): lax.all_to_all(slices, 'wide', split_axis=0, concat_axis=0, tiled=True)  12.5 us
    all_to_all x1, blocking collectives, on_device(): lax.all_to_all(jnp.broadcast_to(own[None], slices.shape), 'wide', split_a...  10.7 us
    all_to_all x1, starting transfers between devices, on_device(): lax.all_to_all(lists.reshape(wide_count, capacity), 'wide', split_axis=0,...  7.28 us
    pallas_call x1, Pallas kernels, on_device(): pl.pallas_call(table_kernel, grid=(nodes // block,), in_specs=[pl.BlockSp...  6.13 us
  transfers between devices with their start and end apart: 5, of which 4 were waited for; matrix products, arithmetic and copies ran while one was open for 0% of the time, Pallas kernels for 4%

profile of v2, /device:TPU:0, one launch (start us, length us, event | category | flops | bytes accessed | tf_op | source)
XLA Modules:
  0.0 143.9 jit_solution(1009292616571536682)
XLA Ops:
  0.6 4.1 %lists.1 = s32[96,128]{1,0:T(8,128)} custom-call(s32[16,1,512]{2,1,0:T(1,128)} %bitcast.43, s32[16,512]{1,0:T(8,128)} %bitcast.44), custom_call_target="tpu_custom_call" | custom-call | tf_op jit(solution)/shard_map/lists/pallas_call | solution.py:145
  4.8 7.3 %all-to-all-start = ((s32[8,1,1536]{2,1,0:T(1,128)}), s32[8,1,1536]{2,1,0:T(1,128)S(1)}, u32[]{:S(2)}, u32[]{:S(2)}) async-start(s32[8,1,1536]{2,1,0:T(1,128)} %bitcast.40), calls=%async_computation | async-start | bytes 98304 | tf_op jit(solution)/shard_map/all_to_all | solution.py:151
  12.0 0.0 slice-start
  12.0 0.0 slice-start.1
  12.1 0.0 copy-start.1
  12.1 6.1 %table.1.table_ref = f32[8192,2,128]{2,1,0:T(2,128)} custom-call(bf16[192,8192]{1,0:T(8,128)(2,1)} %feature_ref.1), custom_call_target="tpu_custom_call" | custom-call | bytes 25165824 | tf_op jit(solution)/shard_map/table/pallas_call | solution.py:156
  18.2 0.0 slice-done
  18.2 0.0 slice-done.1
  18.2 0.0 copy-done.1
  18.2 0.7 pad_maximum_fusion.1.weight_ref
  18.9 0.0 all-to-all-done
  18.9 0.7 compare_select_fusion
  19.6 26.2 %owner.1 = (bf16[2,8,128,256]{3,2,1,0:T(8,128)(2,1)}, bf16[2,8,128,256]{3,2,1,0:T(8,128)(2,1)}, bf16[4,8,128,384]{3,2,1,0:T(8,128)(2,1)}) custom-call(s32[12288]{0:T(1024)} %bitcast.39, s32[1]{0:T(128)} %bitcast.4.place_ref, s32[8,1,1536]{2,1,0:T(1,128)} %get-tuple-element.11.key_ref, f32[8192,2,128]{2,1,0:T(2,128)} %table.1.table_ref, ...), custom_call_target="tpu_custom_call" | custom-call | tf_op jit(solution)/shard_map/owner/pallas_call | solution.py:176
  45.8 0.0 collective-permute-start
  45.8 2.9 %collective-permute-done = bf16[2,8,128,256]{3,2,1,0:T(8,128)(2,1)S(1)} collective-permute-done((bf16[2,8,128,256]{3,2,1,0:T(8,128)(2,1)}, bf16[2,8,128,256]{3,2,1,0:T(8,128)(2,1)S(1)}, u32[]{:S(2)}, u32[]{:S(2)}) %collective-permute-start) | collective-permute-done | bytes 1048608 | tf_op jit(solution)/shard_map/ppermute | solution.py:131
  48.7 1.5 %convert_add_fusion = f32[2,8,128,256]{3,2,1,0:T(8,128)S(1)} fusion(bf16[2,8,128,256]{3,2,1,0:T(8,128)(2,1)S(1)} %collective-permute-done, bf16[2,8,128,256]{3,2,1,0:T(8,128)(2,1)} %get-tuple-element.6), kind=kLoop, calls=%fused_computation | loop fusion | flops 1572864 | bytes 4194304 | tf_op jit(solution)/shard_map/add | solution.py:205
  50.2 0.0 copy-start.2
  50.2 0.1 fusion.4
  50.3 1.6 %collective-permute-start.1 = (bf16[8,128,256]{2,1,0:T(8,128)(2,1)S(1)}, bf16[8,128,256]{2,1,0:T(8,128)(2,1)S(1)}, u32[]{:S(2)}, u32[]{:S(2)}) collective-permute-start(bf16[8,128,256]{2,1,0:T(8,128)(2,1)S(1)} %fusion.4), channel_id=1, source_target_pairs={{0,2},{1,3},{2,0},{3,1},{4,6},{5,7},{6,4},{7,5},{8,10},{9,11},{10,... | collective-permute-start | bytes 1572872 | tf_op jit(solution)/shard_map/ppermute | solution.py:131
  51.8 12.5 %collective-permute-done.1 = bf16[8,128,256]{2,1,0:T(8,128)(2,1)S(1)} collective-permute-done((bf16[8,128,256]{2,1,0:T(8,128)(2,1)S(1)}, bf16[8,128,256]{2,1,0:T(8,128)(2,1)S(1)}, u32[]{:S(2)}, u32[]{:S(2)}) %collective-permute-start.1) | collective-permute-done | bytes 524320 | tf_op jit(solution)/shard_map/ppermute | solution.py:131
  64.3 0.2 fusion.3
  64.5 0.0 copy-start
  64.5 20.0 %all_to_all.29 = bf16[8,128,256]{2,1,0:T(8,128)(2,1)S(1)} all-to-all(bf16[8,128,256]{2,1,0:T(8,128)(2,1)S(1)} %fusion.3), channel_id=1, replica_groups=mesh['wide'=8,'narrow'=4] {'wide'}, dimensions={0} | all-to-all | bytes 1048576 | tf_op jit(solution)/shard_map/all_to_all | solution.py:207
  84.5 0.1 convert_reduce_fusion
  84.5 0.0 copy-done.2
  84.6 0.7 fusion.7
  85.3 17.4 %all_to_all.30 = bf16[8,128,256]{2,1,0:T(8,128)(2,1)S(1)} all-to-all(bf16[8,128,256]{2,1,0:T(8,128)(2,1)S(1)} %broadcast_in_dim.9), channel_id=1, replica_groups=mesh['wide'=8,'narrow'=4] {'wide'}, dimensions={0} | all-to-all | bytes 1048576 | tf_op jit(solution)/shard_map/all_to_all | solution.py:215
  102.8 1.5 %collective-permute-start.2 = (bf16[8,128,256]{2,1,0:T(8,128)(2,1)S(1)}, bf16[8,128,256]{2,1,0:T(8,128)(2,1)S(1)}, u32[]{:S(2)}, u32[]{:S(2)}) collective-permute-start(bf16[8,128,256]{2,1,0:T(8,128)(2,1)S(1)} %all_to_all.30), channel_id=1, source_target_pairs={{0,2},{1,3},{2,0},{3,1},{4,6},{5,7},{6,4},{7,5},{8,10},{9,11},{10,... | collective-permute-start | bytes 1572872 | tf_op jit(solution)/shard_map/ppermute | solution.py:131
  104.2 10.8 %collective-permute-done.2 = bf16[8,128,256]{2,1,0:T(8,128)(2,1)S(1)} collective-permute-done((bf16[8,128,256]{2,1,0:T(8,128)(2,1)S(1)}, bf16[8,128,256]{2,1,0:T(8,128)(2,1)S(1)}, u32[]{:S(2)}, u32[]{:S(2)}) %collective-permute-start.2) | collective-permute-done | bytes 524320 | tf_op jit(solution)/shard_map/ppermute | solution.py:131
  115.1 0.1 pad_maximum_fusion
  115.2 0.1 collective-permute-start.3
  115.3 2.6 %collective-permute-done.3 = bf16[2,8,128,256]{3,2,1,0:T(8,128)(2,1)S(1)} collective-permute-done((bf16[2,8,128,256]{3,2,1,0:T(8,128)(2,1)S(1)}, bf16[2,8,128,256]{3,2,1,0:T(8,128)(2,1)S(1)}, u32[]{:S(2)}, u32[]{:S(2)}) %collective-permute-start.3) | collective-permute-done | bytes 1048608 | tf_op jit(solution)/shard_map/ppermute | solution.py:131
  117.9 0.0 copy-done
  117.9 0.6 convolution_bitcast_fusion
  118.5 0.6 fusion.1
  119.2 12.5 %all_to_all.31 = bf16[8,48,256]{2,1,0:T(8,128)(2,1)S(1)} all-to-all(bf16[8,48,256]{2,1,0:T(8,128)(2,1)S(1)} %bitcast.42), channel_id=1, replica_groups=mesh['wide'=8,'narrow'=4] {'wide'}, dimensions={0} | all-to-all | bytes 393216 | tf_op jit(solution)/shard_map/all_to_all | solution.py:230
  131.7 10.7 %all_to_all.32 = bf16[8,48,256]{2,1,0:T(8,128)(2,1)S(1)} all-to-all(bf16[8,48,256]{2,1,0:T(8,128)(2,1)S(1)} %broadcast_in_dim.18), channel_id=1, replica_groups=mesh['wide'=8,'narrow'=4] {'wide'}, dimensions={0} | all-to-all | bytes 393216 | tf_op jit(solution)/shard_map/all_to_all | solution.py:232
  142.5 0.7 pad_maximum_fusion.2
  143.2 0.7 slice.46
  (6 shorter events, 0.1 us)
Async XLA Ops:
  4.8 14.1 %all-to-all-start = ((s32[8,1,1536]{2,1,0:T(1,128)}), s32[8,1,1536]{2,1,0:T(1,128)S(1)}, u32[]{:S(2)}, u32[]{:S(2)}) async-start(s32[8,1,1536]{2,1,0:T(1,128)} %bitcast.40), calls=%async_computation | async-start | bytes 98304 | tf_op jit(solution)/shard_map/all_to_all | solution.py:151
  12.0 6.2 %slice-start = ((bf16[192,256]{1,0:T(8,128)(2,1)}), bf16[64,256]{1,0:T(8,128)(2,1)S(1)}, s32[]{:S(2)}) async-start(bf16[192,256]{1,0:T(8,128)(2,1)} %param.10), calls=%async_computation.5 | async-start | bytes 65536 | tf_op jit(solution)/shard_map/slice | solution.py:171
  12.0 6.2 %slice-start.1 = ((bf16[192,256]{1,0:T(8,128)(2,1)}), bf16[128,256]{1,0:T(8,128)(2,1)S(1)}, s32[]{:S(2)}) async-start(bf16[192,256]{1,0:T(8,128)(2,1)} %param.10), calls=%async_computation.6 | async-start | bytes 131072 | tf_op jit(solution)/shard_map/slice | solution.py:171
  12.1 6.1 %copy-start.1 = (bf16[192,256]{1,0:T(8,128)(2,1)S(1)}, bf16[192,256]{1,0:T(8,128)(2,1)}, u32[]{:S(2)}) copy-start(bf16[192,256]{1,0:T(8,128)(2,1)} %param.9) | copy-start | bytes 294916
  45.8 2.9 %collective-permute-start = (bf16[2,8,128,256]{3,2,1,0:T(8,128)(2,1)}, bf16[2,8,128,256]{3,2,1,0:T(8,128)(2,1)S(1)}, u32[]{:S(2)}, u32[]{:S(2)}) collective-permute-start(bf16[2,8,128,256]{3,2,1,0:T(8,128)(2,1)} %get-tuple-element.7), channel_id=1, source_target_pairs={{0,1},{1,0},{2,3},{3,2},{4,5},{5,4},{6,7},{7,6},{8,9},{9,8},{10,11... | collective-permute-start | bytes 3145736 | tf_op jit(solution)/shard_map/ppermute | solution.py:131
  50.2 34.3 %copy-start.2 = (bf16[128,256]{1,0:T(8,128)(2,1)S(1)}, bf16[128,256]{1,0:T(8,128)(2,1)}, u32[]{:S(2)}) copy-start(bf16[128,256]{1,0:T(8,128)(2,1)} %param.11) | copy-start | bytes 196612
  50.3 14.0 %collective-permute-start.1 = (bf16[8,128,256]{2,1,0:T(8,128)(2,1)S(1)}, bf16[8,128,256]{2,1,0:T(8,128)(2,1)S(1)}, u32[]{:S(2)}, u32[]{:S(2)}) collective-permute-start(bf16[8,128,256]{2,1,0:T(8,128)(2,1)S(1)} %fusion.4), channel_id=1, source_target_pairs={{0,2},{1,3},{2,0},{3,1},{4,6},{5,7},{6,4},{7,5},{8,10},{9,11},{10,... | collective-permute-start | bytes 1572872 | tf_op jit(solution)/shard_map/ppermute | solution.py:131
  64.5 53.4 %copy-start = (bf16[4,8,128,384]{3,2,1,0:T(8,128)(2,1)S(1)}, bf16[4,8,128,384]{3,2,1,0:T(8,128)(2,1)}, u32[]{:S(2)}) copy-start(bf16[4,8,128,384]{3,2,1,0:T(8,128)(2,1)} %get-tuple-element.8) | copy-start | bytes 9437188
  102.8 12.3 %collective-permute-start.2 = (bf16[8,128,256]{2,1,0:T(8,128)(2,1)S(1)}, bf16[8,128,256]{2,1,0:T(8,128)(2,1)S(1)}, u32[]{:S(2)}, u32[]{:S(2)}) collective-permute-start(bf16[8,128,256]{2,1,0:T(8,128)(2,1)S(1)} %all_to_all.30), channel_id=1, source_target_pairs={{0,2},{1,3},{2,0},{3,1},{4,6},{5,7},{6,4},{7,5},{8,10},{9,11},{10,... | collective-permute-start | bytes 1572872 | tf_op jit(solution)/shard_map/ppermute | solution.py:131
  115.2 2.7 %collective-permute-start.3 = (bf16[2,8,128,256]{3,2,1,0:T(8,128)(2,1)S(1)}, bf16[2,8,128,256]{3,2,1,0:T(8,128)(2,1)S(1)}, u32[]{:S(2)}, u32[]{:S(2)}) collective-permute-start(bf16[2,8,128,256]{3,2,1,0:T(8,128)(2,1)S(1)} %pad_maximum_fusion), channel_id=1, source_target_pairs={{0,1},{1,0},{2,3},{3,2},{4,5},{5,4},{6,7},{7,6},{8,9},{9,8},{10,11... | collective-permute-start | bytes 3145736 | tf_op jit(solution)/shard_map/ppermute | solution.py:131

commit v3 on v2

v3 whole, which is shorter than its diff:
```python
import functools

import jax
import jax.numpy as jnp
from jax import lax
from jax.experimental import pallas as pl
from jax.experimental.pallas import tpu as pltpu
from jax.sharding import PartitionSpec as P

FANOUT = 15
BF16 = jnp.bfloat16
F32 = jnp.float32
MIB = 1024 * 1024


def activation(value):
    return jax.nn.gelu(value, approximate=True)


def contract_rows(left, right):
    return lax.dot_general(
        left, right, (((0,), (0,)), ((), ())), preferred_element_type=F32
    )


def list_kernel(wide_count, capacity, tgt_bits, owner_ref, row_ref, out_ref):
    requests, targets = row_ref.shape
    hi_count = wide_count * capacity // 128
    owners = owner_ref[...].reshape(requests, targets)
    masks = jnp.concatenate(
        [jnp.where(owners == w, 1.0, 0.0).astype(BF16) for w in range(wide_count)], axis=0
    )
    lanes = lax.broadcasted_iota(jnp.int32, (targets, targets), 1)
    upper = jnp.where(lax.broadcasted_iota(jnp.int32, (targets, targets), 0) < lanes, 1.0, 0.0)
    within = jnp.dot(masks, upper.astype(BF16), preferred_element_type=F32)
    total = wide_count * requests
    first = lax.broadcasted_iota(jnp.int32, (total, total), 0)
    second = lax.broadcasted_iota(jnp.int32, (total, total), 1)
    lower = jnp.where((second < first) & (second >= first - first % requests), 1.0, 0.0)
    before = jnp.dot(lower.astype(BF16), masks, preferred_element_type=F32)
    offset = jnp.sum(before, axis=1, keepdims=True)
    ranked = masks.astype(F32) * (within + offset)
    slot = jnp.zeros(owners.shape, F32)
    for w in range(wide_count):
        slot = slot + ranked[w * requests : (w + 1) * requests]
    position = owners * capacity + slot.astype(jnp.int32)
    high = position >> 7
    low = position & 127
    target = lax.broadcasted_iota(jnp.int32, owners.shape, 1)
    kind = jnp.where(lax.broadcasted_iota(jnp.int32, owners.shape, 0) == 0, 0, 1)
    wanted = row_ref[...]
    key = (target | (kind << tgt_bits)) + 1
    parts = [
        (wanted & 255).astype(F32),
        ((wanted >> 8) | ((key >> 8) << 5)).astype(F32),
        (key & 255).astype(F32),
    ]
    high_iota = lax.broadcasted_iota(jnp.int32, (hi_count, targets), 0)
    low_iota = lax.broadcasted_iota(jnp.int32, (128, targets), 0)
    sums = jnp.zeros((hi_count, 384), F32)
    for j in range(requests):
        left = jnp.where(high_iota == high[j : j + 1], 1.0, 0.0).astype(BF16)
        hit = low_iota == low[j : j + 1]
        right = jnp.concatenate(
            [jnp.where(hit, part[j : j + 1], 0.0).astype(BF16) for part in parts], axis=0
        )
        sums = sums + lax.dot_general(
            left, right, (((1,), (1,)), ((), ())), preferred_element_type=F32
        )
    sums = sums.astype(jnp.int32)
    shared = sums[:, 128:256]
    rows = sums[:, :128] | ((shared & 31) << 8)
    keys = sums[:, 256:] | ((shared >> 5) << 8)
    if capacity % 128:
        out_ref[:hi_count] = rows
        out_ref[hi_count:] = keys
    else:
        each = capacity // 128
        for w in range(wide_count):
            out_ref[2 * w * each : (2 * w + 1) * each] = rows[w * each : (w + 1) * each]
            out_ref[(2 * w + 1) * each : (2 * w + 2) * each] = keys[w * each : (w + 1) * each]


def table_kernel(feature_ref, out_ref):
    block = feature_ref[...].astype(F32)
    rest = block[128:]
    count = out_ref.shape[0]
    flat = out_ref.reshape(2 * count, 128)
    flat[pl.ds(0, count, stride=2), :] = jnp.transpose(block[:128])
    flat[pl.ds(1, count, stride=2), :] = jnp.transpose(jnp.concatenate([rest, rest], axis=0))


def owner_kernel(tgt_bits, unroll, asked_ref, key_ref, table_ref, self_ref, neighbor_ref,
                 keep_ref, send_ref, sums_ref, held, dense, weights):
    step = pl.program_id(0)
    count = pl.num_programs(0)
    capacity = held.shape[0]
    columns = self_ref.shape[0]
    targets = 1 << tgt_bits
    share = targets // 4
    now = step & 1
    flat = held.reshape(2 * capacity, 128)
    mine = lax.axis_index("wide")

    def settle(slot):
        dense[slot, :, :128] = flat[pl.ds(0, capacity, stride=2), :].astype(BF16)
        dense[slot, :, 128:] = flat[pl.ds(1, capacity, stride=2), :].astype(BF16)

    @pl.when(step == 0)
    def _():
        weights[:columns] = self_ref[...]
        weights[columns : columns + 64] = neighbor_ref[128:]
        weights[columns + 64 :] = neighbor_ref[:128]

        def fetch(block, carry):
            for u in range(unroll):
                i = block * unroll + u
                held[i] = table_ref[asked_ref[2 * mine * capacity + i]]
            return carry

        lax.fori_loop(0, capacity // unroll, fetch, 0)
        settle(0)

    key = key_ref[mine ^ step][:, capacity:] - 1
    target = key & (targets - 1)
    other = (target // share) ^ lax.axis_index("narrow")
    piece = 2 * (other & 1) + (other >> 1)
    place = (target & (share - 1)) + piece * share + (key >> tgt_bits) * targets
    place = jnp.where(key >= 0, place, -1)
    row = lax.broadcasted_iota(jnp.int32, (2 * targets, capacity), 0)
    onehot = jnp.where(row == place, 1.0, 0.0).astype(BF16)
    both = jnp.dot(onehot, dense[now], preferred_element_type=F32)
    own = both[:targets]
    mean = both[targets:] / FANOUT
    lane = lax.broadcasted_iota(jnp.int32, (targets, 128), 1)
    mid = jnp.where(lane < 64, own[:, 128:], mean[:, 128:])
    summed = jnp.concatenate([own[:, :128], mid, mean[:, :128]], axis=1).astype(BF16)
    preact = jnp.dot(summed, weights[...], preferred_element_type=F32).astype(BF16)
    sums_ref[:, 0] = summed.reshape(4, share, summed.shape[1])
    keep_ref[:, 0] = preact[: 2 * share].reshape(2, share, preact.shape[1])
    send_ref[:, 0] = preact[2 * share :].reshape(2, share, preact.shape[1])

    ahead = 2 * (mine ^ jnp.where(step + 1 < count, step + 1, 0)) * capacity
    for i in range(capacity):
        held[i] = table_ref[asked_ref[ahead + i]]
    settle(1 - now)


def swap(value, axis, bit):
    count = lax.axis_size(axis)
    return lax.ppermute(value, axis, [(i, i ^ bit) for i in range(count)])


def masks_of(stage_bits):
    count = len(stage_bits)
    return [
        sum(b for i, b in enumerate(stage_bits) if m >> (count - 1 - i) & 1)
        for m in range(1 << count)
    ]


def dims_of(way, bits):
    return [
        0 if axis == "narrow" else bits + 1 - b.bit_length()
        for axis, stage_bits in way
        for b in stage_bits
    ]


def add_across(value, axis, stage_bits):
    masks = masks_of(stage_bits)
    parts = value.reshape((len(masks), -1) + value.shape[-2:])
    came = [swap(parts[i].astype(BF16), axis, masks[i]) for i in range(1, len(masks))]
    return functools.reduce(jnp.add, [part.astype(F32) for part in came], parts[0])


def collect(value, axis, stage_bits):
    parts = [value] + [swap(value, axis, mask) for mask in masks_of(stage_bits)[1:]]
    return jnp.stack(parts)


def on_device(features, owner_of, row_of, w_self, w_neighbor, cotangent):
    wide_count = lax.axis_size("wide")
    targets, requests = row_of.shape
    columns, nodes = features.shape
    hidden_units = w_self.shape[1]
    total = targets * requests
    capacity = max(2, 3 * total // (2 * wide_count))
    tgt_bits = (targets - 1).bit_length()
    share = targets // 4
    half = hidden_units // 2

    lists = pl.pallas_call(
        functools.partial(list_kernel, wide_count, capacity, tgt_bits),
        out_shape=jax.ShapeDtypeStruct((2 * wide_count * capacity // 128, 128), jnp.int32),
        compiler_params=pltpu.CompilerParams(vmem_limit_bytes=32 * MIB),
        name="lists",
    )(jnp.transpose(owner_of, (1, 2, 0)), jnp.transpose(row_of))
    if capacity % 128:
        lists = jnp.transpose(lists.reshape(2, wide_count, capacity), (1, 0, 2))
    asked = lax.all_to_all(
        lists.reshape(wide_count, 2 * capacity), "wide", split_axis=0, concat_axis=0, tiled=True
    )

    block = nodes // 4
    table = pl.pallas_call(
        table_kernel,
        grid=(nodes // block,),
        in_specs=[pl.BlockSpec((columns, block), lambda i: (0, i))],
        out_specs=pl.BlockSpec((block, 2, 128), lambda i: (i, 0, 0)),
        out_shape=jax.ShapeDtypeStruct((nodes, 2, 128), F32),
        compiler_params=pltpu.CompilerParams(vmem_limit_bytes=20 * MIB),
        cost_estimate=pl.CostEstimate(flops=0, bytes_accessed=24 * MIB, transcendentals=0),
        name="table",
    )(features)

    unroll = next(u for u in (64, 32, 16, 8, 4, 2, 1) if capacity % u == 0)
    halves = jax.ShapeDtypeStruct((2, wide_count, share, hidden_units), BF16)
    whole = pl.BlockSpec(memory_space=pltpu.VMEM)
    keep, send, sums = pl.pallas_call(
        functools.partial(owner_kernel, tgt_bits, unroll),
        grid_spec=pltpu.PrefetchScalarGridSpec(
            num_scalar_prefetch=1,
            grid=(wide_count,),
            in_specs=[whole] * 4,
            out_specs=[
                pl.BlockSpec((2, 1, share, hidden_units), lambda s, *_: (0, s, 0, 0)),
                pl.BlockSpec((2, 1, share, hidden_units), lambda s, *_: (0, s, 0, 0)),
                pl.BlockSpec((4, 1, share, 2 * columns), lambda s, *_: (0, s, 0, 0)),
            ],
            scratch_shapes=[
                pltpu.VMEM((capacity, 2, 128), F32),
                pltpu.VMEM((2, capacity, 256), BF16),
                pltpu.VMEM((2 * columns, hidden_units), BF16),
            ],
        ),
        out_shape=[
            halves,
            halves,
            jax.ShapeDtypeStruct((4, wide_count, share, 2 * columns), BF16),
        ],
        compiler_params=pltpu.CompilerParams(vmem_limit_bytes=30 * MIB),
        name="owner",
    )(asked.reshape(-1), asked.reshape(wide_count, 1, 2 * capacity), table, w_self, w_neighbor)

    bits = wide_count.bit_length() - 1
    far = ("narrow", (2,))
    steps = [("wide", (1 << b,)) for b in range(bits)]
    pair = ("wide", (2, 1))
    ways = [[far] + steps, [pair] + steps[2:] + [far]]
    backs = [steps[:1:-1] + [pair, far], steps[:1:-1] + [far, pair]]
    pieces = (2,) * (1 + bits) + (share, hidden_units)
    paired = keep.astype(F32).reshape(pieces) + swap(send, "narrow", 1).astype(F32).reshape(pieces)
    chains = [
        jnp.transpose(paired[..., c * half : (c + 1) * half], dims_of(way, bits) + [bits + 1, bits + 2])
        for c, way in enumerate(ways)
    ]
    for s in range(max(map(len, ways))):
        for c, way in enumerate(ways):
            if s < len(way):
                chains[c] = add_across(chains[c], *way[s])
    preact = jnp.concatenate([chain.reshape(share, half) for chain in chains], axis=1)
    value, pullback = jax.vjp(activation, preact)
    hidden = value.astype(BF16)
    slope = pullback(cotangent.astype(F32))[0].astype(BF16)

    chains = [slope[:, :half], slope[:, half:]]
    for s in range(max(map(len, backs))):
        for c in (1, 0):
            if s < len(backs[c]):
                chains[c] = collect(chains[c], *backs[c][s])
    near = []
    for c, back in enumerate(backs):
        dims = dims_of(back[::-1], bits)
        order = [dims.index(d) for d in range(bits + 1)] + [bits + 1, bits + 2]
        whole_chain = chains[c].reshape((2,) * (1 + bits) + (share, half))
        near.append(jnp.transpose(whole_chain, order).reshape(-1, half))
    beside = [swap(n, "narrow", 1) for n in near]
    rows = 2 * wide_count * share
    ours = sums[:2].reshape(rows, 2 * columns)
    theirs = sums[2:].reshape(rows, 2 * columns)
    grads = contract_rows(ours, jnp.concatenate(near, axis=1)) + contract_rows(
        theirs, jnp.concatenate(beside, axis=1)
    )
    chains = [grads[:columns], grads[columns:]]
    turns = [steps, steps[-1:] + steps[:-1]]
    for s in range(bits):
        for c in range(2):
            mine = chains[c].astype(BF16)
            axis, (bit,) = turns[c][s]
            chains[c] = mine.astype(F32) + swap(mine, axis, bit).astype(F32)
    grad_self, mixed = chains
    grad_neighbor = jnp.concatenate([mixed[columns - 128 :], mixed[: columns - 128]], axis=0)
    return (hidden, grad_self, grad_neighbor)


def solution(mesh):
    return jax.shard_map(
        on_device,
        mesh=mesh,
        in_specs=(
            P("narrow", "wide"),
            P("wide", None, None),
            P("wide", None),
            P("narrow", None),
            P("narrow", None),
            P(("wide", "narrow"), None),
        ),
        out_specs=(P(("wide", "narrow"), None), P("narrow", None), P("narrow", None)),
        check_vma=False,
    )
```

time: 145 us -> 121 us (0.83)
  blocking collectives: 60.7 us -> 0 us
  starting transfers between devices: 10.4 us -> 45.6 us
  local copies, waits for them, and re-layouts: 0.84 us -> 11.1 us
  Pallas kernels: 36.5 us -> 26.8 us
  waiting for transfers between devices: 28.8 us -> 31.8 us
  other arithmetic: 4.71 us -> 2.97 us
    all_to_all x4 -> x0, blocking collectives: 60.7 us -> none  [the longest x1 20 us: on_device(): lax.all_to_all(quartet.astype(BF16), 'wide', split_axis=0, concat_axis=0,...]
    ppermute x4 -> x28, starting transfers between devices: 3.12 us -> 38.3 us  [swap(): return lax.ppermute(value, axis, [(i, i ^ bit) for i in range(count)])]
    unnamed x6 -> x16, local copies, waits for them, and re-layouts: 0.02 us -> 10.1 us
    pallas_call x1, Pallas kernels: 6.13 us -> 1.62 us  [on_device(): pl.pallas_call(table_kernel, grid=(nodes // block,), in_specs=[pl.BlockSp...]
    pallas_call x1, Pallas kernels: 26.2 us -> 21.8 us  [on_device(): pl.pallas_call(functools.partial(owner_kernel, tgt_bits, unroll), grid_sp...]
    ppermute x4 -> x28, waiting for transfers between devices: 28.8 us -> 31.5 us  [swap(): return lax.ppermute(value, axis, [(i, i ^ bit) for i in range(count)])]
  transfers between devices with their start and end apart: 5 -> 29, of which waited for: 4 -> 20; matrix products, arithmetic and copies ran while one was open for 0% -> 2% of each run, Pallas kernels for 4% -> 1%
where the time goes in v3:
time: 121 us
  starting transfers between devices  45.6 us (38%)
  waiting for transfers between devices  31.8 us (26%)
  Pallas kernels  26.8 us (22%)
  local copies, waits for them, and re-layouts  11.1 us (9%)
  other arithmetic  2.97 us (2%)
  matrix products  1.23 us (1%)
    ppermute x28, starting transfers between devices, swap(): return lax.ppermute(value, axis, [(i, i ^ bit) for i in range(count)])  38.3 us
    ppermute x28, waiting for transfers between devices, swap(): return lax.ppermute(value, axis, [(i, i ^ bit) for i in range(count)])  31.5 us
    pallas_call x1, Pallas kernels, on_device(): pl.pallas_call(functools.partial(owner_kernel, tgt_bits, unroll), grid_sp...  21.8 us
    unnamed x16, local copies, waits for them, and re-layouts  10.1 us
    all_to_all x1, starting transfers between devices, on_device(): lax.all_to_all(lists.reshape(wide_count, 2 * capacity), 'wide', split_axi...  7.28 us
    pallas_call x1, Pallas kernels, on_device(): pl.pallas_call(functools.partial(list_kernel, wide_count, capacity, tgt_b...  3.37 us
  transfers between devices with their start and end apart: 29, of which 20 were waited for; matrix products, arithmetic and copies ran while one was open for 2% of the time, Pallas kernels for 1%

profile of v3, /device:TPU:0, one launch (start us, length us, event | category | flops | bytes accessed | tf_op | source)
XLA Modules:
  0.0 120.5 jit_solution(12346342257973940567)
XLA Ops:
  0.6 0.7 copy-done.5
  1.4 0.8 copy-done.6
  2.1 3.4 %lists.1 = s32[192,128]{1,0:T(8,128)} custom-call(s32[16,1,512]{2,1,0:T(1,128)S(1)} %bitcast.65, s32[16,512]{1,0:T(8,128)S(1)} %bitcast.66), custom_call_target="tpu_custom_call" | custom-call | tf_op jit(solution)/shard_map/lists/pallas_call | solution.py:193
  5.5 7.3 %all-to-all-start = ((s32[8,1,3072]{2,1,0:T(1,128)}), s32[8,1,3072]{2,1,0:T(1,128)S(1)}, u32[]{:S(2)}, u32[]{:S(2)}) async-start(s32[8,1,3072]{2,1,0:T(1,128)} %bitcast.2), calls=%async_computation | async-start | bytes 196608 | tf_op jit(solution)/shard_map/all_to_all | solution.py:201
  12.8 1.9 %copy-done.2 = bf16[192,8192]{1,0:T(8,128)(2,1)S(1)} copy-done((bf16[192,8192]{1,0:T(8,128)(2,1)S(1)}, bf16[192,8192]{1,0:T(8,128)(2,1)}, u32[]{:S(2)}) %copy-start.2) | copy-done | bytes 3145752
  14.7 1.6 %table.1.table_ref = f32[8192,2,128]{2,1,0:T(2,128)S(1)} custom-call(bf16[192,8192]{1,0:T(8,128)(2,1)S(1)} %copy-done.2), custom_call_target="tpu_custom_call" | custom-call | bytes 25165824 | tf_op jit(solution)/shard_map/table/pallas_call | solution.py:206
  16.3 3.3 %copy-done = f32[8192,2,128]{2,1,0:T(2,128)} copy-done((f32[8192,2,128]{2,1,0:T(2,128)}, f32[8192,2,128]{2,1,0:T(2,128)S(1)}, u32[]{:S(2)}) %copy-start) | copy-done | bytes 8388632
  19.9 3.4 %copy-done.1 = f32[8192,2,128]{2,1,0:T(2,128)S(1)} copy-done((f32[8192,2,128]{2,1,0:T(2,128)S(1)}, f32[8192,2,128]{2,1,0:T(2,128)}, u32[]{:S(2)}) %copy-start.1) | copy-done | bytes 8388632
  23.3 21.8 %owner.1 = (bf16[2,8,128,256]{3,2,1,0:T(8,128)(2,1)S(1)}, bf16[2,8,128,256]{3,2,1,0:T(8,128)(2,1)S(1)}, bf16[4,8,128,384]{3,2,1,0:T(8,128)(2,1)S(1)}) custom-call(s32[24576]{0:T(1024)S(1)} %bitcast.64, s32[8,1,3072]{2,1,0:T(1,128)S(1)} %all-to-all-done.key_ref, f32[8192,2,128]{2,1,0:T(2,128)S(1)} %copy-done.1, bf16[192,256]{1,0:T(8,128)(2,1)S(1)} %copy-done.3, ...), custom_call_target="tpu_custom_call" | custom-call | tf_op jit(solution)/shard_map/owner/pallas_call | solution.py:220
  45.2 2.6 %collective-permute-done = bf16[2,8,128,256]{3,2,1,0:T(8,128)(2,1)S(1)} collective-permute-done((bf16[2,8,128,256]{3,2,1,0:T(8,128)(2,1)S(1)}, bf16[2,8,128,256]{3,2,1,0:T(8,128)(2,1)S(1)}, u32[]{:S(2)}, u32[]{:S(2)}) %collective-permute-start) | collective-permute-done | bytes 1048608 | tf_op jit(solution)/shard_map/ppermute | solution.py:151
  48.5 1.6 %collective-permute-start.1 = (bf16[8,128,128]{2,1,0:T(8,128)(2,1)S(1)}, bf16[8,128,128]{2,1,0:T(8,128)(2,1)S(1)}, u32[]{:S(2)}, u32[]{:S(2)}) collective-permute-start(bf16[8,128,128]{2,1,0:T(8,128)(2,1)S(1)} %bitcast.78), channel_id=1, source_target_pairs={{0,2},{1,3},{2,0},{3,1},{4,6},{5,7},{6,4},{7,5},{8,10},{9,11},{10,... | collective-permute-start | bytes 786440 | tf_op jit(solution)/shard_map/ppermute | solution.py:151
  50.3 1.8 %collective-permute-start.5 = (bf16[4,128,128]{2,1,0:T(8,128)(2,1)S(1)}, bf16[4,128,128]{2,1,0:T(8,128)(2,1)S(1)}, u32[]{:S(2)}, u32[]{:S(2)}) collective-permute-start(bf16[4,128,128]{2,1,0:T(8,128)(2,1)S(1)} %get-tuple-element.13), channel_id=1, source_target_pairs={{0,4},{4,0},{8,12},{12,8},{16,20},{20,16},{24,28},{28,24},{1,5},{5... | collective-permute-start | bytes 393224 | tf_op jit(solution)/shard_map/ppermute | solution.py:151
  52.1 1.4 %collective-permute-start.7 = (bf16[4,128,128]{2,1,0:T(8,128)(2,1)S(1)}, bf16[4,128,128]{2,1,0:T(8,128)(2,1)S(1)}, u32[]{:S(2)}, u32[]{:S(2)}) collective-permute-start(bf16[4,128,128]{2,1,0:T(8,128)(2,1)S(1)} %get-tuple-element.14), channel_id=1, source_target_pairs={{0,12},{4,8},{8,4},{12,0},{16,28},{20,24},{24,20},{28,16},{1,13},{... | collective-permute-start | bytes 393224 | tf_op jit(solution)/shard_map/ppermute | solution.py:151
  53.9 3.0 %collective-permute-done.1 = bf16[8,128,128]{2,1,0:T(8,128)(2,1)S(1)} collective-permute-done((bf16[8,128,128]{2,1,0:T(8,128)(2,1)S(1)}, bf16[8,128,128]{2,1,0:T(8,128)(2,1)S(1)}, u32[]{:S(2)}, u32[]{:S(2)}) %collective-permute-start.1) | collective-permute-done | bytes 262176 | tf_op jit(solution)/shard_map/ppermute | solution.py:151
  57.0 1.8 %collective-permute-start.2 = (bf16[4,128,128]{2,1,0:T(8,128)(2,1)S(1)}, bf16[4,128,128]{2,1,0:T(8,128)(2,1)S(1)}, u32[]{:S(2)}, u32[]{:S(2)}) collective-permute-start(bf16[4,128,128]{2,1,0:T(8,128)(2,1)S(1)} %slice.183), channel_id=1, source_target_pairs={{0,4},{4,0},{8,12},{12,8},{16,20},{20,16},{24,28},{28,24},{1,5},{5... | collective-permute-start | bytes 393224 | tf_op jit(solution)/shard_map/ppermute | solution.py:151
  59.8 2.6 %collective-permute-start.8 = (bf16[2,128,128]{2,1,0:T(8,128)(2,1)S(1)}, bf16[2,128,128]{2,1,0:T(8,128)(2,1)S(1)}, u32[]{:S(2)}, u32[]{:S(2)}) collective-permute-start(bf16[2,128,128]{2,1,0:T(8,128)(2,1)S(1)} %slice.184), channel_id=1, source_target_pairs={{0,16},{4,20},{8,24},{12,28},{16,0},{20,4},{24,8},{28,12},{1,17},{... | collective-permute-start | bytes 196616 | tf_op jit(solution)/shard_map/ppermute | solution.py:151
  62.5 1.5 %collective-permute-start.3 = (bf16[2,128,128]{2,1,0:T(8,128)(2,1)S(1)}, bf16[2,128,128]{2,1,0:T(8,128)(2,1)S(1)}, u32[]{:S(2)}, u32[]{:S(2)}) collective-permute-start(bf16[2,128,128]{2,1,0:T(8,128)(2,1)S(1)} %slice.185), channel_id=1, source_target_pairs={{0,8},{4,12},{8,0},{12,4},{16,24},{20,28},{24,16},{28,20},{1,9},{5... | collective-permute-start | bytes 196616 | tf_op jit(solution)/shard_map/ppermute | solution.py:151
  64.0 1.0 collective-permute-done.8
  65.1 0.7 collective-permute-start.9
  65.8 1.0 collective-permute-done.3
  66.8 2.2 %collective-permute-start.4 = (bf16[1,128,128]{2,1,0:T(8,128)(2,1)S(1)}, bf16[1,128,128]{2,1,0:T(8,128)(2,1)S(1)}, u32[]{:S(2)}, u32[]{:S(2)}) collective-permute-start(bf16[1,128,128]{2,1,0:T(8,128)(2,1)S(1)} %slice.187), channel_id=1, source_target_pairs={{0,16},{4,20},{8,24},{12,28},{16,0},{20,4},{24,8},{28,12},{1,17},{... | collective-permute-start | bytes 98312 | tf_op jit(solution)/shard_map/ppermute | solution.py:151
  69.1 2.6 %collective-permute-done.4 = bf16[1,128,128]{2,1,0:T(8,128)(2,1)S(1)} collective-permute-done((bf16[1,128,128]{2,1,0:T(8,128)(2,1)S(1)}, bf16[1,128,128]{2,1,0:T(8,128)(2,1)S(1)}, u32[]{:S(2)}, u32[]{:S(2)}) %collective-permute-start.4) | collective-permute-done | bytes 32800 | tf_op jit(solution)/shard_map/ppermute | solution.py:151
  71.7 0.7 fusion.13
  72.5 2.3 %collective-permute-start.10 = (bf16[128,128]{1,0:T(8,128)(2,1)S(1)}, bf16[128,128]{1,0:T(8,128)(2,1)S(1)}, u32[]{:S(2)}, u32[]{:S(2)}) collective-permute-start(bf16[128,128]{1,0:T(8,128)(2,1)S(1)} %get-tuple-element.29), channel_id=1, source_target_pairs={{0,16},{4,20},{8,24},{12,28},{16,0},{20,4},{24,8},{28,12},{1,17},{... | collective-permute-start | bytes 98312 | tf_op jit(solution)/shard_map/ppermute | solution.py:151
  74.8 0.7 collective-permute-start.15
  75.5 1.9 %collective-permute-done.10 = bf16[128,128]{1,0:T(8,128)(2,1)S(1)} collective-permute-done((bf16[128,128]{1,0:T(8,128)(2,1)S(1)}, bf16[128,128]{1,0:T(8,128)(2,1)S(1)}, u32[]{:S(2)}, u32[]{:S(2)}) %collective-permute-start.10) | collective-permute-done | bytes 32800 | tf_op jit(solution)/shard_map/ppermute | solution.py:151
  77.4 1.7 %collective-permute-start.12 = (bf16[2,128,128]{2,1,0:T(8,128)(2,1)S(1)}, bf16[2,128,128]{2,1,0:T(8,128)(2,1)S(1)}, u32[]{:S(2)}, u32[]{:S(2)}) collective-permute-start(bf16[2,128,128]{2,1,0:T(8,128)(2,1)S(1)} %get-tuple-element.25), channel_id=1, source_target_pairs={{0,8},{4,12},{8,0},{12,4},{16,24},{20,28},{24,16},{28,20},{1,9},{5... | collective-permute-start | bytes 196616 | tf_op jit(solution)/shard_map/ppermute | solution.py:151
  79.1 1.4 %collective-permute-start.11 = (bf16[2,128,128]{2,1,0:T(8,128)(2,1)S(1)}, bf16[2,128,128]{2,1,0:T(8,128)(2,1)S(1)}, u32[]{:S(2)}, u32[]{:S(2)}) collective-permute-start(bf16[2,128,128]{2,1,0:T(8,128)(2,1)S(1)} %get-tuple-element.25), channel_id=1, source_target_pairs={{0,4},{4,0},{8,12},{12,8},{16,20},{20,16},{24,28},{28,24},{1,5},{5... | collective-permute-start | bytes 196616 | tf_op jit(solution)/shard_map/ppermute | solution.py:151
  81.0 1.3 %collective-permute-start.16 = (bf16[2,128,128]{2,1,0:T(8,128)(2,1)S(1)}, bf16[2,128,128]{2,1,0:T(8,128)(2,1)S(1)}, u32[]{:S(2)}, u32[]{:S(2)}) collective-permute-start(bf16[2,128,128]{2,1,0:T(8,128)(2,1)S(1)} %get-tuple-element.31), channel_id=1, source_target_pairs={{0,2},{1,3},{2,0},{3,1},{4,6},{5,7},{6,4},{7,5},{8,10},{9,11},{10,... | collective-permute-start | bytes 196616 | tf_op jit(solution)/shard_map/ppermute | solution.py:151
  82.2 1.1 collective-permute-done.11
  83.4 3.0 %collective-permute-done.13 = bf16[2,128,128]{2,1,0:T(8,128)(2,1)S(1)} collective-permute-done((bf16[2,128,128]{2,1,0:T(8,128)(2,1)S(1)}, bf16[2,128,128]{2,1,0:T(8,128)(2,1)S(1)}, u32[]{:S(2)}, u32[]{:S(2)}) %collective-permute-start.13) | collective-permute-done | bytes 65568 | tf_op jit(solution)/shard_map/ppermute | solution.py:151
  86.4 1.7 %collective-permute-start.14 = (bf16[4,2,128,128]{3,2,1,0:T(8,128)(2,1)S(1)}, bf16[4,2,128,128]{3,2,1,0:T(8,128)(2,1)S(1)}, u32[]{:S(2)}, u32[]{:S(2)}) collective-permute-start(bf16[4,2,128,128]{3,2,1,0:T(8,128)(2,1)S(1)} %pad_maximum_fusion.2), channel_id=1, source_target_pairs={{0,2},{1,3},{2,0},{3,1},{4,6},{5,7},{6,4},{7,5},{8,10},{9,11},{10,... | collective-permute-start | bytes 786440 | tf_op jit(solution)/shard_map/ppermute | solution.py:151
  88.7 2.9 %collective-permute-start.19 = (bf16[2,2,128,128]{3,2,1,0:T(8,128)(2,1)S(1)}, bf16[2,2,128,128]{3,2,1,0:T(8,128)(2,1)S(1)}, u32[]{:S(2)}, u32[]{:S(2)}) collective-permute-start(bf16[2,2,128,128]{3,2,1,0:T(8,128)(2,1)S(1)} %get-tuple-element.21), channel_id=1, source_target_pairs={{0,12},{4,8},{8,4},{12,0},{16,28},{20,24},{24,20},{28,16},{1,13},{... | collective-permute-start | bytes 393224 | tf_op jit(solution)/shard_map/ppermute | solution.py:151
  91.7 1.5 %collective-permute-done.18 = bf16[2,2,128,128]{3,2,1,0:T(8,128)(2,1)S(1)} collective-permute-done((bf16[2,2,128,128]{3,2,1,0:T(8,128)(2,1)S(1)}, bf16[2,2,128,128]{3,2,1,0:T(8,128)(2,1)S(1)}, u32[]{:S(2)}, u32[]{:S(2)}) %collective-permute-start.18) | collective-permute-done | bytes 131104 | tf_op jit(solution)/shard_map/ppermute | solution.py:151
  93.1 1.6 %collective-permute-done.17 = bf16[2,2,128,128]{3,2,1,0:T(8,128)(2,1)S(1)} collective-permute-done((bf16[2,2,128,128]{3,2,1,0:T(8,128)(2,1)S(1)}, bf16[2,2,128,128]{3,2,1,0:T(8,128)(2,1)S(1)}, u32[]{:S(2)}, u32[]{:S(2)}) %collective-permute-start.17) | collective-permute-done | bytes 131104 | tf_op jit(solution)/shard_map/ppermute | solution.py:151
  96.9 0.7 collective-permute-done.20
  98.3 2.9 %collective-permute-start.25 = (bf16[192,256]{1,0:T(8,128)(2,1)S(1)}, bf16[192,256]{1,0:T(8,128)(2,1)S(1)}, u32[]{:S(2)}, u32[]{:S(2)}) collective-permute-start(bf16[192,256]{1,0:T(8,128)(2,1)S(1)} %get-tuple-element.18), channel_id=1, source_target_pairs={{0,16},{4,20},{8,24},{12,28},{16,0},{20,4},{24,8},{28,12},{1,17},{... | collective-permute-start | bytes 294920 | tf_op jit(solution)/shard_map/ppermute | solution.py:151
  101.2 1.5 %collective-permute-start.22 = (bf16[192,256]{1,0:T(8,128)(2,1)S(1)}, bf16[192,256]{1,0:T(8,128)(2,1)S(1)}, u32[]{:S(2)}, u32[]{:S(2)}) collective-permute-start(bf16[192,256]{1,0:T(8,128)(2,1)S(1)} %get-tuple-element.19), channel_id=1, source_target_pairs={{0,4},{4,0},{8,12},{12,8},{16,20},{20,16},{24,28},{28,24},{1,5},{5... | collective-permute-start | bytes 294920 | tf_op jit(solution)/shard_map/ppermute | solution.py:151
  102.7 3.7 %collective-permute-done.25 = bf16[192,256]{1,0:T(8,128)(2,1)S(1)} collective-permute-done((bf16[192,256]{1,0:T(8,128)(2,1)S(1)}, bf16[192,256]{1,0:T(8,128)(2,1)S(1)}, u32[]{:S(2)}, u32[]{:S(2)}) %collective-permute-start.25) | collective-permute-done | bytes 98336 | tf_op jit(solution)/shard_map/ppermute | solution.py:151
  106.4 1.6 %collective-permute-start.26 = (bf16[192,256]{1,0:T(8,128)(2,1)S(1)}, bf16[192,256]{1,0:T(8,128)(2,1)S(1)}, u32[]{:S(2)}, u32[]{:S(2)}) collective-permute-start(bf16[192,256]{1,0:T(8,128)(2,1)S(1)} %get-tuple-element.16), channel_id=1, source_target_pairs={{0,4},{4,0},{8,12},{12,8},{16,20},{20,16},{24,28},{28,24},{1,5},{5... | collective-permute-start | bytes 294920 | tf_op jit(solution)/shard_map/ppermute | solution.py:151
  108.0 1.0 collective-permute-start.23
  109.1 2.1 %collective-permute-done.26 = bf16[192,256]{1,0:T(8,128)(2,1)S(1)} collective-permute-done((bf16[192,256]{1,0:T(8,128)(2,1)S(1)}, bf16[192,256]{1,0:T(8,128)(2,1)S(1)}, u32[]{:S(2)}, u32[]{:S(2)}) %collective-permute-start.26) | collective-permute-done | bytes 98336 | tf_op jit(solution)/shard_map/ppermute | solution.py:151
  111.2 1.2 collective-permute-start.27
  112.3 0.8 collective-permute-done.23
  113.2 2.4 %collective-permute-start.24 = (bf16[192,256]{1,0:T(8,128)(2,1)S(1)}, bf16[192,256]{1,0:T(8,128)(2,1)S(1)}, u32[]{:S(2)}, u32[]{:S(2)}) collective-permute-start(bf16[192,256]{1,0:T(8,128)(2,1)S(1)} %add_convert_fusion.2), channel_id=1, source_target_pairs={{0,16},{4,20},{8,24},{12,28},{16,0},{20,4},{24,8},{28,12},{1,17},{... | collective-permute-start | bytes 294920 | tf_op jit(solution)/shard_map/ppermute | solution.py:151
  115.5 1.1 collective-permute-done.27
  117.4 2.4 %collective-permute-done.24 = bf16[192,256]{1,0:T(8,128)(2,1)S(1)} collective-permute-done((bf16[192,256]{1,0:T(8,128)(2,1)S(1)}, bf16[192,256]{1,0:T(8,128)(2,1)S(1)}, u32[]{:S(2)}, u32[]{:S(2)}) %collective-permute-start.24) | collective-permute-done | bytes 98336 | tf_op jit(solution)/shard_map/ppermute | solution.py:151
  119.8 0.7 convert_add_fusion.2
  (73 shorter events, 7.4 us)
Async XLA Ops:
  0.6 0.8 copy-start.5
  1.4 0.8 copy-start.6
  5.5 14.4 %all-to-all-start = ((s32[8,1,3072]{2,1,0:T(1,128)}), s32[8,1,3072]{2,1,0:T(1,128)S(1)}, u32[]{:S(2)}, u32[]{:S(2)}) async-start(s32[8,1,3072]{2,1,0:T(1,128)} %bitcast.2), calls=%async_computation | async-start | bytes 196608 | tf_op jit(solution)/shard_map/all_to_all | solution.py:201
  12.8 1.9 %copy-start.2 = (bf16[192,8192]{1,0:T(8,128)(2,1)S(1)}, bf16[192,8192]{1,0:T(8,128)(2,1)}, u32[]{:S(2)}) copy-start(bf16[192,8192]{1,0:T(8,128)(2,1)} %feature_ref.1) | copy-start | bytes 9437188
  14.7 5.2 %copy-start.3 = (bf16[192,256]{1,0:T(8,128)(2,1)S(1)}, bf16[192,256]{1,0:T(8,128)(2,1)}, u32[]{:S(2)}) copy-start(bf16[192,256]{1,0:T(8,128)(2,1)} %self_ref.1) | copy-start | bytes 294916
  14.7 5.2 %copy-start.4 = (bf16[192,256]{1,0:T(8,128)(2,1)S(1)}, bf16[192,256]{1,0:T(8,128)(2,1)}, u32[]{:S(2)}) copy-start(bf16[192,256]{1,0:T(8,128)(2,1)} %neighbor_ref.1) | copy-start | bytes 294916
  16.3 3.3 %copy-start = (f32[8192,2,128]{2,1,0:T(2,128)}, f32[8192,2,128]{2,1,0:T(2,128)S(1)}, u32[]{:S(2)}) copy-start(f32[8192,2,128]{2,1,0:T(2,128)S(1)} %table.1.table_ref) | copy-start | bytes 25165828
  19.9 3.4 %copy-start.1 = (f32[8192,2,128]{2,1,0:T(2,128)S(1)}, f32[8192,2,128]{2,1,0:T(2,128)}, u32[]{:S(2)}) copy-start(f32[8192,2,128]{2,1,0:T(2,128)} %copy-done) | copy-start | bytes 25165828
  45.2 2.7 %collective-permute-start = (bf16[2,8,128,256]{3,2,1,0:T(8,128)(2,1)S(1)}, bf16[2,8,128,256]{3,2,1,0:T(8,128)(2,1)S(1)}, u32[]{:S(2)}, u32[]{:S(2)}) collective-permute-start(bf16[2,8,128,256]{3,2,1,0:T(8,128)(2,1)S(1)} %get-tuple-element.7), channel_id=1, source_target_pairs={{0,1},{1,0},{2,3},{3,2},{4,5},{5,4},{6,7},{7,6},{8,9},{9,8},{10,11... | collective-permute-start | bytes 3145736 | tf_op jit(solution)/shard_map/ppermute | solution.py:151
  48.5 8.4 %collective-permute-start.1 = (bf16[8,128,128]{2,1,0:T(8,128)(2,1)S(1)}, bf16[8,128,128]{2,1,0:T(8,128)(2,1)S(1)}, u32[]{:S(2)}, u32[]{:S(2)}) collective-permute-start(bf16[8,128,128]{2,1,0:T(8,128)(2,1)S(1)} %bitcast.78), channel_id=1, source_target_pairs={{0,2},{1,3},{2,0},{3,1},{4,6},{5,7},{6,4},{7,5},{8,10},{9,11},{10,... | collective-permute-start | bytes 786440 | tf_op jit(solution)/shard_map/ppermute | solution.py:151
  50.3 8.4 %collective-permute-start.5 = (bf16[4,128,128]{2,1,0:T(8,128)(2,1)S(1)}, bf16[4,128,128]{2,1,0:T(8,128)(2,1)S(1)}, u32[]{:S(2)}, u32[]{:S(2)}) collective-permute-start(bf16[4,128,128]{2,1,0:T(8,128)(2,1)S(1)} %get-tuple-element.13), channel_id=1, source_target_pairs={{0,4},{4,0},{8,12},{12,8},{16,20},{20,16},{24,28},{28,24},{1,5},{5... | collective-permute-start | bytes 393224 | tf_op jit(solution)/shard_map/ppermute | solution.py:151
  52.1 7.3 %collective-permute-start.7 = (bf16[4,128,128]{2,1,0:T(8,128)(2,1)S(1)}, bf16[4,128,128]{2,1,0:T(8,128)(2,1)S(1)}, u32[]{:S(2)}, u32[]{:S(2)}) collective-permute-start(bf16[4,128,128]{2,1,0:T(8,128)(2,1)S(1)} %get-tuple-element.14), channel_id=1, source_target_pairs={{0,12},{4,8},{8,4},{12,0},{16,28},{20,24},{24,20},{28,16},{1,13},{... | collective-permute-start | bytes 393224 | tf_op jit(solution)/shard_map/ppermute | solution.py:151
  53.6 18.2 %copy-start.7 = (bf16[128,256]{1,0:T(8,128)(2,1)S(1)}, bf16[128,256]{1,0:T(8,128)(2,1)}, u32[]{:S(2)}) copy-start(bf16[128,256]{1,0:T(8,128)(2,1)} %param.11) | copy-start | bytes 196612
  53.6 6.2 %collective-permute-start.6 = (bf16[4,128,128]{2,1,0:T(8,128)(2,1)S(1)}, bf16[4,128,128]{2,1,0:T(8,128)(2,1)S(1)}, u32[]{:S(2)}, u32[]{:S(2)}) collective-permute-start(bf16[4,128,128]{2,1,0:T(8,128)(2,1)S(1)} %get-tuple-element.15), channel_id=1, source_target_pairs={{0,8},{4,12},{8,0},{12,4},{16,24},{20,28},{24,16},{28,20},{1,9},{5... | collective-permute-start | bytes 393224 | tf_op jit(solution)/shard_map/ppermute | solution.py:151
  57.0 5.4 %collective-permute-start.2 = (bf16[4,128,128]{2,1,0:T(8,128)(2,1)S(1)}, bf16[4,128,128]{2,1,0:T(8,128)(2,1)S(1)}, u32[]{:S(2)}, u32[]{:S(2)}) collective-permute-start(bf16[4,128,128]{2,1,0:T(8,128)(2,1)S(1)} %slice.183), channel_id=1, source_target_pairs={{0,4},{4,0},{8,12},{12,8},{16,20},{20,16},{24,28},{28,24},{1,5},{5... | collective-permute-start | bytes 393224 | tf_op jit(solution)/shard_map/ppermute | solution.py:151
  59.8 5.2 %collective-permute-start.8 = (bf16[2,128,128]{2,1,0:T(8,128)(2,1)S(1)}, bf16[2,128,128]{2,1,0:T(8,128)(2,1)S(1)}, u32[]{:S(2)}, u32[]{:S(2)}) collective-permute-start(bf16[2,128,128]{2,1,0:T(8,128)(2,1)S(1)} %slice.184), channel_id=1, source_target_pairs={{0,16},{4,20},{8,24},{12,28},{16,0},{20,4},{24,8},{28,12},{1,17},{... | collective-permute-start | bytes 196616 | tf_op jit(solution)/shard_map/ppermute | solution.py:151
  62.5 4.3 %collective-permute-start.3 = (bf16[2,128,128]{2,1,0:T(8,128)(2,1)S(1)}, bf16[2,128,128]{2,1,0:T(8,128)(2,1)S(1)}, u32[]{:S(2)}, u32[]{:S(2)}) collective-permute-start(bf16[2,128,128]{2,1,0:T(8,128)(2,1)S(1)} %slice.185), channel_id=1, source_target_pairs={{0,8},{4,12},{8,0},{12,4},{16,24},{20,28},{24,16},{28,20},{1,9},{5... | collective-permute-start | bytes 196616 | tf_op jit(solution)/shard_map/ppermute | solution.py:151
  65.1 4.0 %collective-permute-start.9 = (bf16[1,128,128]{2,1,0:T(8,128)(2,1)S(1)}, bf16[1,128,128]{2,1,0:T(8,128)(2,1)S(1)}, u32[]{:S(2)}, u32[]{:S(2)}) collective-permute-start(bf16[1,128,128]{2,1,0:T(8,128)(2,1)S(1)} %slice.186), channel_id=1, source_target_pairs={{0,2},{1,3},{2,0},{3,1},{4,6},{5,7},{6,4},{7,5},{8,10},{9,11},{10,... | collective-permute-start | bytes 98312 | tf_op jit(solution)/shard_map/ppermute | solution.py:151
  66.8 4.9 %collective-permute-start.4 = (bf16[1,128,128]{2,1,0:T(8,128)(2,1)S(1)}, bf16[1,128,128]{2,1,0:T(8,128)(2,1)S(1)}, u32[]{:S(2)}, u32[]{:S(2)}) collective-permute-start(bf16[1,128,128]{2,1,0:T(8,128)(2,1)S(1)} %slice.187), channel_id=1, source_target_pairs={{0,16},{4,20},{8,24},{12,28},{16,0},{20,4},{24,8},{28,12},{1,17},{... | collective-permute-start | bytes 98312 | tf_op jit(solution)/shard_map/ppermute | solution.py:151
  72.5 4.9 %collective-permute-start.10 = (bf16[128,128]{1,0:T(8,128)(2,1)S(1)}, bf16[128,128]{1,0:T(8,128)(2,1)S(1)}, u32[]{:S(2)}, u32[]{:S(2)}) collective-permute-start(bf16[128,128]{1,0:T(8,128)(2,1)S(1)} %get-tuple-element.29), channel_id=1, source_target_pairs={{0,16},{4,20},{8,24},{12,28},{16,0},{20,4},{24,8},{28,12},{1,17},{... | collective-permute-start | bytes 98312 | tf_op jit(solution)/shard_map/ppermute | solution.py:151
  74.8 6.2 %collective-permute-start.15 = (bf16[128,128]{1,0:T(8,128)(2,1)S(1)}, bf16[128,128]{1,0:T(8,128)(2,1)S(1)}, u32[]{:S(2)}, u32[]{:S(2)}) collective-permute-start(bf16[128,128]{1,0:T(8,128)(2,1)S(1)} %get-tuple-element.28), channel_id=1, source_target_pairs={{0,16},{4,20},{8,24},{12,28},{16,0},{20,4},{24,8},{28,12},{1,17},{... | collective-permute-start | bytes 98312 | tf_op jit(solution)/shard_map/ppermute | solution.py:151
  77.4 4.8 %collective-permute-start.12 = (bf16[2,128,128]{2,1,0:T(8,128)(2,1)S(1)}, bf16[2,128,128]{2,1,0:T(8,128)(2,1)S(1)}, u32[]{:S(2)}, u32[]{:S(2)}) collective-permute-start(bf16[2,128,128]{2,1,0:T(8,128)(2,1)S(1)} %get-tuple-element.25), channel_id=1, source_target_pairs={{0,8},{4,12},{8,0},{12,4},{16,24},{20,28},{24,16},{28,20},{1,9},{5... | collective-permute-start | bytes 196616 | tf_op jit(solution)/shard_map/ppermute | solution.py:151
  79.1 4.3 %collective-permute-start.11 = (bf16[2,128,128]{2,1,0:T(8,128)(2,1)S(1)}, bf16[2,128,128]{2,1,0:T(8,128)(2,1)S(1)}, u32[]{:S(2)}, u32[]{:S(2)}) collective-permute-start(bf16[2,128,128]{2,1,0:T(8,128)(2,1)S(1)} %get-tuple-element.25), channel_id=1, source_target_pairs={{0,4},{4,0},{8,12},{12,8},{16,20},{20,16},{24,28},{28,24},{1,5},{5... | collective-permute-start | bytes 196616 | tf_op jit(solution)/shard_map/ppermute | solution.py:151
  80.5 5.8 %collective-permute-start.13 = (bf16[2,128,128]{2,1,0:T(8,128)(2,1)S(1)}, bf16[2,128,128]{2,1,0:T(8,128)(2,1)S(1)}, u32[]{:S(2)}, u32[]{:S(2)}) collective-permute-start(bf16[2,128,128]{2,1,0:T(8,128)(2,1)S(1)} %get-tuple-element.25), channel_id=1, source_target_pairs={{0,12},{4,8},{8,4},{12,0},{16,28},{20,24},{24,20},{28,16},{1,13},{... | collective-permute-start | bytes 196616 | tf_op jit(solution)/shard_map/ppermute | solution.py:151
  81.0 7.1 %collective-permute-start.16 = (bf16[2,128,128]{2,1,0:T(8,128)(2,1)S(1)}, bf16[2,128,128]{2,1,0:T(8,128)(2,1)S(1)}, u32[]{:S(2)}, u32[]{:S(2)}) collective-permute-start(bf16[2,128,128]{2,1,0:T(8,128)(2,1)S(1)} %get-tuple-element.31), channel_id=1, source_target_pairs={{0,2},{1,3},{2,0},{3,1},{4,6},{5,7},{6,4},{7,5},{8,10},{9,11},{10,... | collective-permute-start | bytes 196616 | tf_op jit(solution)/shard_map/ppermute | solution.py:151
  86.4 8.6 %collective-permute-start.14 = (bf16[4,2,128,128]{3,2,1,0:T(8,128)(2,1)S(1)}, bf16[4,2,128,128]{3,2,1,0:T(8,128)(2,1)S(1)}, u32[]{:S(2)}, u32[]{:S(2)}) collective-permute-start(bf16[4,2,128,128]{3,2,1,0:T(8,128)(2,1)S(1)} %pad_maximum_fusion.2), channel_id=1, source_target_pairs={{0,2},{1,3},{2,0},{3,1},{4,6},{5,7},{6,4},{7,5},{8,10},{9,11},{10,... | collective-permute-start | bytes 786440 | tf_op jit(solution)/shard_map/ppermute | solution.py:151
  88.1 5.0 %collective-permute-start.18 = (bf16[2,2,128,128]{3,2,1,0:T(8,128)(2,1)S(1)}, bf16[2,2,128,128]{3,2,1,0:T(8,128)(2,1)S(1)}, u32[]{:S(2)}, u32[]{:S(2)}) collective-permute-start(bf16[2,2,128,128]{3,2,1,0:T(8,128)(2,1)S(1)} %get-tuple-element.21), channel_id=1, source_target_pairs={{0,8},{4,12},{8,0},{12,4},{16,24},{20,28},{24,16},{28,20},{1,9},{5... | collective-permute-start | bytes 393224 | tf_op jit(solution)/shard_map/ppermute | solution.py:151
  88.4 6.4 %collective-permute-start.17 = (bf16[2,2,128,128]{3,2,1,0:T(8,128)(2,1)S(1)}, bf16[2,2,128,128]{3,2,1,0:T(8,128)(2,1)S(1)}, u32[]{:S(2)}, u32[]{:S(2)}) collective-permute-start(bf16[2,2,128,128]{3,2,1,0:T(8,128)(2,1)S(1)} %get-tuple-element.21), channel_id=1, source_target_pairs={{0,4},{4,0},{8,12},{12,8},{16,20},{20,16},{24,28},{28,24},{1,5},{5... | collective-permute-start | bytes 393224 | tf_op jit(solution)/shard_map/ppermute | solution.py:151
  88.7 6.1 %collective-permute-start.19 = (bf16[2,2,128,128]{3,2,1,0:T(8,128)(2,1)S(1)}, bf16[2,2,128,128]{3,2,1,0:T(8,128)(2,1)S(1)}, u32[]{:S(2)}, u32[]{:S(2)}) collective-permute-start(bf16[2,2,128,128]{3,2,1,0:T(8,128)(2,1)S(1)} %get-tuple-element.21), channel_id=1, source_target_pairs={{0,12},{4,8},{8,4},{12,0},{16,28},{20,24},{24,20},{28,16},{1,13},{... | collective-permute-start | bytes 393224 | tf_op jit(solution)/shard_map/ppermute | solution.py:151
  94.9 2.0 %collective-permute-start.21 = (bf16[2048,128]{1,0:T(8,128)(2,1)S(1)}, bf16[2048,128]{1,0:T(8,128)(2,1)S(1)}, u32[]{:S(2)}, u32[]{:S(2)}) collective-permute-start(bf16[2048,128]{1,0:T(8,128)(2,1)S(1)} %bitcast.74), channel_id=1, source_target_pairs={{0,1},{1,0},{2,3},{3,2},{4,5},{5,4},{6,7},{7,6},{8,9},{9,8},{10,11... | collective-permute-start | bytes 1572872 | tf_op jit(solution)/shard_map/ppermute | solution.py:151
  95.1 2.6 %collective-permute-start.20 = (bf16[2048,128]{1,0:T(8,128)(2,1)S(1)}, bf16[2048,128]{1,0:T(8,128)(2,1)S(1)}, u32[]{:S(2)}, u32[]{:S(2)}) collective-permute-start(bf16[2048,128]{1,0:T(8,128)(2,1)S(1)} %bitcast.76), channel_id=1, source_target_pairs={{0,1},{1,0},{2,3},{3,2},{4,5},{5,4},{6,7},{7,6},{8,9},{9,8},{10,11... | collective-permute-start | bytes 1572872 | tf_op jit(solution)/shard_map/ppermute | solution.py:151
  98.3 8.1 %collective-permute-start.25 = (bf16[192,256]{1,0:T(8,128)(2,1)S(1)}, bf16[192,256]{1,0:T(8,128)(2,1)S(1)}, u32[]{:S(2)}, u32[]{:S(2)}) collective-permute-start(bf16[192,256]{1,0:T(8,128)(2,1)S(1)} %get-tuple-element.18), channel_id=1, source_target_pairs={{0,16},{4,20},{8,24},{12,28},{16,0},{20,4},{24,8},{28,12},{1,17},{... | collective-permute-start | bytes 294920 | tf_op jit(solution)/shard_map/ppermute | solution.py:151
  101.2 5.2 %collective-permute-start.22 = (bf16[192,256]{1,0:T(8,128)(2,1)S(1)}, bf16[192,256]{1,0:T(8,128)(2,1)S(1)}, u32[]{:S(2)}, u32[]{:S(2)}) collective-permute-start(bf16[192,256]{1,0:T(8,128)(2,1)S(1)} %get-tuple-element.19), channel_id=1, source_target_pairs={{0,4},{4,0},{8,12},{12,8},{16,20},{20,16},{24,28},{28,24},{1,5},{5... | collective-permute-start | bytes 294920 | tf_op jit(solution)/shard_map/ppermute | solution.py:151
  106.4 4.7 %collective-permute-start.26 = (bf16[192,256]{1,0:T(8,128)(2,1)S(1)}, bf16[192,256]{1,0:T(8,128)(2,1)S(1)}, u32[]{:S(2)}, u32[]{:S(2)}) collective-permute-start(bf16[192,256]{1,0:T(8,128)(2,1)S(1)} %get-tuple-element.16), channel_id=1, source_target_pairs={{0,4},{4,0},{8,12},{12,8},{16,20},{20,16},{24,28},{28,24},{1,5},{5... | collective-permute-start | bytes 294920 | tf_op jit(solution)/shard_map/ppermute | solution.py:151
  108.0 5.1 %collective-permute-start.23 = (bf16[192,256]{1,0:T(8,128)(2,1)S(1)}, bf16[192,256]{1,0:T(8,128)(2,1)S(1)}, u32[]{:S(2)}, u32[]{:S(2)}) collective-permute-start(bf16[192,256]{1,0:T(8,128)(2,1)S(1)} %get-tuple-element.17), channel_id=1, source_target_pairs={{0,8},{4,12},{8,0},{12,4},{16,24},{20,28},{24,16},{28,20},{1,9},{5... | collective-permute-start | bytes 294920 | tf_op jit(solution)/shard_map/ppermute | solution.py:151
  111.2 5.5 %collective-permute-start.27 = (bf16[192,256]{1,0:T(8,128)(2,1)S(1)}, bf16[192,256]{1,0:T(8,128)(2,1)S(1)}, u32[]{:S(2)}, u32[]{:S(2)}) collective-permute-start(bf16[192,256]{1,0:T(8,128)(2,1)S(1)} %add_convert_fusion), channel_id=1, source_target_pairs={{0,8},{4,12},{8,0},{12,4},{16,24},{20,28},{24,16},{28,20},{1,9},{5... | collective-permute-start | bytes 294920 | tf_op jit(solution)/shard_map/ppermute | solution.py:151
  113.2 6.6 %collective-permute-start.24 = (bf16[192,256]{1,0:T(8,128)(2,1)S(1)}, bf16[192,256]{1,0:T(8,128)(2,1)S(1)}, u32[]{:S(2)}, u32[]{:S(2)}) collective-permute-start(bf16[192,256]{1,0:T(8,128)(2,1)S(1)} %add_convert_fusion.2), channel_id=1, source_target_pairs={{0,16},{4,20},{8,24},{12,28},{16,0},{20,4},{24,8},{28,12},{1,17},{... | collective-permute-start | bytes 294920 | tf_op jit(solution)/shard_map/ppermute | solution.py:151

commit v4 on v3

--- a/solution.py
+++ b/solution.py
@@ -23,7 +23,7 @@
     )
 
 
-def list_kernel(wide_count, capacity, tgt_bits, owner_ref, row_ref, out_ref):
+def list_kernel(wide_count, capacity, tgt_bits, owner_ref, row_ref, *out_refs):
     requests, targets = row_ref.shape
     hi_count = wide_count * capacity // 128
     owners = owner_ref[...].reshape(requests, targets)
@@ -43,9 +43,11 @@
     slot = jnp.zeros(owners.shape, F32)
     for w in range(wide_count):
         slot = slot + ranked[w * requests : (w + 1) * requests]
-    position = owners * capacity + slot.astype(jnp.int32)
-    high = position >> 7
-    low = position & 127
+    apart = owners ^ lax.axis_index("wide")
+    turn = (apart & 3) * (wide_count // 4) + (apart >> 2)
+    position = turn * capacity + slot.astype(jnp.int32)
+    high = (position >> 7) + ((position >> 6) & 1) * hi_count
+    low = position & 63
     target = lax.broadcasted_iota(jnp.int32, owners.shape, 1)
     kind = jnp.where(lax.broadcasted_iota(jnp.int32, owners.shape, 0) == 0, 0, 1)
     wanted = row_ref[...]
@@ -55,9 +57,9 @@
         ((wanted >> 8) | ((key >> 8) << 5)).astype(F32),
         (key & 255).astype(F32),
     ]
-    high_iota = lax.broadcasted_iota(jnp.int32, (hi_count, targets), 0)
-    low_iota = lax.broadcasted_iota(jnp.int32, (128, targets), 0)
-    sums = jnp.zeros((hi_count, 384), F32)
+    high_iota = lax.broadcasted_iota(jnp.int32, (2 * hi_count, targets), 0)
+    low_iota = lax.broadcasted_iota(jnp.int32, (64, targets), 0)
+    sums = jnp.zeros((2 * hi_count, 192), F32)
     for j in range(requests):
         left = jnp.where(high_iota == high[j : j + 1], 1.0, 0.0).astype(BF16)
         hit = low_iota == low[j : j + 1]
@@ -68,17 +70,21 @@
             left, right, (((1,), (1,)), ((), ())), preferred_element_type=F32
         )
     sums = sums.astype(jnp.int32)
-    shared = sums[:, 128:256]
-    rows = sums[:, :128] | ((shared & 31) << 8)
-    keys = sums[:, 256:] | ((shared >> 5) << 8)
+    shared = sums[:, 64:128]
+    rows = sums[:, :64] | ((shared & 31) << 8)
+    keys = sums[:, 128:] | ((shared >> 5) << 8)
+    rows = jnp.concatenate([rows[:hi_count], rows[hi_count:]], axis=1)
+    keys = jnp.concatenate([keys[:hi_count], keys[hi_count:]], axis=1)
     if capacity % 128:
-        out_ref[:hi_count] = rows
-        out_ref[hi_count:] = keys
+        out_refs[0][:hi_count] = rows
+        out_refs[0][hi_count:] = keys
     else:
         each = capacity // 128
         for w in range(wide_count):
-            out_ref[2 * w * each : (2 * w + 1) * each] = rows[w * each : (w + 1) * each]
-            out_ref[(2 * w + 1) * each : (2 * w + 2) * each] = keys[w * each : (w + 1) * each]
+            out_ref = out_refs[w // (wide_count // 4)]
+            at = 2 * (w % (wide_count // 4)) * each
+            out_ref[at : at + each] = rows[w * each : (w + 1) * each]
+            out_ref[at + each : at + 2 * each] = keys[w * each : (w + 1) * each]
 
 
 def table_kernel(feature_ref, out_ref):
@@ -100,7 +106,6 @@
     share = targets // 4
     now = step & 1
     flat = held.reshape(2 * capacity, 128)
-    mine = lax.axis_index("wide")
 
     def settle(slot):
         dense[slot, :, :128] = flat[pl.ds(0, capacity, stride=2), :].astype(BF16)
@@ -113,37 +118,44 @@
         weights[columns + 64 :] = neighbor_ref[:128]
 
         def fetch(block, carry):
+            first = block * unroll
+            into = held.at[pl.ds(first, unroll)]
             for u in range(unroll):
-                i = block * unroll + u
-                held[i] = table_ref[asked_ref[2 * mine * capacity + i]]
+                into[u] = table_ref[asked_ref[first + u]]
             return carry
 
         lax.fori_loop(0, capacity // unroll, fetch, 0)
         settle(0)
 
-    key = key_ref[mine ^ step][:, capacity:] - 1
-    target = key & (targets - 1)
-    other = (target // share) ^ lax.axis_index("narrow")
-    piece = 2 * (other & 1) + (other >> 1)
-    place = (target & (share - 1)) + piece * share + (key >> tgt_bits) * targets
-    place = jnp.where(key >= 0, place, -1)
-    row = lax.broadcasted_iota(jnp.int32, (2 * targets, capacity), 0)
-    onehot = jnp.where(row == place, 1.0, 0.0).astype(BF16)
-    both = jnp.dot(onehot, dense[now], preferred_element_type=F32)
-    own = both[:targets]
-    mean = both[targets:] / FANOUT
-    lane = lax.broadcasted_iota(jnp.int32, (targets, 128), 1)
-    mid = jnp.where(lane < 64, own[:, 128:], mean[:, 128:])
-    summed = jnp.concatenate([own[:, :128], mid, mean[:, :128]], axis=1).astype(BF16)
-    preact = jnp.dot(summed, weights[...], preferred_element_type=F32).astype(BF16)
-    sums_ref[:, 0] = summed.reshape(4, share, summed.shape[1])
-    keep_ref[:, 0] = preact[: 2 * share].reshape(2, share, preact.shape[1])
-    send_ref[:, 0] = preact[2 * share :].reshape(2, share, preact.shape[1])
-
-    ahead = 2 * (mine ^ jnp.where(step + 1 < count, step + 1, 0)) * capacity
-    for i in range(capacity):
-        held[i] = table_ref[asked_ref[ahead + i]]
-    settle(1 - now)
+    def serve(fetches):
+        key = key_ref[step][:, capacity:] - 1
+        target = key & (targets - 1)
+        other = (target // share) ^ lax.axis_index("narrow")
+        piece = 2 * (other & 1) + (other >> 1)
+        place = (target & (share - 1)) + piece * share
+
+        def summed_where(wanted, slots):
+            row = lax.broadcasted_iota(jnp.int32, (targets, slots), 0)
+            onehot = jnp.where(row == jnp.where(wanted, place, -1)[:, :slots], 1.0, 0.0)
+            return jnp.dot(onehot.astype(BF16), dense[now, :slots], preferred_element_type=F32)
+
+        own = summed_where((key >= 0) & (key < targets), min(targets, capacity))
+        mean = summed_where(key >= targets, capacity) * (1.0 / FANOUT)
+        lane = lax.broadcasted_iota(jnp.int32, (targets, 128), 1)
+        mid = jnp.where(lane < 64, own[:, 128:], mean[:, 128:])
+        summed = jnp.concatenate([own[:, :128], mid, mean[:, :128]], axis=1).astype(BF16)
+        preact = jnp.dot(summed, weights[...], preferred_element_type=F32).astype(BF16)
+        sums_ref[:, 0] = summed.reshape(4, share, summed.shape[1])
+        keep_ref[:, 0] = preact[: 2 * share].reshape(2, share, preact.shape[1])
+        send_ref[:, 0] = preact[2 * share :].reshape(2, share, preact.shape[1])
+        if fetches:
+            ahead = 2 * (step + 1) * capacity
+            for i in range(capacity):
+                held[i] = table_ref[asked_ref[ahead + i]]
+            settle(1 - now)
+
+    pl.when(step + 1 < count)(lambda: serve(True))
+    pl.when(step + 1 == count)(lambda: serve(False))
 
 
 def swap(value, axis, bit):
@@ -177,6 +189,15 @@
 def collect(value, axis, stage_bits):
     parts = [value] + [swap(value, axis, mask) for mask in masks_of(stage_bits)[1:]]
     return jnp.stack(parts)
+
+
+def add_all(value, axis, stage_bits):
+    mine = value.astype(BF16)
+    parts = [mine.astype(F32)]
+    parts += [swap(mine, axis, mask).astype(F32) for mask in masks_of(stage_bits)[1:]]
+    while len(parts) > 1:
+        parts = [parts[i] + parts[i + 1] for i in range(0, len(parts), 2)]
+    return parts[0]
 
 
 def on_device(features, owner_of, row_of, w_self, w_neighbor, cotangent):
@@ -189,18 +210,6 @@
     tgt_bits = (targets - 1).bit_length()
     share = targets // 4
     half = hidden_units // 2
-
-    lists = pl.pallas_call(
-        functools.partial(list_kernel, wide_count, capacity, tgt_bits),
-        out_shape=jax.ShapeDtypeStruct((2 * wide_count * capacity // 128, 128), jnp.int32),
-        compiler_params=pltpu.CompilerParams(vmem_limit_bytes=32 * MIB),
-        name="lists",
-    )(jnp.transpose(owner_of, (1, 2, 0)), jnp.transpose(row_of))
-    if capacity % 128:
-        lists = jnp.transpose(lists.reshape(2, wide_count, capacity), (1, 0, 2))
-    asked = lax.all_to_all(
-        lists.reshape(wide_count, 2 * capacity), "wide", split_axis=0, concat_axis=0, tiled=True
-    )
 
     block = nodes // 4
     table = pl.pallas_call(
@@ -214,7 +223,26 @@
         name="table",
     )(features)
 
-    unroll = next(u for u in (64, 32, 16, 8, 4, 2, 1) if capacity % u == 0)
+    quarter = wide_count // 4 * 2 * capacity // 128
+    blocks = [quarter] * 4 if capacity % 128 == 0 else [4 * quarter]
+    parts = pl.pallas_call(
+        functools.partial(list_kernel, wide_count, capacity, tgt_bits),
+        out_shape=[jax.ShapeDtypeStruct((rows, 128), jnp.int32) for rows in blocks],
+        compiler_params=pltpu.CompilerParams(vmem_limit_bytes=56 * MIB),
+        name="lists",
+    )(jnp.transpose(owner_of, (1, 2, 0)), jnp.transpose(row_of))
+    if capacity % 128:
+        both = jnp.transpose(parts[0].reshape(2, wide_count, capacity), (1, 0, 2))
+        parts = list(both.reshape(4, wide_count // 4, 2 * capacity))
+    bits = wide_count.bit_length() - 1
+    came = [swap(parts[m], "wide", m) for m in range(1, 4)]
+    came, table = lax.optimization_barrier((came, table))
+    asked = jnp.stack([parts[0]] + came).reshape(4, wide_count // 4, 2 * capacity)
+    for b in range(2, bits):
+        split = asked.reshape(asked.shape[0], -1, 2, 2 * capacity)
+        asked = jnp.concatenate([split[:, :, 0], swap(split[:, :, 1], "wide", 1 << b)], axis=0)
+
+    unroll = next(u for u in (128, 64, 32, 16, 8, 4, 2, 1) if capacity % u == 0)
     halves = jax.ShapeDtypeStruct((2, wide_count, share, hidden_units), BF16)
     whole = pl.BlockSpec(memory_space=pltpu.VMEM)
     keep, send, sums = pl.pallas_call(
@@ -243,7 +271,6 @@
         name="owner",
     )(asked.reshape(-1), asked.reshape(wide_count, 1, 2 * capacity), table, w_self, w_neighbor)
 
-    bits = wide_count.bit_length() - 1
     far = ("narrow", (2,))
     steps = [("wide", (1 << b,)) for b in range(bits)]
     pair = ("wide", (2, 1))
@@ -283,12 +310,10 @@
         theirs, jnp.concatenate(beside, axis=1)
     )
     chains = [grads[:columns], grads[columns:]]
-    turns = [steps, steps[-1:] + steps[:-1]]
-    for s in range(bits):
+    turns = [[pair] + steps[2:], steps[2:] + [pair]]
+    for s in range(len(turns[0])):
         for c in range(2):
-            mine = chains[c].astype(BF16)
-            axis, (bit,) = turns[c][s]
-            chains[c] = mine.astype(F32) + swap(mine, axis, bit).astype(F32)
+            chains[c] = add_all(chains[c], *turns[c][s])
     grad_self, mixed = chains
     grad_neighbor = jnp.concatenate([mixed[columns - 128 :], mixed[: columns - 128]], axis=0)
     return (hidden, grad_self, grad_neighbor)

time: 121 us -> 113 us (0.934)
  local copies, waits for them, and re-layouts: 11.1 us -> 2.98 us
  waiting for transfers between devices: 31.8 us -> 38.2 us
  starting transfers between devices: 45.6 us -> 42.3 us
  Pallas kernels: 26.8 us -> 24.6 us
    unnamed x16 -> x10, local copies, waits for them, and re-layouts: 10.1 us -> 1.9 us
    all_to_all x1 -> x0, starting transfers between devices: 7.28 us -> none  [on_device(): lax.all_to_all(lists.reshape(wide_count, 2 * capacity), 'wide', split_axi...]
    ppermute x28 -> x34, waiting for transfers between devices: 31.5 us -> 38.2 us  [swap(): return lax.ppermute(value, axis, [(i, i ^ bit) for i in range(count)])]
    ppermute x28 -> x34, starting transfers between devices: 38.3 us -> 42.3 us  [swap(): return lax.ppermute(value, axis, [(i, i ^ bit) for i in range(count)])]
    pallas_call x1, Pallas kernels: 21.8 us -> 19.8 us  [on_device(): pl.pallas_call(functools.partial(owner_kernel, tgt_bits, unroll), grid_sp...]
  transfers between devices with their start and end apart: 29 -> 34, of which waited for: 20 -> 25; matrix products, arithmetic and copies ran while one was open for 2% -> 2% of each run, Pallas kernels for 1% -> 1%
where the time goes in v4:
time: 113 us
  starting transfers between devices  42.3 us (37%)
  waiting for transfers between devices  38.2 us (34%)
  Pallas kernels  24.6 us (22%)
  other arithmetic  2.99 us (3%)
  local copies, waits for them, and re-layouts  2.98 us (3%)
  matrix products  1.22 us (1%)
    ppermute x34, starting transfers between devices, swap(): return lax.ppermute(value, axis, [(i, i ^ bit) for i in range(count)])  42.3 us
    ppermute x34, waiting for transfers between devices, swap(): return lax.ppermute(value, axis, [(i, i ^ bit) for i in range(count)])  38.2 us
    pallas_call x1, Pallas kernels, on_device(): pl.pallas_call(functools.partial(owner_kernel, tgt_bits, unroll), grid_sp...  19.8 us
    pallas_call x1, Pallas kernels, on_device(): pl.pallas_call(functools.partial(list_kernel, wide_count, capacity, tgt_b...  3.17 us
  transfers between devices with their start and end apart: 34, of which 25 were waited for; matrix products, arithmetic and copies ran while one was open for 2% of the time, Pallas kernels for 1%

profile of v4, /device:TPU:0, one launch (start us, length us, event | category | flops | bytes accessed | tf_op | source)
XLA Modules:
  0.0 113.3 jit_solution(6609255724840677998)
XLA Ops:
  0.6 3.2 %lists.1 = (s32[48,128]{1,0:T(8,128)}, s32[48,128]{1,0:T(8,128)}, s32[48,128]{1,0:T(8,128)}, s32[48,128]{1,0:T(8,128)}) custom-call(s32[16,1,512]{2,1,0:T(1,128)} %bitcast.91, s32[16,512]{1,0:T(8,128)} %bitcast.92), custom_call_target="tpu_custom_call" | custom-call | tf_op jit(solution)/shard_map/lists/pallas_call | solution.py:228
  3.8 3.0 %collective-permute-start = (s32[48,128]{1,0:T(8,128)}, s32[48,128]{1,0:T(8,128)S(1)}, u32[]{:S(2)}, u32[]{:S(2)}) collective-permute-start(s32[48,128]{1,0:T(8,128)} %get-tuple-element.15), channel_id=1, source_target_pairs={{0,4},{4,0},{8,12},{12,8},{16,20},{20,16},{24,28},{28,24},{1,5},{5... | collective-permute-start | bytes 73736 | tf_op jit(solution)/shard_map/ppermute | solution.py:163
  6.8 1.6 %collective-permute-start.1 = (s32[48,128]{1,0:T(8,128)}, s32[48,128]{1,0:T(8,128)S(1)}, u32[]{:S(2)}, u32[]{:S(2)}) collective-permute-start(s32[48,128]{1,0:T(8,128)} %get-tuple-element.16), channel_id=1, source_target_pairs={{0,8},{4,12},{8,0},{12,4},{16,24},{20,28},{24,16},{28,20},{1,9},{5... | collective-permute-start | bytes 73736 | tf_op jit(solution)/shard_map/ppermute | solution.py:163
  8.3 1.9 %copy-done = bf16[192,8192]{1,0:T(8,128)(2,1)S(1)} copy-done((bf16[192,8192]{1,0:T(8,128)(2,1)S(1)}, bf16[192,8192]{1,0:T(8,128)(2,1)}, u32[]{:S(2)}) %copy-start) | copy-done | bytes 3145752
  10.2 1.6 %table.1.table_ref = f32[8192,2,128]{2,1,0:T(2,128)S(1)} custom-call(bf16[192,8192]{1,0:T(8,128)(2,1)S(1)} %copy-done), custom_call_target="tpu_custom_call" | custom-call | bytes 25165824 | tf_op jit(solution)/shard_map/table/pallas_call | solution.py:215
  11.9 1.4 %collective-permute-done.2 = s32[48,128]{1,0:T(8,128)S(1)} collective-permute-done((s32[48,128]{1,0:T(8,128)}, s32[48,128]{1,0:T(8,128)S(1)}, u32[]{:S(2)}, u32[]{:S(2)}) %collective-permute-start.2) | collective-permute-done | bytes 24608 | tf_op jit(solution)/shard_map/ppermute | solution.py:163
  13.3 2.7 %collective-permute-start.3 = (s32[4,1,3072]{2,1,0:T(1,128)S(1)}, s32[4,1,3072]{2,1,0:T(1,128)S(1)}, u32[]{:S(2)}, u32[]{:S(2)}) collective-permute-start(s32[4,1,3072]{2,1,0:T(1,128)S(1)} %get-tuple-element.41), channel_id=1, source_target_pairs={{0,16},{4,20},{8,24},{12,28},{16,0},{20,4},{24,8},{28,12},{1,17},{... | collective-permute-start | bytes 147464 | tf_op jit(solution)/shard_map/ppermute | solution.py:163
  16.0 2.9 %collective-permute-done.3 = s32[4,1,3072]{2,1,0:T(1,128)S(1)} collective-permute-done((s32[4,1,3072]{2,1,0:T(1,128)S(1)}, s32[4,1,3072]{2,1,0:T(1,128)S(1)}, u32[]{:S(2)}, u32[]{:S(2)}) %collective-permute-start.3) | collective-permute-done | bytes 49184 | tf_op jit(solution)/shard_map/ppermute | solution.py:163
  18.9 19.8 %owner.1 = (bf16[2,8,128,256]{3,2,1,0:T(8,128)(2,1)S(1)}, bf16[2,8,128,256]{3,2,1,0:T(8,128)(2,1)S(1)}, bf16[4,8,128,384]{3,2,1,0:T(8,128)(2,1)S(1)}) custom-call(s32[24576]{0:T(1024)S(1)} %bitcast.71, s32[8,1,3072]{2,1,0:T(1,128)S(1)} %pad_add_fusion.1.key_ref, f32[8192,2,128]{2,1,0:T(2,128)S(1)} %table.1.table_ref, bf16[192,256]{1,0:T(8,128)(2,1)S(1)} %copy-done.1, ...), custom_call_target="tpu_custom_call" | custom-call | tf_op jit(solution)/shard_map/owner/pallas_call | solution.py:248
  38.8 2.6 %collective-permute-done.4 = bf16[2,8,128,256]{3,2,1,0:T(8,128)(2,1)S(1)} collective-permute-done((bf16[2,8,128,256]{3,2,1,0:T(8,128)(2,1)S(1)}, bf16[2,8,128,256]{3,2,1,0:T(8,128)(2,1)S(1)}, u32[]{:S(2)}, u32[]{:S(2)}) %collective-permute-start.4) | collective-permute-done | bytes 1048608 | tf_op jit(solution)/shard_map/ppermute | solution.py:163
  42.1 1.6 %collective-permute-start.5 = (bf16[8,128,128]{2,1,0:T(8,128)(2,1)S(1)}, bf16[8,128,128]{2,1,0:T(8,128)(2,1)S(1)}, u32[]{:S(2)}, u32[]{:S(2)}) collective-permute-start(bf16[8,128,128]{2,1,0:T(8,128)(2,1)S(1)} %bitcast.83), channel_id=1, source_target_pairs={{0,2},{1,3},{2,0},{3,1},{4,6},{5,7},{6,4},{7,5},{8,10},{9,11},{10,... | collective-permute-start | bytes 786440 | tf_op jit(solution)/shard_map/ppermute | solution.py:163
  44.0 1.6 %collective-permute-start.11 = (bf16[4,128,128]{2,1,0:T(8,128)(2,1)S(1)}, bf16[4,128,128]{2,1,0:T(8,128)(2,1)S(1)}, u32[]{:S(2)}, u32[]{:S(2)}) collective-permute-start(bf16[4,128,128]{2,1,0:T(8,128)(2,1)S(1)} %get-tuple-element.30), channel_id=1, source_target_pairs={{0,12},{4,8},{8,4},{12,0},{16,28},{20,24},{24,20},{28,16},{1,13},{... | collective-permute-start | bytes 393224 | tf_op jit(solution)/shard_map/ppermute | solution.py:163
  45.6 1.8 %collective-permute-start.10 = (bf16[4,128,128]{2,1,0:T(8,128)(2,1)S(1)}, bf16[4,128,128]{2,1,0:T(8,128)(2,1)S(1)}, u32[]{:S(2)}, u32[]{:S(2)}) collective-permute-start(bf16[4,128,128]{2,1,0:T(8,128)(2,1)S(1)} %get-tuple-element.31), channel_id=1, source_target_pairs={{0,8},{4,12},{8,0},{12,4},{16,24},{20,28},{24,16},{28,20},{1,9},{5... | collective-permute-start | bytes 393224 | tf_op jit(solution)/shard_map/ppermute | solution.py:163
  47.5 3.0 %collective-permute-done.5 = bf16[8,128,128]{2,1,0:T(8,128)(2,1)S(1)} collective-permute-done((bf16[8,128,128]{2,1,0:T(8,128)(2,1)S(1)}, bf16[8,128,128]{2,1,0:T(8,128)(2,1)S(1)}, u32[]{:S(2)}, u32[]{:S(2)}) %collective-permute-start.5) | collective-permute-done | bytes 262176 | tf_op jit(solution)/shard_map/ppermute | solution.py:163
  50.6 1.4 %collective-permute-done.9 = bf16[4,128,128]{2,1,0:T(8,128)(2,1)S(1)} collective-permute-done((bf16[4,128,128]{2,1,0:T(8,128)(2,1)S(1)}, bf16[4,128,128]{2,1,0:T(8,128)(2,1)S(1)}, u32[]{:S(2)}, u32[]{:S(2)}) %collective-permute-start.9) | collective-permute-done | bytes 131104 | tf_op jit(solution)/shard_map/ppermute | solution.py:163
  52.0 1.2 %collective-permute-done.10 = bf16[4,128,128]{2,1,0:T(8,128)(2,1)S(1)} collective-permute-done((bf16[4,128,128]{2,1,0:T(8,128)(2,1)S(1)}, bf16[4,128,128]{2,1,0:T(8,128)(2,1)S(1)}, u32[]{:S(2)}, u32[]{:S(2)}) %collective-permute-start.10) | collective-permute-done | bytes 131104 | tf_op jit(solution)/shard_map/ppermute | solution.py:163
  53.3 2.1 %collective-permute-start.12 = (bf16[2,128,128]{2,1,0:T(8,128)(2,1)S(1)}, bf16[2,128,128]{2,1,0:T(8,128)(2,1)S(1)}, u32[]{:S(2)}, u32[]{:S(2)}) collective-permute-start(bf16[2,128,128]{2,1,0:T(8,128)(2,1)S(1)} %slice.196), channel_id=1, source_target_pairs={{0,16},{4,20},{8,24},{12,28},{16,0},{20,4},{24,8},{28,12},{1,17},{... | collective-permute-start | bytes 196616 | tf_op jit(solution)/shard_map/ppermute | solution.py:163
  55.6 0.8 collective-permute-start.7
  56.5 2.4 %collective-permute-done.12 = bf16[2,128,128]{2,1,0:T(8,128)(2,1)S(1)} collective-permute-done((bf16[2,128,128]{2,1,0:T(8,128)(2,1)S(1)}, bf16[2,128,128]{2,1,0:T(8,128)(2,1)S(1)}, u32[]{:S(2)}, u32[]{:S(2)}) %collective-permute-start.12) | collective-permute-done | bytes 65568 | tf_op jit(solution)/shard_map/ppermute | solution.py:163
  60.0 2.1 %collective-permute-start.8 = (bf16[1,128,128]{2,1,0:T(8,128)(2,1)S(1)}, bf16[1,128,128]{2,1,0:T(8,128)(2,1)S(1)}, u32[]{:S(2)}, u32[]{:S(2)}) collective-permute-start(bf16[1,128,128]{2,1,0:T(8,128)(2,1)S(1)} %slice.199), channel_id=1, source_target_pairs={{0,16},{4,20},{8,24},{12,28},{16,0},{20,4},{24,8},{28,12},{1,17},{... | collective-permute-start | bytes 98312 | tf_op jit(solution)/shard_map/ppermute | solution.py:163
  62.1 0.8 collective-permute-done.13
  62.9 2.3 %collective-permute-done.8 = bf16[1,128,128]{2,1,0:T(8,128)(2,1)S(1)} collective-permute-done((bf16[1,128,128]{2,1,0:T(8,128)(2,1)S(1)}, bf16[1,128,128]{2,1,0:T(8,128)(2,1)S(1)}, u32[]{:S(2)}, u32[]{:S(2)}) %collective-permute-start.8) | collective-permute-done | bytes 32800 | tf_op jit(solution)/shard_map/ppermute | solution.py:163
  66.0 1.8 %collective-permute-start.14 = (bf16[128,128]{1,0:T(8,128)(2,1)S(1)}, bf16[128,128]{1,0:T(8,128)(2,1)S(1)}, u32[]{:S(2)}, u32[]{:S(2)}) collective-permute-start(bf16[128,128]{1,0:T(8,128)(2,1)S(1)} %get-tuple-element.47), channel_id=1, source_target_pairs={{0,16},{4,20},{8,24},{12,28},{16,0},{20,4},{24,8},{28,12},{1,17},{... | collective-permute-start | bytes 98312 | tf_op jit(solution)/shard_map/ppermute | solution.py:163
  67.8 1.2 %collective-permute-start.19 = (bf16[128,128]{1,0:T(8,128)(2,1)S(1)}, bf16[128,128]{1,0:T(8,128)(2,1)S(1)}, u32[]{:S(2)}, u32[]{:S(2)}) collective-permute-start(bf16[128,128]{1,0:T(8,128)(2,1)S(1)} %get-tuple-element.46), channel_id=1, source_target_pairs={{0,16},{4,20},{8,24},{12,28},{16,0},{20,4},{24,8},{28,12},{1,17},{... | collective-permute-start | bytes 98312 | tf_op jit(solution)/shard_map/ppermute | solution.py:163
  69.0 2.3 %collective-permute-done.14 = bf16[128,128]{1,0:T(8,128)(2,1)S(1)} collective-permute-done((bf16[128,128]{1,0:T(8,128)(2,1)S(1)}, bf16[128,128]{1,0:T(8,128)(2,1)S(1)}, u32[]{:S(2)}, u32[]{:S(2)}) %collective-permute-start.14) | collective-permute-done | bytes 32800 | tf_op jit(solution)/shard_map/ppermute | solution.py:163
  71.7 1.4 %collective-permute-start.15 = (bf16[2,128,128]{2,1,0:T(8,128)(2,1)S(1)}, bf16[2,128,128]{2,1,0:T(8,128)(2,1)S(1)}, u32[]{:S(2)}, u32[]{:S(2)}) collective-permute-start(bf16[2,128,128]{2,1,0:T(8,128)(2,1)S(1)} %get-tuple-element.43), channel_id=1, source_target_pairs={{0,4},{4,0},{8,12},{12,8},{16,20},{20,16},{24,28},{28,24},{1,5},{5... | collective-permute-start | bytes 196616 | tf_op jit(solution)/shard_map/ppermute | solution.py:163
  73.1 1.8 %collective-permute-start.17 = (bf16[2,128,128]{2,1,0:T(8,128)(2,1)S(1)}, bf16[2,128,128]{2,1,0:T(8,128)(2,1)S(1)}, u32[]{:S(2)}, u32[]{:S(2)}) collective-permute-start(bf16[2,128,128]{2,1,0:T(8,128)(2,1)S(1)} %get-tuple-element.43), channel_id=1, source_target_pairs={{0,12},{4,8},{8,4},{12,0},{16,28},{20,24},{24,20},{28,16},{1,13},{... | collective-permute-start | bytes 196616 | tf_op jit(solution)/shard_map/ppermute | solution.py:163
  74.9 0.8 collective-permute-start.20
  76.1 2.8 %collective-permute-done.17 = bf16[2,128,128]{2,1,0:T(8,128)(2,1)S(1)} collective-permute-done((bf16[2,128,128]{2,1,0:T(8,128)(2,1)S(1)}, bf16[2,128,128]{2,1,0:T(8,128)(2,1)S(1)}, u32[]{:S(2)}, u32[]{:S(2)}) %collective-permute-start.17) | collective-permute-done | bytes 65568 | tf_op jit(solution)/shard_map/ppermute | solution.py:163
  78.9 1.2 %collective-permute-start.18 = (bf16[4,2,128,128]{3,2,1,0:T(8,128)(2,1)S(1)}, bf16[4,2,128,128]{3,2,1,0:T(8,128)(2,1)S(1)}, u32[]{:S(2)}, u32[]{:S(2)}) collective-permute-start(bf16[4,2,128,128]{3,2,1,0:T(8,128)(2,1)S(1)} %pad_maximum_fusion.2), channel_id=1, source_target_pairs={{0,2},{1,3},{2,0},{3,1},{4,6},{5,7},{6,4},{7,5},{8,10},{9,11},{10,... | collective-permute-start | bytes 786440 | tf_op jit(solution)/shard_map/ppermute | solution.py:163
  80.3 1.4 %collective-permute-start.21 = (bf16[2,2,128,128]{3,2,1,0:T(8,128)(2,1)S(1)}, bf16[2,2,128,128]{3,2,1,0:T(8,128)(2,1)S(1)}, u32[]{:S(2)}, u32[]{:S(2)}) collective-permute-start(bf16[2,2,128,128]{3,2,1,0:T(8,128)(2,1)S(1)} %get-tuple-element.37), channel_id=1, source_target_pairs={{0,4},{4,0},{8,12},{12,8},{16,20},{20,16},{24,28},{28,24},{1,5},{5... | collective-permute-start | bytes 393224 | tf_op jit(solution)/shard_map/ppermute | solution.py:163
  81.7 2.0 %collective-permute-start.23 = (bf16[2,2,128,128]{3,2,1,0:T(8,128)(2,1)S(1)}, bf16[2,2,128,128]{3,2,1,0:T(8,128)(2,1)S(1)}, u32[]{:S(2)}, u32[]{:S(2)}) collective-permute-start(bf16[2,2,128,128]{3,2,1,0:T(8,128)(2,1)S(1)} %get-tuple-element.37), channel_id=1, source_target_pairs={{0,12},{4,8},{8,4},{12,0},{16,28},{20,24},{24,20},{28,16},{1,13},{... | collective-permute-start | bytes 393224 | tf_op jit(solution)/shard_map/ppermute | solution.py:163
  83.8 1.5 %collective-permute-done.22 = bf16[2,2,128,128]{3,2,1,0:T(8,128)(2,1)S(1)} collective-permute-done((bf16[2,2,128,128]{3,2,1,0:T(8,128)(2,1)S(1)}, bf16[2,2,128,128]{3,2,1,0:T(8,128)(2,1)S(1)}, u32[]{:S(2)}, u32[]{:S(2)}) %collective-permute-start.22) | collective-permute-done | bytes 131104 | tf_op jit(solution)/shard_map/ppermute | solution.py:163
  85.3 2.3 %collective-permute-done.23 = bf16[2,2,128,128]{3,2,1,0:T(8,128)(2,1)S(1)} collective-permute-done((bf16[2,2,128,128]{3,2,1,0:T(8,128)(2,1)S(1)}, bf16[2,2,128,128]{3,2,1,0:T(8,128)(2,1)S(1)}, u32[]{:S(2)}, u32[]{:S(2)}) %collective-permute-start.23) | collective-permute-done | bytes 131104 | tf_op jit(solution)/shard_map/ppermute | solution.py:163
  89.7 0.7 collective-permute-done.24
  91.1 3.0 %collective-permute-start.30 = (bf16[192,256]{1,0:T(8,128)(2,1)S(1)}, bf16[192,256]{1,0:T(8,128)(2,1)S(1)}, u32[]{:S(2)}, u32[]{:S(2)}) collective-permute-start(bf16[192,256]{1,0:T(8,128)(2,1)S(1)} %get-tuple-element.34), channel_id=1, source_target_pairs={{0,16},{4,20},{8,24},{12,28},{16,0},{20,4},{24,8},{28,12},{1,17},{... | collective-permute-start | bytes 294920 | tf_op jit(solution)/shard_map/ppermute | solution.py:163
  94.1 1.0 collective-permute-start.27
  95.1 1.5 %collective-permute-start.26 = (bf16[192,256]{1,0:T(8,128)(2,1)S(1)}, bf16[192,256]{1,0:T(8,128)(2,1)S(1)}, u32[]{:S(2)}, u32[]{:S(2)}) collective-permute-start(bf16[192,256]{1,0:T(8,128)(2,1)S(1)} %get-tuple-element.35), channel_id=1, source_target_pairs={{0,4},{4,0},{8,12},{12,8},{16,20},{20,16},{24,28},{28,24},{1,5},{5... | collective-permute-start | bytes 294920 | tf_op jit(solution)/shard_map/ppermute | solution.py:163
  96.6 0.9 collective-permute-start.28
  97.6 1.8 %collective-permute-done.30 = bf16[192,256]{1,0:T(8,128)(2,1)S(1)} collective-permute-done((bf16[192,256]{1,0:T(8,128)(2,1)S(1)}, bf16[192,256]{1,0:T(8,128)(2,1)S(1)}, u32[]{:S(2)}, u32[]{:S(2)}) %collective-permute-start.30) | collective-permute-done | bytes 98336 | tf_op jit(solution)/shard_map/ppermute | solution.py:163
  99.4 1.6 %collective-permute-done.27 = bf16[192,256]{1,0:T(8,128)(2,1)S(1)} collective-permute-done((bf16[192,256]{1,0:T(8,128)(2,1)S(1)}, bf16[192,256]{1,0:T(8,128)(2,1)S(1)}, u32[]{:S(2)}, u32[]{:S(2)}) %collective-permute-start.27) | collective-permute-done | bytes 98336 | tf_op jit(solution)/shard_map/ppermute | solution.py:163
  101.0 1.2 %collective-permute-done.28 = bf16[192,256]{1,0:T(8,128)(2,1)S(1)} collective-permute-done((bf16[192,256]{1,0:T(8,128)(2,1)S(1)}, bf16[192,256]{1,0:T(8,128)(2,1)S(1)}, u32[]{:S(2)}, u32[]{:S(2)}) %collective-permute-start.28) | collective-permute-done | bytes 98336 | tf_op jit(solution)/shard_map/ppermute | solution.py:163
  102.2 2.0 %collective-permute-start.33 = (bf16[192,256]{1,0:T(8,128)(2,1)S(1)}, bf16[192,256]{1,0:T(8,128)(2,1)S(1)}, u32[]{:S(2)}, u32[]{:S(2)}) collective-permute-start(bf16[192,256]{1,0:T(8,128)(2,1)S(1)} %get-tuple-element.32), channel_id=1, source_target_pairs={{0,12},{4,8},{8,4},{12,0},{16,28},{20,24},{24,20},{28,16},{1,13},{... | collective-permute-start | bytes 294920 | tf_op jit(solution)/shard_map/ppermute | solution.py:163
  104.2 1.1 %collective-permute-start.32 = (bf16[192,256]{1,0:T(8,128)(2,1)S(1)}, bf16[192,256]{1,0:T(8,128)(2,1)S(1)}, u32[]{:S(2)}, u32[]{:S(2)}) collective-permute-start(bf16[192,256]{1,0:T(8,128)(2,1)S(1)} %get-tuple-element.32), channel_id=1, source_target_pairs={{0,8},{4,12},{8,0},{12,4},{16,24},{20,28},{24,16},{28,20},{1,9},{5... | collective-permute-start | bytes 294920 | tf_op jit(solution)/shard_map/ppermute | solution.py:163
  105.8 1.3 %collective-permute-start.29 = (bf16[192,256]{1,0:T(8,128)(2,1)S(1)}, bf16[192,256]{1,0:T(8,128)(2,1)S(1)}, u32[]{:S(2)}, u32[]{:S(2)}) collective-permute-start(bf16[192,256]{1,0:T(8,128)(2,1)S(1)} %get-tuple-element.33), channel_id=1, source_target_pairs={{0,16},{4,20},{8,24},{12,28},{16,0},{20,4},{24,8},{28,12},{1,17},{... | collective-permute-start | bytes 294920 | tf_op jit(solution)/shard_map/ppermute | solution.py:163
  107.0 1.3 %collective-permute-done.33 = bf16[192,256]{1,0:T(8,128)(2,1)S(1)} collective-permute-done((bf16[192,256]{1,0:T(8,128)(2,1)S(1)}, bf16[192,256]{1,0:T(8,128)(2,1)S(1)}, u32[]{:S(2)}, u32[]{:S(2)}) %collective-permute-start.33) | collective-permute-done | bytes 98336 | tf_op jit(solution)/shard_map/ppermute | solution.py:163
  108.3 2.3 %collective-permute-done.32 = bf16[192,256]{1,0:T(8,128)(2,1)S(1)} collective-permute-done((bf16[192,256]{1,0:T(8,128)(2,1)S(1)}, bf16[192,256]{1,0:T(8,128)(2,1)S(1)}, u32[]{:S(2)}, u32[]{:S(2)}) %collective-permute-start.32) | collective-permute-done | bytes 98336 | tf_op jit(solution)/shard_map/ppermute | solution.py:163
  111.4 1.1 collective-permute-done.29
  (78 shorter events, 8.9 us)
Async XLA Ops:
  3.8 8.1 %collective-permute-start = (s32[48,128]{1,0:T(8,128)}, s32[48,128]{1,0:T(8,128)S(1)}, u32[]{:S(2)}, u32[]{:S(2)}) collective-permute-start(s32[48,128]{1,0:T(8,128)} %get-tuple-element.15), channel_id=1, source_target_pairs={{0,4},{4,0},{8,12},{12,8},{16,20},{20,16},{24,28},{28,24},{1,5},{5... | collective-permute-start | bytes 73736 | tf_op jit(solution)/shard_map/ppermute | solution.py:163
  6.8 5.1 %collective-permute-start.1 = (s32[48,128]{1,0:T(8,128)}, s32[48,128]{1,0:T(8,128)S(1)}, u32[]{:S(2)}, u32[]{:S(2)}) collective-permute-start(s32[48,128]{1,0:T(8,128)} %get-tuple-element.16), channel_id=1, source_target_pairs={{0,8},{4,12},{8,0},{12,4},{16,24},{20,28},{24,16},{28,20},{1,9},{5... | collective-permute-start | bytes 73736 | tf_op jit(solution)/shard_map/ppermute | solution.py:163
  8.3 4.9 %collective-permute-start.2 = (s32[48,128]{1,0:T(8,128)}, s32[48,128]{1,0:T(8,128)S(1)}, u32[]{:S(2)}, u32[]{:S(2)}) collective-permute-start(s32[48,128]{1,0:T(8,128)} %get-tuple-element.17), channel_id=1, source_target_pairs={{0,12},{4,8},{8,4},{12,0},{16,28},{20,24},{24,20},{28,16},{1,13},{... | collective-permute-start | bytes 73736 | tf_op jit(solution)/shard_map/ppermute | solution.py:163
  8.3 1.9 %copy-start = (bf16[192,8192]{1,0:T(8,128)(2,1)S(1)}, bf16[192,8192]{1,0:T(8,128)(2,1)}, u32[]{:S(2)}) copy-start(bf16[192,8192]{1,0:T(8,128)(2,1)} %feature_ref.1) | copy-start | bytes 9437188
  10.2 3.0 %copy-start.4 = (s32[48,128]{1,0:T(8,128)S(1)}, s32[48,128]{1,0:T(8,128)}, u32[]{:S(2)}) copy-start(s32[48,128]{1,0:T(8,128)} %get-tuple-element.14) | copy-start | bytes 73732
  10.2 8.7 %copy-start.1 = (bf16[192,256]{1,0:T(8,128)(2,1)S(1)}, bf16[192,256]{1,0:T(8,128)(2,1)}, u32[]{:S(2)}) copy-start(bf16[192,256]{1,0:T(8,128)(2,1)} %self_ref.1) | copy-start | bytes 294916
  10.2 8.7 %copy-start.2 = (bf16[192,256]{1,0:T(8,128)(2,1)S(1)}, bf16[192,256]{1,0:T(8,128)(2,1)}, u32[]{:S(2)}) copy-start(bf16[192,256]{1,0:T(8,128)(2,1)} %neighbor_ref.1) | copy-start | bytes 294916
  13.3 5.6 %collective-permute-start.3 = (s32[4,1,3072]{2,1,0:T(1,128)S(1)}, s32[4,1,3072]{2,1,0:T(1,128)S(1)}, u32[]{:S(2)}, u32[]{:S(2)}) collective-permute-start(s32[4,1,3072]{2,1,0:T(1,128)S(1)} %get-tuple-element.41), channel_id=1, source_target_pairs={{0,16},{4,20},{8,24},{12,28},{16,0},{20,4},{24,8},{28,12},{1,17},{... | collective-permute-start | bytes 147464 | tf_op jit(solution)/shard_map/ppermute | solution.py:163
  38.7 2.7 %collective-permute-start.4 = (bf16[2,8,128,256]{3,2,1,0:T(8,128)(2,1)S(1)}, bf16[2,8,128,256]{3,2,1,0:T(8,128)(2,1)S(1)}, u32[]{:S(2)}, u32[]{:S(2)}) collective-permute-start(bf16[2,8,128,256]{3,2,1,0:T(8,128)(2,1)S(1)} %get-tuple-element.23), channel_id=1, source_target_pairs={{0,1},{1,0},{2,3},{3,2},{4,5},{5,4},{6,7},{7,6},{8,9},{9,8},{10,11... | collective-permute-start | bytes 3145736 | tf_op jit(solution)/shard_map/ppermute | solution.py:163
  42.1 8.4 %collective-permute-start.5 = (bf16[8,128,128]{2,1,0:T(8,128)(2,1)S(1)}, bf16[8,128,128]{2,1,0:T(8,128)(2,1)S(1)}, u32[]{:S(2)}, u32[]{:S(2)}) collective-permute-start(bf16[8,128,128]{2,1,0:T(8,128)(2,1)S(1)} %bitcast.83), channel_id=1, source_target_pairs={{0,2},{1,3},{2,0},{3,1},{4,6},{5,7},{6,4},{7,5},{8,10},{9,11},{10,... | collective-permute-start | bytes 786440 | tf_op jit(solution)/shard_map/ppermute | solution.py:163
  43.9 8.1 %collective-permute-start.9 = (bf16[4,128,128]{2,1,0:T(8,128)(2,1)S(1)}, bf16[4,128,128]{2,1,0:T(8,128)(2,1)S(1)}, u32[]{:S(2)}, u32[]{:S(2)}) collective-permute-start(bf16[4,128,128]{2,1,0:T(8,128)(2,1)S(1)} %get-tuple-element.29), channel_id=1, source_target_pairs={{0,4},{4,0},{8,12},{12,8},{16,20},{20,16},{24,28},{28,24},{1,5},{5... | collective-permute-start | bytes 393224 | tf_op jit(solution)/shard_map/ppermute | solution.py:163
  44.0 8.0 %collective-permute-start.11 = (bf16[4,128,128]{2,1,0:T(8,128)(2,1)S(1)}, bf16[4,128,128]{2,1,0:T(8,128)(2,1)S(1)}, u32[]{:S(2)}, u32[]{:S(2)}) collective-permute-start(bf16[4,128,128]{2,1,0:T(8,128)(2,1)S(1)} %get-tuple-element.30), channel_id=1, source_target_pairs={{0,12},{4,8},{8,4},{12,0},{16,28},{20,24},{24,20},{28,16},{1,13},{... | collective-permute-start | bytes 393224 | tf_op jit(solution)/shard_map/ppermute | solution.py:163
  45.6 19.6 %copy-start.3 = (bf16[128,256]{1,0:T(8,128)(2,1)S(1)}, bf16[128,256]{1,0:T(8,128)(2,1)}, u32[]{:S(2)}) copy-start(bf16[128,256]{1,0:T(8,128)(2,1)} %param.11) | copy-start | bytes 196612
  45.6 7.6 %collective-permute-start.10 = (bf16[4,128,128]{2,1,0:T(8,128)(2,1)S(1)}, bf16[4,128,128]{2,1,0:T(8,128)(2,1)S(1)}, u32[]{:S(2)}, u32[]{:S(2)}) collective-permute-start(bf16[4,128,128]{2,1,0:T(8,128)(2,1)S(1)} %get-tuple-element.31), channel_id=1, source_target_pairs={{0,8},{4,12},{8,0},{12,4},{16,24},{20,28},{24,16},{28,20},{1,9},{5... | collective-permute-start | bytes 393224 | tf_op jit(solution)/shard_map/ppermute | solution.py:163
  50.6 5.0 %collective-permute-start.6 = (bf16[4,128,128]{2,1,0:T(8,128)(2,1)S(1)}, bf16[4,128,128]{2,1,0:T(8,128)(2,1)S(1)}, u32[]{:S(2)}, u32[]{:S(2)}) collective-permute-start(bf16[4,128,128]{2,1,0:T(8,128)(2,1)S(1)} %slice.195), channel_id=1, source_target_pairs={{0,4},{4,0},{8,12},{12,8},{16,20},{20,16},{24,28},{28,24},{1,5},{5... | collective-permute-start | bytes 393224 | tf_op jit(solution)/shard_map/ppermute | solution.py:163
  53.3 5.6 %collective-permute-start.12 = (bf16[2,128,128]{2,1,0:T(8,128)(2,1)S(1)}, bf16[2,128,128]{2,1,0:T(8,128)(2,1)S(1)}, u32[]{:S(2)}, u32[]{:S(2)}) collective-permute-start(bf16[2,128,128]{2,1,0:T(8,128)(2,1)S(1)} %slice.196), channel_id=1, source_target_pairs={{0,16},{4,20},{8,24},{12,28},{16,0},{20,4},{24,8},{28,12},{1,17},{... | collective-permute-start | bytes 196616 | tf_op jit(solution)/shard_map/ppermute | solution.py:163
  55.6 4.3 %collective-permute-start.7 = (bf16[2,128,128]{2,1,0:T(8,128)(2,1)S(1)}, bf16[2,128,128]{2,1,0:T(8,128)(2,1)S(1)}, u32[]{:S(2)}, u32[]{:S(2)}) collective-permute-start(bf16[2,128,128]{2,1,0:T(8,128)(2,1)S(1)} %slice.197), channel_id=1, source_target_pairs={{0,8},{4,12},{8,0},{12,4},{16,24},{20,28},{24,16},{28,20},{1,9},{5... | collective-permute-start | bytes 196616 | tf_op jit(solution)/shard_map/ppermute | solution.py:163
  58.9 4.0 %collective-permute-start.13 = (bf16[1,128,128]{2,1,0:T(8,128)(2,1)S(1)}, bf16[1,128,128]{2,1,0:T(8,128)(2,1)S(1)}, u32[]{:S(2)}, u32[]{:S(2)}) collective-permute-start(bf16[1,128,128]{2,1,0:T(8,128)(2,1)S(1)} %slice.198), channel_id=1, source_target_pairs={{0,2},{1,3},{2,0},{3,1},{4,6},{5,7},{6,4},{7,5},{8,10},{9,11},{10,... | collective-permute-start | bytes 98312 | tf_op jit(solution)/shard_map/ppermute | solution.py:163
  60.0 5.2 %collective-permute-start.8 = (bf16[1,128,128]{2,1,0:T(8,128)(2,1)S(1)}, bf16[1,128,128]{2,1,0:T(8,128)(2,1)S(1)}, u32[]{:S(2)}, u32[]{:S(2)}) collective-permute-start(bf16[1,128,128]{2,1,0:T(8,128)(2,1)S(1)} %slice.199), channel_id=1, source_target_pairs={{0,16},{4,20},{8,24},{12,28},{16,0},{20,4},{24,8},{28,12},{1,17},{... | collective-permute-start | bytes 98312 | tf_op jit(solution)/shard_map/ppermute | solution.py:163
  66.0 5.3 %collective-permute-start.14 = (bf16[128,128]{1,0:T(8,128)(2,1)S(1)}, bf16[128,128]{1,0:T(8,128)(2,1)S(1)}, u32[]{:S(2)}, u32[]{:S(2)}) collective-permute-start(bf16[128,128]{1,0:T(8,128)(2,1)S(1)} %get-tuple-element.47), channel_id=1, source_target_pairs={{0,16},{4,20},{8,24},{12,28},{16,0},{20,4},{24,8},{28,12},{1,17},{... | collective-permute-start | bytes 98312 | tf_op jit(solution)/shard_map/ppermute | solution.py:163
  67.8 7.1 %collective-permute-start.19 = (bf16[128,128]{1,0:T(8,128)(2,1)S(1)}, bf16[128,128]{1,0:T(8,128)(2,1)S(1)}, u32[]{:S(2)}, u32[]{:S(2)}) collective-permute-start(bf16[128,128]{1,0:T(8,128)(2,1)S(1)} %get-tuple-element.46), channel_id=1, source_target_pairs={{0,16},{4,20},{8,24},{12,28},{16,0},{20,4},{24,8},{28,12},{1,17},{... | collective-permute-start | bytes 98312 | tf_op jit(solution)/shard_map/ppermute | solution.py:163
  71.3 4.8 %collective-permute-start.16 = (bf16[2,128,128]{2,1,0:T(8,128)(2,1)S(1)}, bf16[2,128,128]{2,1,0:T(8,128)(2,1)S(1)}, u32[]{:S(2)}, u32[]{:S(2)}) collective-permute-start(bf16[2,128,128]{2,1,0:T(8,128)(2,1)S(1)} %get-tuple-element.43), channel_id=1, source_target_pairs={{0,8},{4,12},{8,0},{12,4},{16,24},{20,28},{24,16},{28,20},{1,9},{5... | collective-permute-start | bytes 196616 | tf_op jit(solution)/shard_map/ppermute | solution.py:163
  71.7 4.4 %collective-permute-start.15 = (bf16[2,128,128]{2,1,0:T(8,128)(2,1)S(1)}, bf16[2,128,128]{2,1,0:T(8,128)(2,1)S(1)}, u32[]{:S(2)}, u32[]{:S(2)}) collective-permute-start(bf16[2,128,128]{2,1,0:T(8,128)(2,1)S(1)} %get-tuple-element.43), channel_id=1, source_target_pairs={{0,4},{4,0},{8,12},{12,8},{16,20},{20,16},{24,28},{28,24},{1,5},{5... | collective-permute-start | bytes 196616 | tf_op jit(solution)/shard_map/ppermute | solution.py:163
  73.1 5.8 %collective-permute-start.17 = (bf16[2,128,128]{2,1,0:T(8,128)(2,1)S(1)}, bf16[2,128,128]{2,1,0:T(8,128)(2,1)S(1)}, u32[]{:S(2)}, u32[]{:S(2)}) collective-permute-start(bf16[2,128,128]{2,1,0:T(8,128)(2,1)S(1)} %get-tuple-element.43), channel_id=1, source_target_pairs={{0,12},{4,8},{8,4},{12,0},{16,28},{20,24},{24,20},{28,16},{1,13},{... | collective-permute-start | bytes 196616 | tf_op jit(solution)/shard_map/ppermute | solution.py:163
  74.9 5.3 %collective-permute-start.20 = (bf16[2,128,128]{2,1,0:T(8,128)(2,1)S(1)}, bf16[2,128,128]{2,1,0:T(8,128)(2,1)S(1)}, u32[]{:S(2)}, u32[]{:S(2)}) collective-permute-start(bf16[2,128,128]{2,1,0:T(8,128)(2,1)S(1)} %get-tuple-element.49), channel_id=1, source_target_pairs={{0,2},{1,3},{2,0},{3,1},{4,6},{5,7},{6,4},{7,5},{8,10},{9,11},{10,... | collective-permute-start | bytes 196616 | tf_op jit(solution)/shard_map/ppermute | solution.py:163
  78.9 8.8 %collective-permute-start.18 = (bf16[4,2,128,128]{3,2,1,0:T(8,128)(2,1)S(1)}, bf16[4,2,128,128]{3,2,1,0:T(8,128)(2,1)S(1)}, u32[]{:S(2)}, u32[]{:S(2)}) collective-permute-start(bf16[4,2,128,128]{3,2,1,0:T(8,128)(2,1)S(1)} %pad_maximum_fusion.2), channel_id=1, source_target_pairs={{0,2},{1,3},{2,0},{3,1},{4,6},{5,7},{6,4},{7,5},{8,10},{9,11},{10,... | collective-permute-start | bytes 786440 | tf_op jit(solution)/shard_map/ppermute | solution.py:163
  80.2 5.0 %collective-permute-start.22 = (bf16[2,2,128,128]{3,2,1,0:T(8,128)(2,1)S(1)}, bf16[2,2,128,128]{3,2,1,0:T(8,128)(2,1)S(1)}, u32[]{:S(2)}, u32[]{:S(2)}) collective-permute-start(bf16[2,2,128,128]{3,2,1,0:T(8,128)(2,1)S(1)} %get-tuple-element.37), channel_id=1, source_target_pairs={{0,8},{4,12},{8,0},{12,4},{16,24},{20,28},{24,16},{28,20},{1,9},{5... | collective-permute-start | bytes 393224 | tf_op jit(solution)/shard_map/ppermute | solution.py:163
  80.3 5.0 %collective-permute-start.21 = (bf16[2,2,128,128]{3,2,1,0:T(8,128)(2,1)S(1)}, bf16[2,2,128,128]{3,2,1,0:T(8,128)(2,1)S(1)}, u32[]{:S(2)}, u32[]{:S(2)}) collective-permute-start(bf16[2,2,128,128]{3,2,1,0:T(8,128)(2,1)S(1)} %get-tuple-element.37), channel_id=1, source_target_pairs={{0,4},{4,0},{8,12},{12,8},{16,20},{20,16},{24,28},{28,24},{1,5},{5... | collective-permute-start | bytes 393224 | tf_op jit(solution)/shard_map/ppermute | solution.py:163
  81.7 5.9 %collective-permute-start.23 = (bf16[2,2,128,128]{3,2,1,0:T(8,128)(2,1)S(1)}, bf16[2,2,128,128]{3,2,1,0:T(8,128)(2,1)S(1)}, u32[]{:S(2)}, u32[]{:S(2)}) collective-permute-start(bf16[2,2,128,128]{3,2,1,0:T(8,128)(2,1)S(1)} %get-tuple-element.37), channel_id=1, source_target_pairs={{0,12},{4,8},{8,4},{12,0},{16,28},{20,24},{24,20},{28,16},{1,13},{... | collective-permute-start | bytes 393224 | tf_op jit(solution)/shard_map/ppermute | solution.py:163
  87.7 2.0 %collective-permute-start.25 = (bf16[2048,128]{1,0:T(8,128)(2,1)S(1)}, bf16[2048,128]{1,0:T(8,128)(2,1)S(1)}, u32[]{:S(2)}, u32[]{:S(2)}) collective-permute-start(bf16[2048,128]{1,0:T(8,128)(2,1)S(1)} %bitcast.79), channel_id=1, source_target_pairs={{0,1},{1,0},{2,3},{3,2},{4,5},{5,4},{6,7},{7,6},{8,9},{9,8},{10,11... | collective-permute-start | bytes 1572872 | tf_op jit(solution)/shard_map/ppermute | solution.py:163
  87.9 2.6 %collective-permute-start.24 = (bf16[2048,128]{1,0:T(8,128)(2,1)S(1)}, bf16[2048,128]{1,0:T(8,128)(2,1)S(1)}, u32[]{:S(2)}, u32[]{:S(2)}) collective-permute-start(bf16[2048,128]{1,0:T(8,128)(2,1)S(1)} %bitcast.81), channel_id=1, source_target_pairs={{0,1},{1,0},{2,3},{3,2},{4,5},{5,4},{6,7},{7,6},{8,9},{9,8},{10,11... | collective-permute-start | bytes 1572872 | tf_op jit(solution)/shard_map/ppermute | solution.py:163
  91.1 8.3 %collective-permute-start.30 = (bf16[192,256]{1,0:T(8,128)(2,1)S(1)}, bf16[192,256]{1,0:T(8,128)(2,1)S(1)}, u32[]{:S(2)}, u32[]{:S(2)}) collective-permute-start(bf16[192,256]{1,0:T(8,128)(2,1)S(1)} %get-tuple-element.34), channel_id=1, source_target_pairs={{0,16},{4,20},{8,24},{12,28},{16,0},{20,4},{24,8},{28,12},{1,17},{... | collective-permute-start | bytes 294920 | tf_op jit(solution)/shard_map/ppermute | solution.py:163
  94.1 6.9 %collective-permute-start.27 = (bf16[192,256]{1,0:T(8,128)(2,1)S(1)}, bf16[192,256]{1,0:T(8,128)(2,1)S(1)}, u32[]{:S(2)}, u32[]{:S(2)}) collective-permute-start(bf16[192,256]{1,0:T(8,128)(2,1)S(1)} %get-tuple-element.35), channel_id=1, source_target_pairs={{0,8},{4,12},{8,0},{12,4},{16,24},{20,28},{24,16},{28,20},{1,9},{5... | collective-permute-start | bytes 294920 | tf_op jit(solution)/shard_map/ppermute | solution.py:163
  95.1 5.9 %collective-permute-start.26 = (bf16[192,256]{1,0:T(8,128)(2,1)S(1)}, bf16[192,256]{1,0:T(8,128)(2,1)S(1)}, u32[]{:S(2)}, u32[]{:S(2)}) collective-permute-start(bf16[192,256]{1,0:T(8,128)(2,1)S(1)} %get-tuple-element.35), channel_id=1, source_target_pairs={{0,4},{4,0},{8,12},{12,8},{16,20},{20,16},{24,28},{28,24},{1,5},{5... | collective-permute-start | bytes 294920 | tf_op jit(solution)/shard_map/ppermute | solution.py:163
  96.6 5.5 %collective-permute-start.28 = (bf16[192,256]{1,0:T(8,128)(2,1)S(1)}, bf16[192,256]{1,0:T(8,128)(2,1)S(1)}, u32[]{:S(2)}, u32[]{:S(2)}) collective-permute-start(bf16[192,256]{1,0:T(8,128)(2,1)S(1)} %get-tuple-element.35), channel_id=1, source_target_pairs={{0,12},{4,8},{8,4},{12,0},{16,28},{20,24},{24,20},{28,16},{1,13},{... | collective-permute-start | bytes 294920 | tf_op jit(solution)/shard_map/ppermute | solution.py:163
  102.2 6.1 %collective-permute-start.33 = (bf16[192,256]{1,0:T(8,128)(2,1)S(1)}, bf16[192,256]{1,0:T(8,128)(2,1)S(1)}, u32[]{:S(2)}, u32[]{:S(2)}) collective-permute-start(bf16[192,256]{1,0:T(8,128)(2,1)S(1)} %get-tuple-element.32), channel_id=1, source_target_pairs={{0,12},{4,8},{8,4},{12,0},{16,28},{20,24},{24,20},{28,16},{1,13},{... | collective-permute-start | bytes 294920 | tf_op jit(solution)/shard_map/ppermute | solution.py:163
  104.2 6.4 %collective-permute-start.32 = (bf16[192,256]{1,0:T(8,128)(2,1)S(1)}, bf16[192,256]{1,0:T(8,128)(2,1)S(1)}, u32[]{:S(2)}, u32[]{:S(2)}) collective-permute-start(bf16[192,256]{1,0:T(8,128)(2,1)S(1)} %get-tuple-element.32), channel_id=1, source_target_pairs={{0,8},{4,12},{8,0},{12,4},{16,24},{20,28},{24,16},{28,20},{1,9},{5... | collective-permute-start | bytes 294920 | tf_op jit(solution)/shard_map/ppermute | solution.py:163
  105.4 5.3 %collective-permute-start.31 = (bf16[192,256]{1,0:T(8,128)(2,1)S(1)}, bf16[192,256]{1,0:T(8,128)(2,1)S(1)}, u32[]{:S(2)}, u32[]{:S(2)}) collective-permute-start(bf16[192,256]{1,0:T(8,128)(2,1)S(1)} %get-tuple-element.32), channel_id=1, source_target_pairs={{0,4},{4,0},{8,12},{12,8},{16,20},{20,16},{24,28},{28,24},{1,5},{5... | collective-permute-start | bytes 294920 | tf_op jit(solution)/shard_map/ppermute | solution.py:163
  105.8 6.8 %collective-permute-start.29 = (bf16[192,256]{1,0:T(8,128)(2,1)S(1)}, bf16[192,256]{1,0:T(8,128)(2,1)S(1)}, u32[]{:S(2)}, u32[]{:S(2)}) collective-permute-start(bf16[192,256]{1,0:T(8,128)(2,1)S(1)} %get-tuple-element.33), channel_id=1, source_target_pairs={{0,16},{4,20},{8,24},{12,28},{16,0},{20,4},{24,8},{28,12},{1,17},{... | collective-permute-start | bytes 294920 | tf_op jit(solution)/shard_map/ppermute | solution.py:163

commit v5 on v4

--- a/solution.py
+++ b/solution.py
@@ -96,36 +96,36 @@
     flat[pl.ds(1, count, stride=2), :] = jnp.transpose(jnp.concatenate([rest, rest], axis=0))
 
 
-def owner_kernel(tgt_bits, unroll, asked_ref, key_ref, table_ref, self_ref, neighbor_ref,
-                 keep_ref, send_ref, sums_ref, held, dense, weights):
+def settle(held, into):
+    count = held.shape[0]
+    flat = held.reshape(2 * count, 128)
+    into[:, :128] = flat[pl.ds(0, count, stride=2), :].astype(BF16)
+    into[:, 128:] = flat[pl.ds(1, count, stride=2), :].astype(BF16)
+
+
+def first_kernel(unroll, asked_ref, table_ref, out_ref, held):
+    def fetch(block, carry):
+        first = block * unroll
+        into = held.at[pl.ds(first, unroll)]
+        for u in range(unroll):
+            into[u] = table_ref[asked_ref[first + u]]
+        return carry
+
+    lax.fori_loop(0, held.shape[0] // unroll, fetch, 0)
+    settle(held, out_ref)
+
+
+def owner_kernel(tgt_bits, asked_ref, key_ref, table_ref, first_ref, near_ref, beside_ref, held, dense):
     step = pl.program_id(0)
     count = pl.num_programs(0)
     capacity = held.shape[0]
-    columns = self_ref.shape[0]
     targets = 1 << tgt_bits
     share = targets // 4
     now = step & 1
-    flat = held.reshape(2 * capacity, 128)
-
-    def settle(slot):
-        dense[slot, :, :128] = flat[pl.ds(0, capacity, stride=2), :].astype(BF16)
-        dense[slot, :, 128:] = flat[pl.ds(1, capacity, stride=2), :].astype(BF16)
 
     @pl.when(step == 0)
     def _():
-        weights[:columns] = self_ref[...]
-        weights[columns : columns + 64] = neighbor_ref[128:]
-        weights[columns + 64 :] = neighbor_ref[:128]
-
-        def fetch(block, carry):
-            first = block * unroll
-            into = held.at[pl.ds(first, unroll)]
-            for u in range(unroll):
-                into[u] = table_ref[asked_ref[first + u]]
-            return carry
-
-        lax.fori_loop(0, capacity // unroll, fetch, 0)
-        settle(0)
+        dense[0] = first_ref[...]
 
     def serve(fetches):
         key = key_ref[step][:, capacity:] - 1
@@ -144,15 +144,14 @@
         lane = lax.broadcasted_iota(jnp.int32, (targets, 128), 1)
         mid = jnp.where(lane < 64, own[:, 128:], mean[:, 128:])
         summed = jnp.concatenate([own[:, :128], mid, mean[:, :128]], axis=1).astype(BF16)
-        preact = jnp.dot(summed, weights[...], preferred_element_type=F32).astype(BF16)
-        sums_ref[:, 0] = summed.reshape(4, share, summed.shape[1])
-        keep_ref[:, 0] = preact[: 2 * share].reshape(2, share, preact.shape[1])
-        send_ref[:, 0] = preact[2 * share :].reshape(2, share, preact.shape[1])
+        halves = summed.reshape(2, 2, share, summed.shape[1])
+        near_ref[:, 0] = halves[0]
+        beside_ref[:, 0] = halves[1]
         if fetches:
             ahead = 2 * (step + 1) * capacity
             for i in range(capacity):
                 held[i] = table_ref[asked_ref[ahead + i]]
-            settle(1 - now)
+            settle(held, dense.at[1 - now])
 
     pl.when(step + 1 < count)(lambda: serve(True))
     pl.when(step + 1 == count)(lambda: serve(False))
@@ -235,6 +234,9 @@
         both = jnp.transpose(parts[0].reshape(2, wide_count, capacity), (1, 0, 2))
         parts = list(both.reshape(4, wide_count // 4, 2 * capacity))
     bits = wide_count.bit_length() - 1
+    weights = jnp.concatenate(
+        [w_self, w_neighbor[128:], w_neighbor[:128]], axis=0
+    )
     came = [swap(parts[m], "wide", m) for m in range(1, 4)]
     came, table = lax.optimization_barrier((came, table))
     asked = jnp.stack([parts[0]] + came).reshape(4, wide_count // 4, 2 * capacity)
@@ -243,49 +245,60 @@
         asked = jnp.concatenate([split[:, :, 0], swap(split[:, :, 1], "wide", 1 << b)], axis=0)
 
     unroll = next(u for u in (128, 64, 32, 16, 8, 4, 2, 1) if capacity % u == 0)
-    halves = jax.ShapeDtypeStruct((2, wide_count, share, hidden_units), BF16)
     whole = pl.BlockSpec(memory_space=pltpu.VMEM)
-    keep, send, sums = pl.pallas_call(
-        functools.partial(owner_kernel, tgt_bits, unroll),
+    first = pl.pallas_call(
+        functools.partial(first_kernel, unroll),
+        grid_spec=pltpu.PrefetchScalarGridSpec(
+            num_scalar_prefetch=1,
+            grid=(1,),
+            in_specs=[whole],
+            out_specs=whole,
+            scratch_shapes=[pltpu.VMEM((capacity, 2, 128), F32)],
+        ),
+        out_shape=jax.ShapeDtypeStruct((capacity, 256), BF16),
+        compiler_params=pltpu.CompilerParams(vmem_limit_bytes=10 * MIB),
+        cost_estimate=pl.CostEstimate(flops=0, bytes_accessed=4 * MIB, transcendentals=0),
+        name="first",
+    )(parts[0].reshape(-1), table)
+    half_sums = (2, wide_count, share, 2 * columns)
+    near_sums, beside_sums = pl.pallas_call(
+        functools.partial(owner_kernel, tgt_bits),
         grid_spec=pltpu.PrefetchScalarGridSpec(
             num_scalar_prefetch=1,
             grid=(wide_count,),
-            in_specs=[whole] * 4,
+            in_specs=[whole] * 3,
             out_specs=[
-                pl.BlockSpec((2, 1, share, hidden_units), lambda s, *_: (0, s, 0, 0)),
-                pl.BlockSpec((2, 1, share, hidden_units), lambda s, *_: (0, s, 0, 0)),
-                pl.BlockSpec((4, 1, share, 2 * columns), lambda s, *_: (0, s, 0, 0)),
-            ],
+                pl.BlockSpec((2, 1, share, 2 * columns), lambda s, *_: (0, s, 0, 0))
+            ] * 2,
             scratch_shapes=[
                 pltpu.VMEM((capacity, 2, 128), F32),
                 pltpu.VMEM((2, capacity, 256), BF16),
-                pltpu.VMEM((2 * columns, hidden_units), BF16),
             ],
         ),
-        out_shape=[
-            halves,
-            halves,
-            jax.ShapeDtypeStruct((4, wide_count, share, 2 * columns), BF16),
-        ],
+        out_shape=[jax.ShapeDtypeStruct(half_sums, BF16)] * 2,
         compiler_params=pltpu.CompilerParams(vmem_limit_bytes=30 * MIB),
         name="owner",
-    )(asked.reshape(-1), asked.reshape(wide_count, 1, 2 * capacity), table, w_self, w_neighbor)
-
+    )(asked.reshape(-1), asked.reshape(wide_count, 1, 2 * capacity), table, first)
+    rows = 2 * wide_count * share
+    ours = near_sums.reshape(rows, 2 * columns)
+    theirs = beside_sums.reshape(rows, 2 * columns)
     far = ("narrow", (2,))
     steps = [("wide", (1 << b,)) for b in range(bits)]
     pair = ("wide", (2, 1))
-    ways = [[far] + steps, [pair] + steps[2:] + [far]]
+    ways = [[far] + steps, [pair, far] + steps[2:]]
     backs = [steps[:1:-1] + [pair, far], steps[:1:-1] + [far, pair]]
-    pieces = (2,) * (1 + bits) + (share, hidden_units)
-    paired = keep.astype(F32).reshape(pieces) + swap(send, "narrow", 1).astype(F32).reshape(pieces)
-    chains = [
-        jnp.transpose(paired[..., c * half : (c + 1) * half], dims_of(way, bits) + [bits + 1, bits + 2])
-        for c, way in enumerate(ways)
-    ]
+    pieces = (2,) * (1 + bits) + (share, half)
+    chains = []
+    for c, way in enumerate(ways):
+        columns_of = weights[:, c * half : (c + 1) * half]
+        send = jnp.dot(theirs, columns_of, preferred_element_type=F32).astype(BF16)
+        keep = lax.optimization_barrier(jnp.dot(ours, columns_of, preferred_element_type=F32))
+        paired = keep.reshape(pieces) + swap(send, "narrow", 1).reshape(pieces)
+        chains.append(jnp.transpose(paired, dims_of(way, bits) + [bits + 1, bits + 2]))
     for s in range(max(map(len, ways))):
-        for c, way in enumerate(ways):
-            if s < len(way):
-                chains[c] = add_across(chains[c], *way[s])
+        for c in (0, 1):
+            if s < len(ways[c]):
+                chains[c] = add_across(chains[c], *ways[c][s])
     preact = jnp.concatenate([chain.reshape(share, half) for chain in chains], axis=1)
     value, pullback = jax.vjp(activation, preact)
     hidden = value.astype(BF16)
@@ -303,16 +316,13 @@
         whole_chain = chains[c].reshape((2,) * (1 + bits) + (share, half))
         near.append(jnp.transpose(whole_chain, order).reshape(-1, half))
     beside = [swap(n, "narrow", 1) for n in near]
-    rows = 2 * wide_count * share
-    ours = sums[:2].reshape(rows, 2 * columns)
-    theirs = sums[2:].reshape(rows, 2 * columns)
     grads = contract_rows(ours, jnp.concatenate(near, axis=1)) + contract_rows(
         theirs, jnp.concatenate(beside, axis=1)
     )
     chains = [grads[:columns], grads[columns:]]
     turns = [[pair] + steps[2:], steps[2:] + [pair]]
     for s in range(len(turns[0])):
-        for c in range(2):
+        for c in (0, 1):
             chains[c] = add_all(chains[c], *turns[c][s])
     grad_self, mixed = chains
     grad_neighbor = jnp.concatenate([mixed[columns - 128 :], mixed[: columns - 128]], axis=0)

time: 113 us -> 112 us (level)
  waiting for transfers between devices: 38.2 us -> 35 us
  matrix products: 1.22 us -> 3.51 us
    ppermute x34 -> x35, waiting for transfers between devices: 38.2 us -> 35 us  [swap(): return lax.ppermute(value, axis, [(i, i ^ bit) for i in range(count)])]
    dot_general x0 -> x4, matrix products: none -> 2.28 us  [the longest x2 1.15 us: on_device(): send = jnp.dot(theirs, columns_of, preferred_element_type=F32).astype(BF16)]
    pallas_call x1 -> x2, Pallas kernels: 19.8 us -> 20.3 us  [the longest x1 17.6 us: on_device(): pl.pallas_call(functools.partial(owner_kernel, tgt_bits), grid_spec=pltpu...]
    ppermute x34 -> x35, starting transfers between devices: 42.3 us -> 42.1 us  [swap(): return lax.ppermute(value, axis, [(i, i ^ bit) for i in range(count)])]
  transfers between devices with their start and end apart: 34 -> 35, of which waited for: 25 -> 23; matrix products, arithmetic and copies ran while one was open for 2% -> 3% of each run, Pallas kernels for 1% -> 4%
where the time goes in v5:
time: 112 us
  starting transfers between devices  42.1 us (38%)
  waiting for transfers between devices  35 us (31%)
  Pallas kernels  25.1 us (22%)
  matrix products  3.51 us (3%)
  other arithmetic  2.91 us (3%)
  local copies, waits for them, and re-layouts  2.32 us (2%)
    ppermute x35, starting transfers between devices, swap(): return lax.ppermute(value, axis, [(i, i ^ bit) for i in range(count)])  42.1 us
    ppermute x35, waiting for transfers between devices, swap(): return lax.ppermute(value, axis, [(i, i ^ bit) for i in range(count)])  35 us
    pallas_call x1, Pallas kernels, on_device(): pl.pallas_call(functools.partial(owner_kernel, tgt_bits), grid_spec=pltpu...  17.6 us
    pallas_call x1, Pallas kernels, on_device(): pl.pallas_call(functools.partial(list_kernel, wide_count, capacity, tgt_b...  3.17 us
    pallas_call x1, Pallas kernels, on_device(): pl.pallas_call(functools.partial(first_kernel, unroll), grid_spec=pltpu.P...  2.75 us
  transfers between devices with their start and end apart: 35, of which 23 were waited for; matrix products, arithmetic and copies ran while one was open for 3% of the time, Pallas kernels for 4%

profile of v5, /device:TPU:0, one launch (start us, length us, event | category | flops | bytes accessed | tf_op | source)
XLA Modules:
  0.0 112.0 jit_solution(12132031169318176919)
XLA Ops:
  0.6 3.2 %lists.1 = (s32[48,128]{1,0:T(8,128)}, s32[48,128]{1,0:T(8,128)}, s32[48,128]{1,0:T(8,128)}, s32[48,128]{1,0:T(8,128)}) custom-call(s32[16,1,512]{2,1,0:T(1,128)} %bitcast.105, s32[16,512]{1,0:T(8,128)} %bitcast.106), custom_call_target="tpu_custom_call" | custom-call | tf_op jit(solution)/shard_map/lists/pallas_call | solution.py:227
  3.8 3.0 %collective-permute-start = (s32[48,128]{1,0:T(8,128)}, s32[48,128]{1,0:T(8,128)S(1)}, u32[]{:S(2)}, u32[]{:S(2)}) collective-permute-start(s32[48,128]{1,0:T(8,128)} %get-tuple-element.14), channel_id=1, source_target_pairs={{0,4},{4,0},{8,12},{12,8},{16,20},{20,16},{24,28},{28,24},{1,5},{5... | collective-permute-start | bytes 73736 | tf_op jit(solution)/shard_map/ppermute | solution.py:162
  6.8 1.6 %collective-permute-start.1 = (s32[48,128]{1,0:T(8,128)}, s32[48,128]{1,0:T(8,128)S(1)}, u32[]{:S(2)}, u32[]{:S(2)}) collective-permute-start(s32[48,128]{1,0:T(8,128)} %get-tuple-element.15), channel_id=1, source_target_pairs={{0,8},{4,12},{8,0},{12,4},{16,24},{20,28},{24,16},{28,20},{1,9},{5... | collective-permute-start | bytes 73736 | tf_op jit(solution)/shard_map/ppermute | solution.py:162
  8.3 1.9 %copy-done = bf16[192,8192]{1,0:T(8,128)(2,1)S(1)} copy-done((bf16[192,8192]{1,0:T(8,128)(2,1)S(1)}, bf16[192,8192]{1,0:T(8,128)(2,1)}, u32[]{:S(2)}) %copy-start) | copy-done | bytes 3145752
  10.2 1.6 %table.1.table_ref = f32[8192,2,128]{2,1,0:T(2,128)S(1)} custom-call(bf16[192,8192]{1,0:T(8,128)(2,1)S(1)} %copy-done), custom_call_target="tpu_custom_call" | custom-call | bytes 25165824 | tf_op jit(solution)/shard_map/table/pallas_call | solution.py:214
  11.9 1.4 %collective-permute-done.2 = s32[48,128]{1,0:T(8,128)S(1)} collective-permute-done((s32[48,128]{1,0:T(8,128)}, s32[48,128]{1,0:T(8,128)S(1)}, u32[]{:S(2)}, u32[]{:S(2)}) %collective-permute-start.2) | collective-permute-done | bytes 24608 | tf_op jit(solution)/shard_map/ppermute | solution.py:162
  13.3 2.7 %collective-permute-start.3 = (s32[4,1,3072]{2,1,0:T(1,128)S(1)}, s32[4,1,3072]{2,1,0:T(1,128)S(1)}, u32[]{:S(2)}, u32[]{:S(2)}) collective-permute-start(s32[4,1,3072]{2,1,0:T(1,128)S(1)} %get-tuple-element.35), channel_id=1, source_target_pairs={{0,16},{4,20},{8,24},{12,28},{16,0},{20,4},{24,8},{28,12},{1,17},{... | collective-permute-start | bytes 147464 | tf_op jit(solution)/shard_map/ppermute | solution.py:162
  16.0 2.7 %first.1.first_ref = bf16[1536,256]{1,0:T(8,128)(2,1)S(1)} custom-call(s32[6144]{0:T(1024)S(1)} %bitcast.85, f32[8192,2,128]{2,1,0:T(2,128)S(1)} %table.1.table_ref), custom_call_target="tpu_custom_call" | custom-call | bytes 4194304 | tf_op jit(solution)/shard_map/first/pallas_call | solution.py:249
  18.9 17.6 %owner.1 = (bf16[2,8,128,384]{3,2,1,0:T(8,128)(2,1)S(1)}, bf16[2,8,128,384]{3,2,1,0:T(8,128)(2,1)S(1)}) custom-call(s32[24576]{0:T(1024)S(1)} %bitcast.83, s32[8,1,3072]{2,1,0:T(1,128)S(1)} %pad_add_fusion.1.key_ref, f32[8192,2,128]{2,1,0:T(2,128)S(1)} %table.1.table_ref, bf16[1536,256]{1,0:T(8,128)(2,1)S(1)} %first.1.first_ref), custom_call_target="tpu_custom_call" | custom-call | tf_op jit(solution)/shard_map/owner/pallas_call | solution.py:264
  39.8 1.6 %collective-permute-start.5 = (bf16[8,128,128]{2,1,0:T(8,128)(2,1)S(1)}, bf16[8,128,128]{2,1,0:T(8,128)(2,1)S(1)}, u32[]{:S(2)}, u32[]{:S(2)}) collective-permute-start(bf16[8,128,128]{2,1,0:T(8,128)(2,1)S(1)} %bitcast.97), channel_id=1, source_target_pairs={{0,2},{1,3},{2,0},{3,1},{4,6},{5,7},{6,4},{7,5},{8,10},{9,11},{10,... | collective-permute-start | bytes 786440 | tf_op jit(solution)/shard_map/ppermute | solution.py:162
  42.2 1.6 %collective-permute-start.11 = (bf16[4,128,128]{2,1,0:T(8,128)(2,1)S(1)}, bf16[4,128,128]{2,1,0:T(8,128)(2,1)S(1)}, u32[]{:S(2)}, u32[]{:S(2)}) collective-permute-start(bf16[4,128,128]{2,1,0:T(8,128)(2,1)S(1)} %get-tuple-element.25), channel_id=1, source_target_pairs={{0,8},{4,12},{8,0},{12,4},{16,24},{20,28},{24,16},{28,20},{1,9},{5... | collective-permute-start | bytes 393224 | tf_op jit(solution)/shard_map/ppermute | solution.py:162
  43.8 1.5 %collective-permute-start.12 = (bf16[4,128,128]{2,1,0:T(8,128)(2,1)S(1)}, bf16[4,128,128]{2,1,0:T(8,128)(2,1)S(1)}, u32[]{:S(2)}, u32[]{:S(2)}) collective-permute-start(bf16[4,128,128]{2,1,0:T(8,128)(2,1)S(1)} %get-tuple-element.24), channel_id=1, source_target_pairs={{0,12},{4,8},{8,4},{12,0},{16,28},{20,24},{24,20},{28,16},{1,13},{... | collective-permute-start | bytes 393224 | tf_op jit(solution)/shard_map/ppermute | solution.py:162
  45.3 2.9 %collective-permute-done.5 = bf16[8,128,128]{2,1,0:T(8,128)(2,1)S(1)} collective-permute-done((bf16[8,128,128]{2,1,0:T(8,128)(2,1)S(1)}, bf16[8,128,128]{2,1,0:T(8,128)(2,1)S(1)}, u32[]{:S(2)}, u32[]{:S(2)}) %collective-permute-start.5) | collective-permute-done | bytes 262176 | tf_op jit(solution)/shard_map/ppermute | solution.py:162
  48.8 2.3 %collective-permute-done.12 = bf16[4,128,128]{2,1,0:T(8,128)(2,1)S(1)} collective-permute-done((bf16[4,128,128]{2,1,0:T(8,128)(2,1)S(1)}, bf16[4,128,128]{2,1,0:T(8,128)(2,1)S(1)}, u32[]{:S(2)}, u32[]{:S(2)}) %collective-permute-start.12) | collective-permute-done | bytes 131104 | tf_op jit(solution)/shard_map/ppermute | solution.py:162
  51.2 0.8 collective-permute-start.13
  52.0 1.9 %collective-permute-done.6 = bf16[4,128,128]{2,1,0:T(8,128)(2,1)S(1)} collective-permute-done((bf16[4,128,128]{2,1,0:T(8,128)(2,1)S(1)}, bf16[4,128,128]{2,1,0:T(8,128)(2,1)S(1)}, u32[]{:S(2)}, u32[]{:S(2)}) %collective-permute-start.6) | collective-permute-done | bytes 131104 | tf_op jit(solution)/shard_map/ppermute | solution.py:162
  54.5 1.1 collective-permute-done.13
  55.6 2.1 %collective-permute-start.14 = (bf16[1,128,128]{2,1,0:T(8,128)(2,1)S(1)}, bf16[1,128,128]{2,1,0:T(8,128)(2,1)S(1)}, u32[]{:S(2)}, u32[]{:S(2)}) collective-permute-start(bf16[1,128,128]{2,1,0:T(8,128)(2,1)S(1)} %slice.204), channel_id=1, source_target_pairs={{0,16},{4,20},{8,24},{12,28},{16,0},{20,4},{24,8},{28,12},{1,17},{... | collective-permute-start | bytes 98312 | tf_op jit(solution)/shard_map/ppermute | solution.py:162
  58.3 2.1 %collective-permute-start.8 = (bf16[1,128,128]{2,1,0:T(8,128)(2,1)S(1)}, bf16[1,128,128]{2,1,0:T(8,128)(2,1)S(1)}, u32[]{:S(2)}, u32[]{:S(2)}) collective-permute-start(bf16[1,128,128]{2,1,0:T(8,128)(2,1)S(1)} %slice.205), channel_id=1, source_target_pairs={{0,16},{4,20},{8,24},{12,28},{16,0},{20,4},{24,8},{28,12},{1,17},{... | collective-permute-start | bytes 98312 | tf_op jit(solution)/shard_map/ppermute | solution.py:162
  60.4 0.8 collective-permute-done.14
  61.2 2.3 %collective-permute-done.8 = bf16[1,128,128]{2,1,0:T(8,128)(2,1)S(1)} collective-permute-done((bf16[1,128,128]{2,1,0:T(8,128)(2,1)S(1)}, bf16[1,128,128]{2,1,0:T(8,128)(2,1)S(1)}, u32[]{:S(2)}, u32[]{:S(2)}) %collective-permute-start.8) | collective-permute-done | bytes 32800 | tf_op jit(solution)/shard_map/ppermute | solution.py:162
  63.5 0.7 fusion.13
  64.3 1.8 %collective-permute-start.15 = (bf16[128,128]{1,0:T(8,128)(2,1)S(1)}, bf16[128,128]{1,0:T(8,128)(2,1)S(1)}, u32[]{:S(2)}, u32[]{:S(2)}) collective-permute-start(bf16[128,128]{1,0:T(8,128)(2,1)S(1)} %get-tuple-element.41), channel_id=1, source_target_pairs={{0,16},{4,20},{8,24},{12,28},{16,0},{20,4},{24,8},{28,12},{1,17},{... | collective-permute-start | bytes 98312 | tf_op jit(solution)/shard_map/ppermute | solution.py:162
  66.1 1.1 %collective-permute-start.20 = (bf16[128,128]{1,0:T(8,128)(2,1)S(1)}, bf16[128,128]{1,0:T(8,128)(2,1)S(1)}, u32[]{:S(2)}, u32[]{:S(2)}) collective-permute-start(bf16[128,128]{1,0:T(8,128)(2,1)S(1)} %get-tuple-element.40), channel_id=1, source_target_pairs={{0,16},{4,20},{8,24},{12,28},{16,0},{20,4},{24,8},{28,12},{1,17},{... | collective-permute-start | bytes 98312 | tf_op jit(solution)/shard_map/ppermute | solution.py:162
  67.3 2.1 %collective-permute-done.15 = bf16[128,128]{1,0:T(8,128)(2,1)S(1)} collective-permute-done((bf16[128,128]{1,0:T(8,128)(2,1)S(1)}, bf16[128,128]{1,0:T(8,128)(2,1)S(1)}, u32[]{:S(2)}, u32[]{:S(2)}) %collective-permute-start.15) | collective-permute-done | bytes 32800 | tf_op jit(solution)/shard_map/ppermute | solution.py:162
  70.0 1.0 collective-permute-start.17
  71.0 1.9 %collective-permute-start.18 = (bf16[2,128,128]{2,1,0:T(8,128)(2,1)S(1)}, bf16[2,128,128]{2,1,0:T(8,128)(2,1)S(1)}, u32[]{:S(2)}, u32[]{:S(2)}) collective-permute-start(bf16[2,128,128]{2,1,0:T(8,128)(2,1)S(1)} %get-tuple-element.37), channel_id=1, source_target_pairs={{0,12},{4,8},{8,4},{12,0},{16,28},{20,24},{24,20},{28,16},{1,13},{... | collective-permute-start | bytes 196616 | tf_op jit(solution)/shard_map/ppermute | solution.py:162
  73.0 1.4 %collective-permute-start.21 = (bf16[2,128,128]{2,1,0:T(8,128)(2,1)S(1)}, bf16[2,128,128]{2,1,0:T(8,128)(2,1)S(1)}, u32[]{:S(2)}, u32[]{:S(2)}) collective-permute-start(bf16[2,128,128]{2,1,0:T(8,128)(2,1)S(1)} %get-tuple-element.43), channel_id=1, source_target_pairs={{0,2},{1,3},{2,0},{3,1},{4,6},{5,7},{6,4},{7,5},{8,10},{9,11},{10,... | collective-permute-start | bytes 196616 | tf_op jit(solution)/shard_map/ppermute | solution.py:162
  74.4 2.1 %collective-permute-done.18 = bf16[2,128,128]{2,1,0:T(8,128)(2,1)S(1)} collective-permute-done((bf16[2,128,128]{2,1,0:T(8,128)(2,1)S(1)}, bf16[2,128,128]{2,1,0:T(8,128)(2,1)S(1)}, u32[]{:S(2)}, u32[]{:S(2)}) %collective-permute-start.18) | collective-permute-done | bytes 65568 | tf_op jit(solution)/shard_map/ppermute | solution.py:162
  76.6 1.1 collective-permute-start.19
  77.8 1.1 collective-permute-start.22
  78.9 1.9 %collective-permute-start.23 = (bf16[2,2,128,128]{3,2,1,0:T(8,128)(2,1)S(1)}, bf16[2,2,128,128]{3,2,1,0:T(8,128)(2,1)S(1)}, u32[]{:S(2)}, u32[]{:S(2)}) collective-permute-start(bf16[2,2,128,128]{3,2,1,0:T(8,128)(2,1)S(1)} %get-tuple-element.31), channel_id=1, source_target_pairs={{0,8},{4,12},{8,0},{12,4},{16,24},{20,28},{24,16},{28,20},{1,9},{5... | collective-permute-start | bytes 393224 | tf_op jit(solution)/shard_map/ppermute | solution.py:162
  81.4 1.5 %collective-permute-done.22 = bf16[2,2,128,128]{3,2,1,0:T(8,128)(2,1)S(1)} collective-permute-done((bf16[2,2,128,128]{3,2,1,0:T(8,128)(2,1)S(1)}, bf16[2,2,128,128]{3,2,1,0:T(8,128)(2,1)S(1)}, u32[]{:S(2)}, u32[]{:S(2)}) %collective-permute-start.22) | collective-permute-done | bytes 131104 | tf_op jit(solution)/shard_map/ppermute | solution.py:162
  82.9 1.0 collective-permute-done.23
  83.9 2.8 %collective-permute-done.24 = bf16[2,2,128,128]{3,2,1,0:T(8,128)(2,1)S(1)} collective-permute-done((bf16[2,2,128,128]{3,2,1,0:T(8,128)(2,1)S(1)}, bf16[2,2,128,128]{3,2,1,0:T(8,128)(2,1)S(1)}, u32[]{:S(2)}, u32[]{:S(2)}) %collective-permute-start.24) | collective-permute-done | bytes 131104 | tf_op jit(solution)/shard_map/ppermute | solution.py:162
  88.1 0.6 collective-permute-done.26
  88.8 0.7 collective-permute-done.25
  90.3 1.9 %collective-permute-start.28 = (bf16[192,256]{1,0:T(8,128)(2,1)S(1)}, bf16[192,256]{1,0:T(8,128)(2,1)S(1)}, u32[]{:S(2)}, u32[]{:S(2)}) collective-permute-start(bf16[192,256]{1,0:T(8,128)(2,1)S(1)} %get-tuple-element.29), channel_id=1, source_target_pairs={{0,8},{4,12},{8,0},{12,4},{16,24},{20,28},{24,16},{28,20},{1,9},{5... | collective-permute-start | bytes 294920 | tf_op jit(solution)/shard_map/ppermute | solution.py:162
  92.2 1.5 %collective-permute-start.29 = (bf16[192,256]{1,0:T(8,128)(2,1)S(1)}, bf16[192,256]{1,0:T(8,128)(2,1)S(1)}, u32[]{:S(2)}, u32[]{:S(2)}) collective-permute-start(bf16[192,256]{1,0:T(8,128)(2,1)S(1)} %get-tuple-element.29), channel_id=1, source_target_pairs={{0,12},{4,8},{8,4},{12,0},{16,28},{20,24},{24,20},{28,16},{1,13},{... | collective-permute-start | bytes 294920 | tf_op jit(solution)/shard_map/ppermute | solution.py:162
  93.7 1.9 %collective-permute-start.31 = (bf16[192,256]{1,0:T(8,128)(2,1)S(1)}, bf16[192,256]{1,0:T(8,128)(2,1)S(1)}, u32[]{:S(2)}, u32[]{:S(2)}) collective-permute-start(bf16[192,256]{1,0:T(8,128)(2,1)S(1)} %get-tuple-element.28), channel_id=1, source_target_pairs={{0,16},{4,20},{8,24},{12,28},{16,0},{20,4},{24,8},{28,12},{1,17},{... | collective-permute-start | bytes 294920 | tf_op jit(solution)/shard_map/ppermute | solution.py:162
  95.9 4.6 %collective-permute-done.29 = bf16[192,256]{1,0:T(8,128)(2,1)S(1)} collective-permute-done((bf16[192,256]{1,0:T(8,128)(2,1)S(1)}, bf16[192,256]{1,0:T(8,128)(2,1)S(1)}, u32[]{:S(2)}, u32[]{:S(2)}) %collective-permute-start.29) | collective-permute-done | bytes 98336 | tf_op jit(solution)/shard_map/ppermute | solution.py:162
  101.3 1.9 %collective-permute-start.33 = (bf16[192,256]{1,0:T(8,128)(2,1)S(1)}, bf16[192,256]{1,0:T(8,128)(2,1)S(1)}, u32[]{:S(2)}, u32[]{:S(2)}) collective-permute-start(bf16[192,256]{1,0:T(8,128)(2,1)S(1)} %get-tuple-element.26), channel_id=1, source_target_pairs={{0,8},{4,12},{8,0},{12,4},{16,24},{20,28},{24,16},{28,20},{1,9},{5... | collective-permute-start | bytes 294920 | tf_op jit(solution)/shard_map/ppermute | solution.py:162
  103.1 1.6 %collective-permute-start.34 = (bf16[192,256]{1,0:T(8,128)(2,1)S(1)}, bf16[192,256]{1,0:T(8,128)(2,1)S(1)}, u32[]{:S(2)}, u32[]{:S(2)}) collective-permute-start(bf16[192,256]{1,0:T(8,128)(2,1)S(1)} %get-tuple-element.26), channel_id=1, source_target_pairs={{0,12},{4,8},{8,4},{12,0},{16,28},{20,24},{24,20},{28,16},{1,13},{... | collective-permute-start | bytes 294920 | tf_op jit(solution)/shard_map/ppermute | solution.py:162
  104.7 0.9 collective-permute-start.30
  105.7 1.2 %collective-permute-done.32 = bf16[192,256]{1,0:T(8,128)(2,1)S(1)} collective-permute-done((bf16[192,256]{1,0:T(8,128)(2,1)S(1)}, bf16[192,256]{1,0:T(8,128)(2,1)S(1)}, u32[]{:S(2)}, u32[]{:S(2)}) %collective-permute-start.32) | collective-permute-done | bytes 98336 | tf_op jit(solution)/shard_map/ppermute | solution.py:162
  106.9 3.6 %collective-permute-done.34 = bf16[192,256]{1,0:T(8,128)(2,1)S(1)} collective-permute-done((bf16[192,256]{1,0:T(8,128)(2,1)S(1)}, bf16[192,256]{1,0:T(8,128)(2,1)S(1)}, u32[]{:S(2)}, u32[]{:S(2)}) %collective-permute-start.34) | collective-permute-done | bytes 98336 | tf_op jit(solution)/shard_map/ppermute | solution.py:162
  110.6 0.7 pad_maximum_fusion.4
  111.3 0.7 convert_add_fusion.2
  (87 shorter events, 10.8 us)
Async XLA Ops:
  3.8 8.1 %collective-permute-start = (s32[48,128]{1,0:T(8,128)}, s32[48,128]{1,0:T(8,128)S(1)}, u32[]{:S(2)}, u32[]{:S(2)}) collective-permute-start(s32[48,128]{1,0:T(8,128)} %get-tuple-element.14), channel_id=1, source_target_pairs={{0,4},{4,0},{8,12},{12,8},{16,20},{20,16},{24,28},{28,24},{1,5},{5... | collective-permute-start | bytes 73736 | tf_op jit(solution)/shard_map/ppermute | solution.py:162
  6.8 5.1 %collective-permute-start.1 = (s32[48,128]{1,0:T(8,128)}, s32[48,128]{1,0:T(8,128)S(1)}, u32[]{:S(2)}, u32[]{:S(2)}) collective-permute-start(s32[48,128]{1,0:T(8,128)} %get-tuple-element.15), channel_id=1, source_target_pairs={{0,8},{4,12},{8,0},{12,4},{16,24},{20,28},{24,16},{28,20},{1,9},{5... | collective-permute-start | bytes 73736 | tf_op jit(solution)/shard_map/ppermute | solution.py:162
  8.3 4.9 %collective-permute-start.2 = (s32[48,128]{1,0:T(8,128)}, s32[48,128]{1,0:T(8,128)S(1)}, u32[]{:S(2)}, u32[]{:S(2)}) collective-permute-start(s32[48,128]{1,0:T(8,128)} %get-tuple-element.16), channel_id=1, source_target_pairs={{0,12},{4,8},{8,4},{12,0},{16,28},{20,24},{24,20},{28,16},{1,13},{... | collective-permute-start | bytes 73736 | tf_op jit(solution)/shard_map/ppermute | solution.py:162
  8.3 1.9 %copy-start = (bf16[192,8192]{1,0:T(8,128)(2,1)S(1)}, bf16[192,8192]{1,0:T(8,128)(2,1)}, u32[]{:S(2)}) copy-start(bf16[192,8192]{1,0:T(8,128)(2,1)} %feature_ref.1) | copy-start | bytes 9437188
  10.2 3.0 %copy-start.1 = (s32[48,128]{1,0:T(8,128)S(1)}, s32[48,128]{1,0:T(8,128)}, u32[]{:S(2)}) copy-start(s32[48,128]{1,0:T(8,128)} %get-tuple-element.13) | copy-start | bytes 73732
  10.2 5.7 %slice-start = ((bf16[192,256]{1,0:T(8,128)(2,1)}), bf16[128,256]{1,0:T(8,128)(2,1)S(1)}, s32[]{:S(2)}) async-start(bf16[192,256]{1,0:T(8,128)(2,1)} %param.10), calls=%async_computation | async-start | bytes 131072 | tf_op jit(solution)/shard_map/slice | solution.py:238
  10.2 5.7 %slice-start.1 = ((bf16[192,256]{1,0:T(8,128)(2,1)}), bf16[64,256]{1,0:T(8,128)(2,1)S(1)}, s32[]{:S(2)}) async-start(bf16[192,256]{1,0:T(8,128)(2,1)} %param.10), calls=%async_computation.1 | async-start | bytes 65536 | tf_op jit(solution)/shard_map/slice | solution.py:238
  10.2 5.7 %copy-start.2 = (bf16[192,256]{1,0:T(8,128)(2,1)S(1)}, bf16[192,256]{1,0:T(8,128)(2,1)}, u32[]{:S(2)}) copy-start(bf16[192,256]{1,0:T(8,128)(2,1)} %param.9) | copy-start | bytes 294916
  13.3 5.6 %collective-permute-start.3 = (s32[4,1,3072]{2,1,0:T(1,128)S(1)}, s32[4,1,3072]{2,1,0:T(1,128)S(1)}, u32[]{:S(2)}, u32[]{:S(2)}) collective-permute-start(s32[4,1,3072]{2,1,0:T(1,128)S(1)} %get-tuple-element.35), channel_id=1, source_target_pairs={{0,16},{4,20},{8,24},{12,28},{16,0},{20,4},{24,8},{28,12},{1,17},{... | collective-permute-start | bytes 147464 | tf_op jit(solution)/shard_map/ppermute | solution.py:162
  37.7 2.0 %collective-permute-start.4 = (bf16[2048,128]{1,0:T(8,128)(2,1)S(1)}, bf16[2048,128]{1,0:T(8,128)(2,1)S(1)}, u32[]{:S(2)}, u32[]{:S(2)}) collective-permute-start(bf16[2048,128]{1,0:T(8,128)(2,1)S(1)} %convolution_convert_fusion.1), channel_id=1, source_target_pairs={{0,1},{1,0},{2,3},{3,2},{4,5},{5,4},{6,7},{7,6},{8,9},{9,8},{10,11... | collective-permute-start | bytes 1572872 | tf_op jit(solution)/shard_map/ppermute | solution.py:162
  37.7 3.6 %collective-permute-start.9 = (bf16[2048,128]{1,0:T(8,128)(2,1)S(1)}, bf16[2048,128]{1,0:T(8,128)(2,1)S(1)}, u32[]{:S(2)}, u32[]{:S(2)}) collective-permute-start(bf16[2048,128]{1,0:T(8,128)(2,1)S(1)} %convolution_convert_fusion), channel_id=1, source_target_pairs={{0,1},{1,0},{2,3},{3,2},{4,5},{5,4},{6,7},{7,6},{8,9},{9,8},{10,11... | collective-permute-start | bytes 1572872 | tf_op jit(solution)/shard_map/ppermute | solution.py:162
  39.8 8.4 %collective-permute-start.5 = (bf16[8,128,128]{2,1,0:T(8,128)(2,1)S(1)}, bf16[8,128,128]{2,1,0:T(8,128)(2,1)S(1)}, u32[]{:S(2)}, u32[]{:S(2)}) collective-permute-start(bf16[8,128,128]{2,1,0:T(8,128)(2,1)S(1)} %bitcast.97), channel_id=1, source_target_pairs={{0,2},{1,3},{2,0},{3,1},{4,6},{5,7},{6,4},{7,5},{8,10},{9,11},{10,... | collective-permute-start | bytes 786440 | tf_op jit(solution)/shard_map/ppermute | solution.py:162
  41.7 7.0 %collective-permute-start.10 = (bf16[4,128,128]{2,1,0:T(8,128)(2,1)S(1)}, bf16[4,128,128]{2,1,0:T(8,128)(2,1)S(1)}, u32[]{:S(2)}, u32[]{:S(2)}) collective-permute-start(bf16[4,128,128]{2,1,0:T(8,128)(2,1)S(1)} %get-tuple-element.23), channel_id=1, source_target_pairs={{0,4},{4,0},{8,12},{12,8},{16,20},{20,16},{24,28},{28,24},{1,5},{5... | collective-permute-start | bytes 393224 | tf_op jit(solution)/shard_map/ppermute | solution.py:162
  42.2 6.6 %collective-permute-start.11 = (bf16[4,128,128]{2,1,0:T(8,128)(2,1)S(1)}, bf16[4,128,128]{2,1,0:T(8,128)(2,1)S(1)}, u32[]{:S(2)}, u32[]{:S(2)}) collective-permute-start(bf16[4,128,128]{2,1,0:T(8,128)(2,1)S(1)} %get-tuple-element.25), channel_id=1, source_target_pairs={{0,8},{4,12},{8,0},{12,4},{16,24},{20,28},{24,16},{28,20},{1,9},{5... | collective-permute-start | bytes 393224 | tf_op jit(solution)/shard_map/ppermute | solution.py:162
  43.8 7.3 %collective-permute-start.12 = (bf16[4,128,128]{2,1,0:T(8,128)(2,1)S(1)}, bf16[4,128,128]{2,1,0:T(8,128)(2,1)S(1)}, u32[]{:S(2)}, u32[]{:S(2)}) collective-permute-start(bf16[4,128,128]{2,1,0:T(8,128)(2,1)S(1)} %get-tuple-element.24), channel_id=1, source_target_pairs={{0,12},{4,8},{8,4},{12,0},{16,28},{20,24},{24,20},{28,16},{1,13},{... | collective-permute-start | bytes 393224 | tf_op jit(solution)/shard_map/ppermute | solution.py:162
  48.3 15.3 %copy-start.3 = (bf16[128,256]{1,0:T(8,128)(2,1)S(1)}, bf16[128,256]{1,0:T(8,128)(2,1)}, u32[]{:S(2)}) copy-start(bf16[128,256]{1,0:T(8,128)(2,1)} %param.11) | copy-start | bytes 196612
  48.3 5.6 %collective-permute-start.6 = (bf16[4,128,128]{2,1,0:T(8,128)(2,1)S(1)}, bf16[4,128,128]{2,1,0:T(8,128)(2,1)S(1)}, u32[]{:S(2)}, u32[]{:S(2)}) collective-permute-start(bf16[4,128,128]{2,1,0:T(8,128)(2,1)S(1)} %slice.201), channel_id=1, source_target_pairs={{0,4},{4,0},{8,12},{12,8},{16,20},{20,16},{24,28},{28,24},{1,5},{5... | collective-permute-start | bytes 393224 | tf_op jit(solution)/shard_map/ppermute | solution.py:162
  51.2 4.3 %collective-permute-start.13 = (bf16[2,128,128]{2,1,0:T(8,128)(2,1)S(1)}, bf16[2,128,128]{2,1,0:T(8,128)(2,1)S(1)}, u32[]{:S(2)}, u32[]{:S(2)}) collective-permute-start(bf16[2,128,128]{2,1,0:T(8,128)(2,1)S(1)} %slice.202), channel_id=1, source_target_pairs={{0,2},{1,3},{2,0},{3,1},{4,6},{5,7},{6,4},{7,5},{8,10},{9,11},{10,... | collective-permute-start | bytes 196616 | tf_op jit(solution)/shard_map/ppermute | solution.py:162
  53.9 4.3 %collective-permute-start.7 = (bf16[2,128,128]{2,1,0:T(8,128)(2,1)S(1)}, bf16[2,128,128]{2,1,0:T(8,128)(2,1)S(1)}, u32[]{:S(2)}, u32[]{:S(2)}) collective-permute-start(bf16[2,128,128]{2,1,0:T(8,128)(2,1)S(1)} %slice.203), channel_id=1, source_target_pairs={{0,8},{4,12},{8,0},{12,4},{16,24},{20,28},{24,16},{28,20},{1,9},{5... | collective-permute-start | bytes 196616 | tf_op jit(solution)/shard_map/ppermute | solution.py:162
  55.6 5.7 %collective-permute-start.14 = (bf16[1,128,128]{2,1,0:T(8,128)(2,1)S(1)}, bf16[1,128,128]{2,1,0:T(8,128)(2,1)S(1)}, u32[]{:S(2)}, u32[]{:S(2)}) collective-permute-start(bf16[1,128,128]{2,1,0:T(8,128)(2,1)S(1)} %slice.204), channel_id=1, source_target_pairs={{0,16},{4,20},{8,24},{12,28},{16,0},{20,4},{24,8},{28,12},{1,17},{... | collective-permute-start | bytes 98312 | tf_op jit(solution)/shard_map/ppermute | solution.py:162
  58.3 5.2 %collective-permute-start.8 = (bf16[1,128,128]{2,1,0:T(8,128)(2,1)S(1)}, bf16[1,128,128]{2,1,0:T(8,128)(2,1)S(1)}, u32[]{:S(2)}, u32[]{:S(2)}) collective-permute-start(bf16[1,128,128]{2,1,0:T(8,128)(2,1)S(1)} %slice.205), channel_id=1, source_target_pairs={{0,16},{4,20},{8,24},{12,28},{16,0},{20,4},{24,8},{28,12},{1,17},{... | collective-permute-start | bytes 98312 | tf_op jit(solution)/shard_map/ppermute | solution.py:162
  64.3 5.1 %collective-permute-start.15 = (bf16[128,128]{1,0:T(8,128)(2,1)S(1)}, bf16[128,128]{1,0:T(8,128)(2,1)S(1)}, u32[]{:S(2)}, u32[]{:S(2)}) collective-permute-start(bf16[128,128]{1,0:T(8,128)(2,1)S(1)} %get-tuple-element.41), channel_id=1, source_target_pairs={{0,16},{4,20},{8,24},{12,28},{16,0},{20,4},{24,8},{28,12},{1,17},{... | collective-permute-start | bytes 98312 | tf_op jit(solution)/shard_map/ppermute | solution.py:162
  66.1 6.8 %collective-permute-start.20 = (bf16[128,128]{1,0:T(8,128)(2,1)S(1)}, bf16[128,128]{1,0:T(8,128)(2,1)S(1)}, u32[]{:S(2)}, u32[]{:S(2)}) collective-permute-start(bf16[128,128]{1,0:T(8,128)(2,1)S(1)} %get-tuple-element.40), channel_id=1, source_target_pairs={{0,16},{4,20},{8,24},{12,28},{16,0},{20,4},{24,8},{28,12},{1,17},{... | collective-permute-start | bytes 98312 | tf_op jit(solution)/shard_map/ppermute | solution.py:162
  69.4 5.0 %collective-permute-start.16 = (bf16[2,128,128]{2,1,0:T(8,128)(2,1)S(1)}, bf16[2,128,128]{2,1,0:T(8,128)(2,1)S(1)}, u32[]{:S(2)}, u32[]{:S(2)}) collective-permute-start(bf16[2,128,128]{2,1,0:T(8,128)(2,1)S(1)} %get-tuple-element.37), channel_id=1, source_target_pairs={{0,4},{4,0},{8,12},{12,8},{16,20},{20,16},{24,28},{28,24},{1,5},{5... | collective-permute-start | bytes 196616 | tf_op jit(solution)/shard_map/ppermute | solution.py:162
  70.0 4.4 %collective-permute-start.17 = (bf16[2,128,128]{2,1,0:T(8,128)(2,1)S(1)}, bf16[2,128,128]{2,1,0:T(8,128)(2,1)S(1)}, u32[]{:S(2)}, u32[]{:S(2)}) collective-permute-start(bf16[2,128,128]{2,1,0:T(8,128)(2,1)S(1)} %get-tuple-element.37), channel_id=1, source_target_pairs={{0,8},{4,12},{8,0},{12,4},{16,24},{20,28},{24,16},{28,20},{1,9},{5... | collective-permute-start | bytes 196616 | tf_op jit(solution)/shard_map/ppermute | solution.py:162
  71.0 5.5 %collective-permute-start.18 = (bf16[2,128,128]{2,1,0:T(8,128)(2,1)S(1)}, bf16[2,128,128]{2,1,0:T(8,128)(2,1)S(1)}, u32[]{:S(2)}, u32[]{:S(2)}) collective-permute-start(bf16[2,128,128]{2,1,0:T(8,128)(2,1)S(1)} %get-tuple-element.37), channel_id=1, source_target_pairs={{0,12},{4,8},{8,4},{12,0},{16,28},{20,24},{24,20},{28,16},{1,13},{... | collective-permute-start | bytes 196616 | tf_op jit(solution)/shard_map/ppermute | solution.py:162
  73.0 4.8 %collective-permute-start.21 = (bf16[2,128,128]{2,1,0:T(8,128)(2,1)S(1)}, bf16[2,128,128]{2,1,0:T(8,128)(2,1)S(1)}, u32[]{:S(2)}, u32[]{:S(2)}) collective-permute-start(bf16[2,128,128]{2,1,0:T(8,128)(2,1)S(1)} %get-tuple-element.43), channel_id=1, source_target_pairs={{0,2},{1,3},{2,0},{3,1},{4,6},{5,7},{6,4},{7,5},{8,10},{9,11},{10,... | collective-permute-start | bytes 196616 | tf_op jit(solution)/shard_map/ppermute | solution.py:162
  76.6 10.3 %collective-permute-start.19 = (bf16[4,2,128,128]{3,2,1,0:T(8,128)(2,1)S(1)}, bf16[4,2,128,128]{3,2,1,0:T(8,128)(2,1)S(1)}, u32[]{:S(2)}, u32[]{:S(2)}) collective-permute-start(bf16[4,2,128,128]{3,2,1,0:T(8,128)(2,1)S(1)} %pad_maximum_fusion.2), channel_id=1, source_target_pairs={{0,2},{1,3},{2,0},{3,1},{4,6},{5,7},{6,4},{7,5},{8,10},{9,11},{10,... | collective-permute-start | bytes 786440 | tf_op jit(solution)/shard_map/ppermute | solution.py:162
  77.8 5.0 %collective-permute-start.22 = (bf16[2,2,128,128]{3,2,1,0:T(8,128)(2,1)S(1)}, bf16[2,2,128,128]{3,2,1,0:T(8,128)(2,1)S(1)}, u32[]{:S(2)}, u32[]{:S(2)}) collective-permute-start(bf16[2,2,128,128]{3,2,1,0:T(8,128)(2,1)S(1)} %get-tuple-element.31), channel_id=1, source_target_pairs={{0,4},{4,0},{8,12},{12,8},{16,20},{20,16},{24,28},{28,24},{1,5},{5... | collective-permute-start | bytes 393224 | tf_op jit(solution)/shard_map/ppermute | solution.py:162
  78.9 5.0 %collective-permute-start.23 = (bf16[2,2,128,128]{3,2,1,0:T(8,128)(2,1)S(1)}, bf16[2,2,128,128]{3,2,1,0:T(8,128)(2,1)S(1)}, u32[]{:S(2)}, u32[]{:S(2)}) collective-permute-start(bf16[2,2,128,128]{3,2,1,0:T(8,128)(2,1)S(1)} %get-tuple-element.31), channel_id=1, source_target_pairs={{0,8},{4,12},{8,0},{12,4},{16,24},{20,28},{24,16},{28,20},{1,9},{5... | collective-permute-start | bytes 393224 | tf_op jit(solution)/shard_map/ppermute | solution.py:162
  80.8 5.9 %collective-permute-start.24 = (bf16[2,2,128,128]{3,2,1,0:T(8,128)(2,1)S(1)}, bf16[2,2,128,128]{3,2,1,0:T(8,128)(2,1)S(1)}, u32[]{:S(2)}, u32[]{:S(2)}) collective-permute-start(bf16[2,2,128,128]{3,2,1,0:T(8,128)(2,1)S(1)} %get-tuple-element.31), channel_id=1, source_target_pairs={{0,12},{4,8},{8,4},{12,0},{16,28},{20,24},{24,20},{28,16},{1,13},{... | collective-permute-start | bytes 393224 | tf_op jit(solution)/shard_map/ppermute | solution.py:162
  86.8 2.0 %collective-permute-start.26 = (bf16[2048,128]{1,0:T(8,128)(2,1)S(1)}, bf16[2048,128]{1,0:T(8,128)(2,1)S(1)}, u32[]{:S(2)}, u32[]{:S(2)}) collective-permute-start(bf16[2048,128]{1,0:T(8,128)(2,1)S(1)} %bitcast.93), channel_id=1, source_target_pairs={{0,1},{1,0},{2,3},{3,2},{4,5},{5,4},{6,7},{7,6},{8,9},{9,8},{10,11... | collective-permute-start | bytes 1572872 | tf_op jit(solution)/shard_map/ppermute | solution.py:162
  87.0 2.6 %collective-permute-start.25 = (bf16[2048,128]{1,0:T(8,128)(2,1)S(1)}, bf16[2048,128]{1,0:T(8,128)(2,1)S(1)}, u32[]{:S(2)}, u32[]{:S(2)}) collective-permute-start(bf16[2048,128]{1,0:T(8,128)(2,1)S(1)} %bitcast.95), channel_id=1, source_target_pairs={{0,1},{1,0},{2,3},{3,2},{4,5},{5,4},{6,7},{7,6},{8,9},{9,8},{10,11... | collective-permute-start | bytes 1572872 | tf_op jit(solution)/shard_map/ppermute | solution.py:162
  90.2 5.5 %collective-permute-start.27 = (bf16[192,256]{1,0:T(8,128)(2,1)S(1)}, bf16[192,256]{1,0:T(8,128)(2,1)S(1)}, u32[]{:S(2)}, u32[]{:S(2)}) collective-permute-start(bf16[192,256]{1,0:T(8,128)(2,1)S(1)} %get-tuple-element.29), channel_id=1, source_target_pairs={{0,4},{4,0},{8,12},{12,8},{16,20},{20,16},{24,28},{28,24},{1,5},{5... | collective-permute-start | bytes 294920 | tf_op jit(solution)/shard_map/ppermute | solution.py:162
  90.3 5.6 %collective-permute-start.28 = (bf16[192,256]{1,0:T(8,128)(2,1)S(1)}, bf16[192,256]{1,0:T(8,128)(2,1)S(1)}, u32[]{:S(2)}, u32[]{:S(2)}) collective-permute-start(bf16[192,256]{1,0:T(8,128)(2,1)S(1)} %get-tuple-element.29), channel_id=1, source_target_pairs={{0,8},{4,12},{8,0},{12,4},{16,24},{20,28},{24,16},{28,20},{1,9},{5... | collective-permute-start | bytes 294920 | tf_op jit(solution)/shard_map/ppermute | solution.py:162
  92.2 8.3 %collective-permute-start.29 = (bf16[192,256]{1,0:T(8,128)(2,1)S(1)}, bf16[192,256]{1,0:T(8,128)(2,1)S(1)}, u32[]{:S(2)}, u32[]{:S(2)}) collective-permute-start(bf16[192,256]{1,0:T(8,128)(2,1)S(1)} %get-tuple-element.29), channel_id=1, source_target_pairs={{0,12},{4,8},{8,4},{12,0},{16,28},{20,24},{24,20},{28,16},{1,13},{... | collective-permute-start | bytes 294920 | tf_op jit(solution)/shard_map/ppermute | solution.py:162
  93.7 7.4 %collective-permute-start.31 = (bf16[192,256]{1,0:T(8,128)(2,1)S(1)}, bf16[192,256]{1,0:T(8,128)(2,1)S(1)}, u32[]{:S(2)}, u32[]{:S(2)}) collective-permute-start(bf16[192,256]{1,0:T(8,128)(2,1)S(1)} %get-tuple-element.28), channel_id=1, source_target_pairs={{0,16},{4,20},{8,24},{12,28},{16,0},{20,4},{24,8},{28,12},{1,17},{... | collective-permute-start | bytes 294920 | tf_op jit(solution)/shard_map/ppermute | solution.py:162
  101.2 5.7 %collective-permute-start.32 = (bf16[192,256]{1,0:T(8,128)(2,1)S(1)}, bf16[192,256]{1,0:T(8,128)(2,1)S(1)}, u32[]{:S(2)}, u32[]{:S(2)}) collective-permute-start(bf16[192,256]{1,0:T(8,128)(2,1)S(1)} %get-tuple-element.26), channel_id=1, source_target_pairs={{0,4},{4,0},{8,12},{12,8},{16,20},{20,16},{24,28},{28,24},{1,5},{5... | collective-permute-start | bytes 294920 | tf_op jit(solution)/shard_map/ppermute | solution.py:162
  101.3 5.6 %collective-permute-start.33 = (bf16[192,256]{1,0:T(8,128)(2,1)S(1)}, bf16[192,256]{1,0:T(8,128)(2,1)S(1)}, u32[]{:S(2)}, u32[]{:S(2)}) collective-permute-start(bf16[192,256]{1,0:T(8,128)(2,1)S(1)} %get-tuple-element.26), channel_id=1, source_target_pairs={{0,8},{4,12},{8,0},{12,4},{16,24},{20,28},{24,16},{28,20},{1,9},{5... | collective-permute-start | bytes 294920 | tf_op jit(solution)/shard_map/ppermute | solution.py:162
  103.1 7.4 %collective-permute-start.34 = (bf16[192,256]{1,0:T(8,128)(2,1)S(1)}, bf16[192,256]{1,0:T(8,128)(2,1)S(1)}, u32[]{:S(2)}, u32[]{:S(2)}) collective-permute-start(bf16[192,256]{1,0:T(8,128)(2,1)S(1)} %get-tuple-element.26), channel_id=1, source_target_pairs={{0,12},{4,8},{8,4},{12,0},{16,28},{20,24},{24,20},{28,16},{1,13},{... | collective-permute-start | bytes 294920 | tf_op jit(solution)/shard_map/ppermute | solution.py:162
  104.7 6.5 %collective-permute-start.30 = (bf16[192,256]{1,0:T(8,128)(2,1)S(1)}, bf16[192,256]{1,0:T(8,128)(2,1)S(1)}, u32[]{:S(2)}, u32[]{:S(2)}) collective-permute-start(bf16[192,256]{1,0:T(8,128)(2,1)S(1)} %get-tuple-element.27), channel_id=1, source_target_pairs={{0,16},{4,20},{8,24},{12,28},{16,0},{20,4},{24,8},{28,12},{1,17},{... | collective-permute-start | bytes 294920 | tf_op jit(solution)/shard_map/ppermute | solution.py:162

commit v6 on v5

--- a/solution.py
+++ b/solution.py
@@ -320,7 +320,7 @@
         theirs, jnp.concatenate(beside, axis=1)
     )
     chains = [grads[:columns], grads[columns:]]
-    turns = [[pair] + steps[2:], steps[2:] + [pair]]
+    turns = [steps, steps[1:] + steps[:1]]
     for s in range(len(turns[0])):
         for c in (0, 1):
             chains[c] = add_all(chains[c], *turns[c][s])

time: 112 us -> 111 us (level)
  starting transfers between devices: 42.1 us -> 40.3 us
    ppermute x35 -> x33, starting transfers between devices: 42.1 us -> 40.3 us  [swap(): return lax.ppermute(value, axis, [(i, i ^ bit) for i in range(count)])]
    ppermute x35 -> x33, waiting for transfers between devices: 35 us -> 35.1 us  [swap(): return lax.ppermute(value, axis, [(i, i ^ bit) for i in range(count)])]
  transfers between devices with their start and end apart: 35 -> 33, of which waited for: 23 -> 23; matrix products, arithmetic and copies ran while one was open for 3% -> 3% of each run, Pallas kernels for 4% -> 4%
where the time goes in v6:
time: 111 us; the launch traced here: 110 us
  starting transfers between devices  40.3 us (36%)
  waiting for transfers between devices  35.1 us (32%)
  Pallas kernels  25.1 us (23%)
  matrix products  3.5 us (3%)
  other arithmetic  2.91 us (3%)
  local copies, waits for them, and re-layouts  2.32 us (2%)
    ppermute x33, starting transfers between devices, swap(): return lax.ppermute(value, axis, [(i, i ^ bit) for i in range(count)])  40.3 us
    ppermute x33, waiting for transfers between devices, swap(): return lax.ppermute(value, axis, [(i, i ^ bit) for i in range(count)])  35.1 us
    pallas_call x1, Pallas kernels, on_device(): pl.pallas_call(functools.partial(owner_kernel, tgt_bits), grid_spec=pltpu...  17.6 us
    pallas_call x1, Pallas kernels, on_device(): pl.pallas_call(functools.partial(list_kernel, wide_count, capacity, tgt_b...  3.17 us
    pallas_call x1, Pallas kernels, on_device(): pl.pallas_call(functools.partial(first_kernel, unroll), grid_spec=pltpu.P...  2.75 us
  transfers between devices with their start and end apart: 33, of which 23 were waited for; matrix products, arithmetic and copies ran while one was open for 3% of the time, Pallas kernels for 4%

profile of v6, /device:TPU:0, one launch (start us, length us, event | category | flops | bytes accessed | tf_op | source)
XLA Modules:
  0.0 110.4 jit_solution(15792531380385997361)
XLA Ops:
  0.6 3.2 %lists.1 = (s32[48,128]{1,0:T(8,128)}, s32[48,128]{1,0:T(8,128)}, s32[48,128]{1,0:T(8,128)}, s32[48,128]{1,0:T(8,128)}) custom-call(s32[16,1,512]{2,1,0:T(1,128)} %bitcast.105, s32[16,512]{1,0:T(8,128)} %bitcast.106), custom_call_target="tpu_custom_call" | custom-call | tf_op jit(solution)/shard_map/lists/pallas_call | solution.py:227
  3.8 3.0 %collective-permute-start = (s32[48,128]{1,0:T(8,128)}, s32[48,128]{1,0:T(8,128)S(1)}, u32[]{:S(2)}, u32[]{:S(2)}) collective-permute-start(s32[48,128]{1,0:T(8,128)} %get-tuple-element.14), channel_id=1, source_target_pairs={{0,4},{4,0},{8,12},{12,8},{16,20},{20,16},{24,28},{28,24},{1,5},{5... | collective-permute-start | bytes 73736 | tf_op jit(solution)/shard_map/ppermute | solution.py:162
  6.8 1.6 %collective-permute-start.1 = (s32[48,128]{1,0:T(8,128)}, s32[48,128]{1,0:T(8,128)S(1)}, u32[]{:S(2)}, u32[]{:S(2)}) collective-permute-start(s32[48,128]{1,0:T(8,128)} %get-tuple-element.15), channel_id=1, source_target_pairs={{0,8},{4,12},{8,0},{12,4},{16,24},{20,28},{24,16},{28,20},{1,9},{5... | collective-permute-start | bytes 73736 | tf_op jit(solution)/shard_map/ppermute | solution.py:162
  8.3 1.9 %copy-done = bf16[192,8192]{1,0:T(8,128)(2,1)S(1)} copy-done((bf16[192,8192]{1,0:T(8,128)(2,1)S(1)}, bf16[192,8192]{1,0:T(8,128)(2,1)}, u32[]{:S(2)}) %copy-start) | copy-done | bytes 3145752
  10.2 1.6 %table.1.table_ref = f32[8192,2,128]{2,1,0:T(2,128)S(1)} custom-call(bf16[192,8192]{1,0:T(8,128)(2,1)S(1)} %copy-done), custom_call_target="tpu_custom_call" | custom-call | bytes 25165824 | tf_op jit(solution)/shard_map/table/pallas_call | solution.py:214
  11.9 1.4 %collective-permute-done.2 = s32[48,128]{1,0:T(8,128)S(1)} collective-permute-done((s32[48,128]{1,0:T(8,128)}, s32[48,128]{1,0:T(8,128)S(1)}, u32[]{:S(2)}, u32[]{:S(2)}) %collective-permute-start.2) | collective-permute-done | bytes 24608 | tf_op jit(solution)/shard_map/ppermute | solution.py:162
  13.3 2.7 %collective-permute-start.3 = (s32[4,1,3072]{2,1,0:T(1,128)S(1)}, s32[4,1,3072]{2,1,0:T(1,128)S(1)}, u32[]{:S(2)}, u32[]{:S(2)}) collective-permute-start(s32[4,1,3072]{2,1,0:T(1,128)S(1)} %get-tuple-element.35), channel_id=1, source_target_pairs={{0,16},{4,20},{8,24},{12,28},{16,0},{20,4},{24,8},{28,12},{1,17},{... | collective-permute-start | bytes 147464 | tf_op jit(solution)/shard_map/ppermute | solution.py:162
  16.0 2.7 %first.1.first_ref = bf16[1536,256]{1,0:T(8,128)(2,1)S(1)} custom-call(s32[6144]{0:T(1024)S(1)} %bitcast.85, f32[8192,2,128]{2,1,0:T(2,128)S(1)} %table.1.table_ref), custom_call_target="tpu_custom_call" | custom-call | bytes 4194304 | tf_op jit(solution)/shard_map/first/pallas_call | solution.py:249
  18.9 17.6 %owner.1 = (bf16[2,8,128,384]{3,2,1,0:T(8,128)(2,1)S(1)}, bf16[2,8,128,384]{3,2,1,0:T(8,128)(2,1)S(1)}) custom-call(s32[24576]{0:T(1024)S(1)} %bitcast.83, s32[8,1,3072]{2,1,0:T(1,128)S(1)} %pad_add_fusion.1.key_ref, f32[8192,2,128]{2,1,0:T(2,128)S(1)} %table.1.table_ref, bf16[1536,256]{1,0:T(8,128)(2,1)S(1)} %first.1.first_ref), custom_call_target="tpu_custom_call" | custom-call | tf_op jit(solution)/shard_map/owner/pallas_call | solution.py:264
  39.8 1.6 %collective-permute-start.5 = (bf16[8,128,128]{2,1,0:T(8,128)(2,1)S(1)}, bf16[8,128,128]{2,1,0:T(8,128)(2,1)S(1)}, u32[]{:S(2)}, u32[]{:S(2)}) collective-permute-start(bf16[8,128,128]{2,1,0:T(8,128)(2,1)S(1)} %bitcast.97), channel_id=1, source_target_pairs={{0,2},{1,3},{2,0},{3,1},{4,6},{5,7},{6,4},{7,5},{8,10},{9,11},{10,... | collective-permute-start | bytes 786440 | tf_op jit(solution)/shard_map/ppermute | solution.py:162
  42.2 1.6 %collective-permute-start.11 = (bf16[4,128,128]{2,1,0:T(8,128)(2,1)S(1)}, bf16[4,128,128]{2,1,0:T(8,128)(2,1)S(1)}, u32[]{:S(2)}, u32[]{:S(2)}) collective-permute-start(bf16[4,128,128]{2,1,0:T(8,128)(2,1)S(1)} %get-tuple-element.25), channel_id=1, source_target_pairs={{0,8},{4,12},{8,0},{12,4},{16,24},{20,28},{24,16},{28,20},{1,9},{5... | collective-permute-start | bytes 393224 | tf_op jit(solution)/shard_map/ppermute | solution.py:162
  43.8 1.5 %collective-permute-start.12 = (bf16[4,128,128]{2,1,0:T(8,128)(2,1)S(1)}, bf16[4,128,128]{2,1,0:T(8,128)(2,1)S(1)}, u32[]{:S(2)}, u32[]{:S(2)}) collective-permute-start(bf16[4,128,128]{2,1,0:T(8,128)(2,1)S(1)} %get-tuple-element.24), channel_id=1, source_target_pairs={{0,12},{4,8},{8,4},{12,0},{16,28},{20,24},{24,20},{28,16},{1,13},{... | collective-permute-start | bytes 393224 | tf_op jit(solution)/shard_map/ppermute | solution.py:162
  45.3 2.9 %collective-permute-done.5 = bf16[8,128,128]{2,1,0:T(8,128)(2,1)S(1)} collective-permute-done((bf16[8,128,128]{2,1,0:T(8,128)(2,1)S(1)}, bf16[8,128,128]{2,1,0:T(8,128)(2,1)S(1)}, u32[]{:S(2)}, u32[]{:S(2)}) %collective-permute-start.5) | collective-permute-done | bytes 262176 | tf_op jit(solution)/shard_map/ppermute | solution.py:162
  48.8 2.3 %collective-permute-done.12 = bf16[4,128,128]{2,1,0:T(8,128)(2,1)S(1)} collective-permute-done((bf16[4,128,128]{2,1,0:T(8,128)(2,1)S(1)}, bf16[4,128,128]{2,1,0:T(8,128)(2,1)S(1)}, u32[]{:S(2)}, u32[]{:S(2)}) %collective-permute-start.12) | collective-permute-done | bytes 131104 | tf_op jit(solution)/shard_map/ppermute | solution.py:162
  51.2 0.8 collective-permute-start.13
  52.0 1.9 %collective-permute-done.6 = bf16[4,128,128]{2,1,0:T(8,128)(2,1)S(1)} collective-permute-done((bf16[4,128,128]{2,1,0:T(8,128)(2,1)S(1)}, bf16[4,128,128]{2,1,0:T(8,128)(2,1)S(1)}, u32[]{:S(2)}, u32[]{:S(2)}) %collective-permute-start.6) | collective-permute-done | bytes 131104 | tf_op jit(solution)/shard_map/ppermute | solution.py:162
  54.5 1.1 collective-permute-done.13
  55.6 2.1 %collective-permute-start.14 = (bf16[1,128,128]{2,1,0:T(8,128)(2,1)S(1)}, bf16[1,128,128]{2,1,0:T(8,128)(2,1)S(1)}, u32[]{:S(2)}, u32[]{:S(2)}) collective-permute-start(bf16[1,128,128]{2,1,0:T(8,128)(2,1)S(1)} %slice.204), channel_id=1, source_target_pairs={{0,16},{4,20},{8,24},{12,28},{16,0},{20,4},{24,8},{28,12},{1,17},{... | collective-permute-start | bytes 98312 | tf_op jit(solution)/shard_map/ppermute | solution.py:162
  58.3 2.1 %collective-permute-start.8 = (bf16[1,128,128]{2,1,0:T(8,128)(2,1)S(1)}, bf16[1,128,128]{2,1,0:T(8,128)(2,1)S(1)}, u32[]{:S(2)}, u32[]{:S(2)}) collective-permute-start(bf16[1,128,128]{2,1,0:T(8,128)(2,1)S(1)} %slice.205), channel_id=1, source_target_pairs={{0,16},{4,20},{8,24},{12,28},{16,0},{20,4},{24,8},{28,12},{1,17},{... | collective-permute-start | bytes 98312 | tf_op jit(solution)/shard_map/ppermute | solution.py:162
  60.4 0.8 collective-permute-done.14
  61.2 2.2 %collective-permute-done.8 = bf16[1,128,128]{2,1,0:T(8,128)(2,1)S(1)} collective-permute-done((bf16[1,128,128]{2,1,0:T(8,128)(2,1)S(1)}, bf16[1,128,128]{2,1,0:T(8,128)(2,1)S(1)}, u32[]{:S(2)}, u32[]{:S(2)}) %collective-permute-start.8) | collective-permute-done | bytes 32800 | tf_op jit(solution)/shard_map/ppermute | solution.py:162
  63.5 0.7 fusion.13
  64.2 1.9 %collective-permute-start.15 = (bf16[128,128]{1,0:T(8,128)(2,1)S(1)}, bf16[128,128]{1,0:T(8,128)(2,1)S(1)}, u32[]{:S(2)}, u32[]{:S(2)}) collective-permute-start(bf16[128,128]{1,0:T(8,128)(2,1)S(1)} %get-tuple-element.41), channel_id=1, source_target_pairs={{0,16},{4,20},{8,24},{12,28},{16,0},{20,4},{24,8},{28,12},{1,17},{... | collective-permute-start | bytes 98312 | tf_op jit(solution)/shard_map/ppermute | solution.py:162
  66.1 1.1 collective-permute-start.20
  67.2 2.2 %collective-permute-done.15 = bf16[128,128]{1,0:T(8,128)(2,1)S(1)} collective-permute-done((bf16[128,128]{1,0:T(8,128)(2,1)S(1)}, bf16[128,128]{1,0:T(8,128)(2,1)S(1)}, u32[]{:S(2)}, u32[]{:S(2)}) %collective-permute-start.15) | collective-permute-done | bytes 32800 | tf_op jit(solution)/shard_map/ppermute | solution.py:162
  70.0 1.0 collective-permute-start.17
  71.0 2.0 %collective-permute-start.18 = (bf16[2,128,128]{2,1,0:T(8,128)(2,1)S(1)}, bf16[2,128,128]{2,1,0:T(8,128)(2,1)S(1)}, u32[]{:S(2)}, u32[]{:S(2)}) collective-permute-start(bf16[2,128,128]{2,1,0:T(8,128)(2,1)S(1)} %get-tuple-element.37), channel_id=1, source_target_pairs={{0,12},{4,8},{8,4},{12,0},{16,28},{20,24},{24,20},{28,16},{1,13},{... | collective-permute-start | bytes 196616 | tf_op jit(solution)/shard_map/ppermute | solution.py:162
  73.0 1.4 %collective-permute-start.21 = (bf16[2,128,128]{2,1,0:T(8,128)(2,1)S(1)}, bf16[2,128,128]{2,1,0:T(8,128)(2,1)S(1)}, u32[]{:S(2)}, u32[]{:S(2)}) collective-permute-start(bf16[2,128,128]{2,1,0:T(8,128)(2,1)S(1)} %get-tuple-element.43), channel_id=1, source_target_pairs={{0,2},{1,3},{2,0},{3,1},{4,6},{5,7},{6,4},{7,5},{8,10},{9,11},{10,... | collective-permute-start | bytes 196616 | tf_op jit(solution)/shard_map/ppermute | solution.py:162
  74.4 2.1 %collective-permute-done.18 = bf16[2,128,128]{2,1,0:T(8,128)(2,1)S(1)} collective-permute-done((bf16[2,128,128]{2,1,0:T(8,128)(2,1)S(1)}, bf16[2,128,128]{2,1,0:T(8,128)(2,1)S(1)}, u32[]{:S(2)}, u32[]{:S(2)}) %collective-permute-start.18) | collective-permute-done | bytes 65568 | tf_op jit(solution)/shard_map/ppermute | solution.py:162
  76.5 1.1 collective-permute-start.19
  77.8 0.9 collective-permute-start.22
  78.8 2.0 %collective-permute-start.23 = (bf16[2,2,128,128]{3,2,1,0:T(8,128)(2,1)S(1)}, bf16[2,2,128,128]{3,2,1,0:T(8,128)(2,1)S(1)}, u32[]{:S(2)}, u32[]{:S(2)}) collective-permute-start(bf16[2,2,128,128]{3,2,1,0:T(8,128)(2,1)S(1)} %get-tuple-element.31), channel_id=1, source_target_pairs={{0,8},{4,12},{8,0},{12,4},{16,24},{20,28},{24,16},{28,20},{1,9},{5... | collective-permute-start | bytes 393224 | tf_op jit(solution)/shard_map/ppermute | solution.py:162
  81.4 1.5 %collective-permute-done.22 = bf16[2,2,128,128]{3,2,1,0:T(8,128)(2,1)S(1)} collective-permute-done((bf16[2,2,128,128]{3,2,1,0:T(8,128)(2,1)S(1)}, bf16[2,2,128,128]{3,2,1,0:T(8,128)(2,1)S(1)}, u32[]{:S(2)}, u32[]{:S(2)}) %collective-permute-start.22) | collective-permute-done | bytes 131104 | tf_op jit(solution)/shard_map/ppermute | solution.py:162
  82.9 0.9 collective-permute-done.23
  83.8 2.9 %collective-permute-done.24 = bf16[2,2,128,128]{3,2,1,0:T(8,128)(2,1)S(1)} collective-permute-done((bf16[2,2,128,128]{3,2,1,0:T(8,128)(2,1)S(1)}, bf16[2,2,128,128]{3,2,1,0:T(8,128)(2,1)S(1)}, u32[]{:S(2)}, u32[]{:S(2)}) %collective-permute-start.24) | collective-permute-done | bytes 131104 | tf_op jit(solution)/shard_map/ppermute | solution.py:162
  88.1 0.6 collective-permute-done.26
  88.7 0.7 collective-permute-done.25
  90.3 1.9 %collective-permute-start.30 = (bf16[192,256]{1,0:T(8,128)(2,1)S(1)}, bf16[192,256]{1,0:T(8,128)(2,1)S(1)}, u32[]{:S(2)}, u32[]{:S(2)}) collective-permute-start(bf16[192,256]{1,0:T(8,128)(2,1)S(1)} %get-tuple-element.28), channel_id=1, source_target_pairs={{0,8},{4,12},{8,0},{12,4},{16,24},{20,28},{24,16},{28,20},{1,9},{5... | collective-permute-start | bytes 294920 | tf_op jit(solution)/shard_map/ppermute | solution.py:162
  92.2 2.9 %collective-permute-done.27 = bf16[192,256]{1,0:T(8,128)(2,1)S(1)} collective-permute-done((bf16[192,256]{1,0:T(8,128)(2,1)S(1)}, bf16[192,256]{1,0:T(8,128)(2,1)S(1)}, u32[]{:S(2)}, u32[]{:S(2)}) %collective-permute-start.27) | collective-permute-done | bytes 98336 | tf_op jit(solution)/shard_map/ppermute | solution.py:162
  95.2 2.0 %collective-permute-start.31 = (bf16[192,256]{1,0:T(8,128)(2,1)S(1)}, bf16[192,256]{1,0:T(8,128)(2,1)S(1)}, u32[]{:S(2)}, u32[]{:S(2)}) collective-permute-start(bf16[192,256]{1,0:T(8,128)(2,1)S(1)} %get-tuple-element.26), channel_id=1, source_target_pairs={{0,16},{4,20},{8,24},{12,28},{16,0},{20,4},{24,8},{28,12},{1,17},{... | collective-permute-start | bytes 294920 | tf_op jit(solution)/shard_map/ppermute | solution.py:162
  97.2 1.8 %collective-permute-start.28 = (bf16[192,256]{1,0:T(8,128)(2,1)S(1)}, bf16[192,256]{1,0:T(8,128)(2,1)S(1)}, u32[]{:S(2)}, u32[]{:S(2)}) collective-permute-start(bf16[192,256]{1,0:T(8,128)(2,1)S(1)} %get-tuple-element.27), channel_id=1, source_target_pairs={{0,8},{4,12},{8,0},{12,4},{16,24},{20,28},{24,16},{28,20},{1,9},{5... | collective-permute-start | bytes 294920 | tf_op jit(solution)/shard_map/ppermute | solution.py:162
  98.9 3.4 %collective-permute-done.31 = bf16[192,256]{1,0:T(8,128)(2,1)S(1)} collective-permute-done((bf16[192,256]{1,0:T(8,128)(2,1)S(1)}, bf16[192,256]{1,0:T(8,128)(2,1)S(1)}, u32[]{:S(2)}, u32[]{:S(2)}) %collective-permute-start.31) | collective-permute-done | bytes 98336 | tf_op jit(solution)/shard_map/ppermute | solution.py:162
  102.3 1.2 %collective-permute-start.32 = (bf16[192,256]{1,0:T(8,128)(2,1)S(1)}, bf16[192,256]{1,0:T(8,128)(2,1)S(1)}, u32[]{:S(2)}, u32[]{:S(2)}) collective-permute-start(bf16[192,256]{1,0:T(8,128)(2,1)S(1)} %add_convert_fusion), channel_id=1, source_target_pairs={{0,4},{4,0},{8,12},{12,8},{16,20},{20,16},{24,28},{28,24},{1,5},{5... | collective-permute-start | bytes 294920 | tf_op jit(solution)/shard_map/ppermute | solution.py:162
  103.6 1.1 collective-permute-start.29
  104.7 2.3 %collective-permute-done.32 = bf16[192,256]{1,0:T(8,128)(2,1)S(1)} collective-permute-done((bf16[192,256]{1,0:T(8,128)(2,1)S(1)}, bf16[192,256]{1,0:T(8,128)(2,1)S(1)}, u32[]{:S(2)}, u32[]{:S(2)}) %collective-permute-start.32) | collective-permute-done | bytes 98336 | tf_op jit(solution)/shard_map/ppermute | solution.py:162
  107.1 0.7 pad_maximum_fusion.4
  107.8 1.9 %collective-permute-done.29 = bf16[192,256]{1,0:T(8,128)(2,1)S(1)} collective-permute-done((bf16[192,256]{1,0:T(8,128)(2,1)S(1)}, bf16[192,256]{1,0:T(8,128)(2,1)S(1)}, u32[]{:S(2)}, u32[]{:S(2)}) %collective-permute-start.29) | collective-permute-done | bytes 98336 | tf_op jit(solution)/shard_map/ppermute | solution.py:162
  109.7 0.7 convert_add_fusion.3
  (85 shorter events, 10.0 us)
Async XLA Ops:
  3.8 8.1 %collective-permute-start = (s32[48,128]{1,0:T(8,128)}, s32[48,128]{1,0:T(8,128)S(1)}, u32[]{:S(2)}, u32[]{:S(2)}) collective-permute-start(s32[48,128]{1,0:T(8,128)} %get-tuple-element.14), channel_id=1, source_target_pairs={{0,4},{4,0},{8,12},{12,8},{16,20},{20,16},{24,28},{28,24},{1,5},{5... | collective-permute-start | bytes 73736 | tf_op jit(solution)/shard_map/ppermute | solution.py:162
  6.8 5.1 %collective-permute-start.1 = (s32[48,128]{1,0:T(8,128)}, s32[48,128]{1,0:T(8,128)S(1)}, u32[]{:S(2)}, u32[]{:S(2)}) collective-permute-start(s32[48,128]{1,0:T(8,128)} %get-tuple-element.15), channel_id=1, source_target_pairs={{0,8},{4,12},{8,0},{12,4},{16,24},{20,28},{24,16},{28,20},{1,9},{5... | collective-permute-start | bytes 73736 | tf_op jit(solution)/shard_map/ppermute | solution.py:162
  8.3 4.9 %collective-permute-start.2 = (s32[48,128]{1,0:T(8,128)}, s32[48,128]{1,0:T(8,128)S(1)}, u32[]{:S(2)}, u32[]{:S(2)}) collective-permute-start(s32[48,128]{1,0:T(8,128)} %get-tuple-element.16), channel_id=1, source_target_pairs={{0,12},{4,8},{8,4},{12,0},{16,28},{20,24},{24,20},{28,16},{1,13},{... | collective-permute-start | bytes 73736 | tf_op jit(solution)/shard_map/ppermute | solution.py:162
  8.3 1.9 %copy-start = (bf16[192,8192]{1,0:T(8,128)(2,1)S(1)}, bf16[192,8192]{1,0:T(8,128)(2,1)}, u32[]{:S(2)}) copy-start(bf16[192,8192]{1,0:T(8,128)(2,1)} %feature_ref.1) | copy-start | bytes 9437188
  10.2 3.0 %copy-start.1 = (s32[48,128]{1,0:T(8,128)S(1)}, s32[48,128]{1,0:T(8,128)}, u32[]{:S(2)}) copy-start(s32[48,128]{1,0:T(8,128)} %get-tuple-element.13) | copy-start | bytes 73732
  10.2 5.7 %slice-start = ((bf16[192,256]{1,0:T(8,128)(2,1)}), bf16[128,256]{1,0:T(8,128)(2,1)S(1)}, s32[]{:S(2)}) async-start(bf16[192,256]{1,0:T(8,128)(2,1)} %param.10), calls=%async_computation | async-start | bytes 131072 | tf_op jit(solution)/shard_map/slice | solution.py:238
  10.2 5.7 %slice-start.1 = ((bf16[192,256]{1,0:T(8,128)(2,1)}), bf16[64,256]{1,0:T(8,128)(2,1)S(1)}, s32[]{:S(2)}) async-start(bf16[192,256]{1,0:T(8,128)(2,1)} %param.10), calls=%async_computation.1 | async-start | bytes 65536 | tf_op jit(solution)/shard_map/slice | solution.py:238
  10.2 5.7 %copy-start.2 = (bf16[192,256]{1,0:T(8,128)(2,1)S(1)}, bf16[192,256]{1,0:T(8,128)(2,1)}, u32[]{:S(2)}) copy-start(bf16[192,256]{1,0:T(8,128)(2,1)} %param.9) | copy-start | bytes 294916
  13.3 5.6 %collective-permute-start.3 = (s32[4,1,3072]{2,1,0:T(1,128)S(1)}, s32[4,1,3072]{2,1,0:T(1,128)S(1)}, u32[]{:S(2)}, u32[]{:S(2)}) collective-permute-start(s32[4,1,3072]{2,1,0:T(1,128)S(1)} %get-tuple-element.35), channel_id=1, source_target_pairs={{0,16},{4,20},{8,24},{12,28},{16,0},{20,4},{24,8},{28,12},{1,17},{... | collective-permute-start | bytes 147464 | tf_op jit(solution)/shard_map/ppermute | solution.py:162
  37.6 2.0 %collective-permute-start.4 = (bf16[2048,128]{1,0:T(8,128)(2,1)S(1)}, bf16[2048,128]{1,0:T(8,128)(2,1)S(1)}, u32[]{:S(2)}, u32[]{:S(2)}) collective-permute-start(bf16[2048,128]{1,0:T(8,128)(2,1)S(1)} %convolution_convert_fusion.1), channel_id=1, source_target_pairs={{0,1},{1,0},{2,3},{3,2},{4,5},{5,4},{6,7},{7,6},{8,9},{9,8},{10,11... | collective-permute-start | bytes 1572872 | tf_op jit(solution)/shard_map/ppermute | solution.py:162
  37.7 3.6 %collective-permute-start.9 = (bf16[2048,128]{1,0:T(8,128)(2,1)S(1)}, bf16[2048,128]{1,0:T(8,128)(2,1)S(1)}, u32[]{:S(2)}, u32[]{:S(2)}) collective-permute-start(bf16[2048,128]{1,0:T(8,128)(2,1)S(1)} %convolution_convert_fusion), channel_id=1, source_target_pairs={{0,1},{1,0},{2,3},{3,2},{4,5},{5,4},{6,7},{7,6},{8,9},{9,8},{10,11... | collective-permute-start | bytes 1572872 | tf_op jit(solution)/shard_map/ppermute | solution.py:162
  39.8 8.4 %collective-permute-start.5 = (bf16[8,128,128]{2,1,0:T(8,128)(2,1)S(1)}, bf16[8,128,128]{2,1,0:T(8,128)(2,1)S(1)}, u32[]{:S(2)}, u32[]{:S(2)}) collective-permute-start(bf16[8,128,128]{2,1,0:T(8,128)(2,1)S(1)} %bitcast.97), channel_id=1, source_target_pairs={{0,2},{1,3},{2,0},{3,1},{4,6},{5,7},{6,4},{7,5},{8,10},{9,11},{10,... | collective-permute-start | bytes 786440 | tf_op jit(solution)/shard_map/ppermute | solution.py:162
  41.7 7.1 %collective-permute-start.10 = (bf16[4,128,128]{2,1,0:T(8,128)(2,1)S(1)}, bf16[4,128,128]{2,1,0:T(8,128)(2,1)S(1)}, u32[]{:S(2)}, u32[]{:S(2)}) collective-permute-start(bf16[4,128,128]{2,1,0:T(8,128)(2,1)S(1)} %get-tuple-element.23), channel_id=1, source_target_pairs={{0,4},{4,0},{8,12},{12,8},{16,20},{20,16},{24,28},{28,24},{1,5},{5... | collective-permute-start | bytes 393224 | tf_op jit(solution)/shard_map/ppermute | solution.py:162
  42.2 6.6 %collective-permute-start.11 = (bf16[4,128,128]{2,1,0:T(8,128)(2,1)S(1)}, bf16[4,128,128]{2,1,0:T(8,128)(2,1)S(1)}, u32[]{:S(2)}, u32[]{:S(2)}) collective-permute-start(bf16[4,128,128]{2,1,0:T(8,128)(2,1)S(1)} %get-tuple-element.25), channel_id=1, source_target_pairs={{0,8},{4,12},{8,0},{12,4},{16,24},{20,28},{24,16},{28,20},{1,9},{5... | collective-permute-start | bytes 393224 | tf_op jit(solution)/shard_map/ppermute | solution.py:162
  43.8 7.3 %collective-permute-start.12 = (bf16[4,128,128]{2,1,0:T(8,128)(2,1)S(1)}, bf16[4,128,128]{2,1,0:T(8,128)(2,1)S(1)}, u32[]{:S(2)}, u32[]{:S(2)}) collective-permute-start(bf16[4,128,128]{2,1,0:T(8,128)(2,1)S(1)} %get-tuple-element.24), channel_id=1, source_target_pairs={{0,12},{4,8},{8,4},{12,0},{16,28},{20,24},{24,20},{28,16},{1,13},{... | collective-permute-start | bytes 393224 | tf_op jit(solution)/shard_map/ppermute | solution.py:162
  48.2 15.2 %copy-start.3 = (bf16[128,256]{1,0:T(8,128)(2,1)S(1)}, bf16[128,256]{1,0:T(8,128)(2,1)}, u32[]{:S(2)}) copy-start(bf16[128,256]{1,0:T(8,128)(2,1)} %param.11) | copy-start | bytes 196612
  48.3 5.6 %collective-permute-start.6 = (bf16[4,128,128]{2,1,0:T(8,128)(2,1)S(1)}, bf16[4,128,128]{2,1,0:T(8,128)(2,1)S(1)}, u32[]{:S(2)}, u32[]{:S(2)}) collective-permute-start(bf16[4,128,128]{2,1,0:T(8,128)(2,1)S(1)} %slice.201), channel_id=1, source_target_pairs={{0,4},{4,0},{8,12},{12,8},{16,20},{20,16},{24,28},{28,24},{1,5},{5... | collective-permute-start | bytes 393224 | tf_op jit(solution)/shard_map/ppermute | solution.py:162
  51.2 4.3 %collective-permute-start.13 = (bf16[2,128,128]{2,1,0:T(8,128)(2,1)S(1)}, bf16[2,128,128]{2,1,0:T(8,128)(2,1)S(1)}, u32[]{:S(2)}, u32[]{:S(2)}) collective-permute-start(bf16[2,128,128]{2,1,0:T(8,128)(2,1)S(1)} %slice.202), channel_id=1, source_target_pairs={{0,2},{1,3},{2,0},{3,1},{4,6},{5,7},{6,4},{7,5},{8,10},{9,11},{10,... | collective-permute-start | bytes 196616 | tf_op jit(solution)/shard_map/ppermute | solution.py:162
  53.9 4.3 %collective-permute-start.7 = (bf16[2,128,128]{2,1,0:T(8,128)(2,1)S(1)}, bf16[2,128,128]{2,1,0:T(8,128)(2,1)S(1)}, u32[]{:S(2)}, u32[]{:S(2)}) collective-permute-start(bf16[2,128,128]{2,1,0:T(8,128)(2,1)S(1)} %slice.203), channel_id=1, source_target_pairs={{0,8},{4,12},{8,0},{12,4},{16,24},{20,28},{24,16},{28,20},{1,9},{5... | collective-permute-start | bytes 196616 | tf_op jit(solution)/shard_map/ppermute | solution.py:162
  55.6 5.7 %collective-permute-start.14 = (bf16[1,128,128]{2,1,0:T(8,128)(2,1)S(1)}, bf16[1,128,128]{2,1,0:T(8,128)(2,1)S(1)}, u32[]{:S(2)}, u32[]{:S(2)}) collective-permute-start(bf16[1,128,128]{2,1,0:T(8,128)(2,1)S(1)} %slice.204), channel_id=1, source_target_pairs={{0,16},{4,20},{8,24},{12,28},{16,0},{20,4},{24,8},{28,12},{1,17},{... | collective-permute-start | bytes 98312 | tf_op jit(solution)/shard_map/ppermute | solution.py:162
  58.3 5.2 %collective-permute-start.8 = (bf16[1,128,128]{2,1,0:T(8,128)(2,1)S(1)}, bf16[1,128,128]{2,1,0:T(8,128)(2,1)S(1)}, u32[]{:S(2)}, u32[]{:S(2)}) collective-permute-start(bf16[1,128,128]{2,1,0:T(8,128)(2,1)S(1)} %slice.205), channel_id=1, source_target_pairs={{0,16},{4,20},{8,24},{12,28},{16,0},{20,4},{24,8},{28,12},{1,17},{... | collective-permute-start | bytes 98312 | tf_op jit(solution)/shard_map/ppermute | solution.py:162
  64.2 5.2 %collective-permute-start.15 = (bf16[128,128]{1,0:T(8,128)(2,1)S(1)}, bf16[128,128]{1,0:T(8,128)(2,1)S(1)}, u32[]{:S(2)}, u32[]{:S(2)}) collective-permute-start(bf16[128,128]{1,0:T(8,128)(2,1)S(1)} %get-tuple-element.41), channel_id=1, source_target_pairs={{0,16},{4,20},{8,24},{12,28},{16,0},{20,4},{24,8},{28,12},{1,17},{... | collective-permute-start | bytes 98312 | tf_op jit(solution)/shard_map/ppermute | solution.py:162
  66.1 6.8 %collective-permute-start.20 = (bf16[128,128]{1,0:T(8,128)(2,1)S(1)}, bf16[128,128]{1,0:T(8,128)(2,1)S(1)}, u32[]{:S(2)}, u32[]{:S(2)}) collective-permute-start(bf16[128,128]{1,0:T(8,128)(2,1)S(1)} %get-tuple-element.40), channel_id=1, source_target_pairs={{0,16},{4,20},{8,24},{12,28},{16,0},{20,4},{24,8},{28,12},{1,17},{... | collective-permute-start | bytes 98312 | tf_op jit(solution)/shard_map/ppermute | solution.py:162
  69.4 4.9 %collective-permute-start.16 = (bf16[2,128,128]{2,1,0:T(8,128)(2,1)S(1)}, bf16[2,128,128]{2,1,0:T(8,128)(2,1)S(1)}, u32[]{:S(2)}, u32[]{:S(2)}) collective-permute-start(bf16[2,128,128]{2,1,0:T(8,128)(2,1)S(1)} %get-tuple-element.37), channel_id=1, source_target_pairs={{0,4},{4,0},{8,12},{12,8},{16,20},{20,16},{24,28},{28,24},{1,5},{5... | collective-permute-start | bytes 196616 | tf_op jit(solution)/shard_map/ppermute | solution.py:162
  70.0 4.4 %collective-permute-start.17 = (bf16[2,128,128]{2,1,0:T(8,128)(2,1)S(1)}, bf16[2,128,128]{2,1,0:T(8,128)(2,1)S(1)}, u32[]{:S(2)}, u32[]{:S(2)}) collective-permute-start(bf16[2,128,128]{2,1,0:T(8,128)(2,1)S(1)} %get-tuple-element.37), channel_id=1, source_target_pairs={{0,8},{4,12},{8,0},{12,4},{16,24},{20,28},{24,16},{28,20},{1,9},{5... | collective-permute-start | bytes 196616 | tf_op jit(solution)/shard_map/ppermute | solution.py:162
  71.0 5.5 %collective-permute-start.18 = (bf16[2,128,128]{2,1,0:T(8,128)(2,1)S(1)}, bf16[2,128,128]{2,1,0:T(8,128)(2,1)S(1)}, u32[]{:S(2)}, u32[]{:S(2)}) collective-permute-start(bf16[2,128,128]{2,1,0:T(8,128)(2,1)S(1)} %get-tuple-element.37), channel_id=1, source_target_pairs={{0,12},{4,8},{8,4},{12,0},{16,28},{20,24},{24,20},{28,16},{1,13},{... | collective-permute-start | bytes 196616 | tf_op jit(solution)/shard_map/ppermute | solution.py:162
  73.0 4.8 %collective-permute-start.21 = (bf16[2,128,128]{2,1,0:T(8,128)(2,1)S(1)}, bf16[2,128,128]{2,1,0:T(8,128)(2,1)S(1)}, u32[]{:S(2)}, u32[]{:S(2)}) collective-permute-start(bf16[2,128,128]{2,1,0:T(8,128)(2,1)S(1)} %get-tuple-element.43), channel_id=1, source_target_pairs={{0,2},{1,3},{2,0},{3,1},{4,6},{5,7},{6,4},{7,5},{8,10},{9,11},{10,... | collective-permute-start | bytes 196616 | tf_op jit(solution)/shard_map/ppermute | solution.py:162
  76.5 10.3 %collective-permute-start.19 = (bf16[4,2,128,128]{3,2,1,0:T(8,128)(2,1)S(1)}, bf16[4,2,128,128]{3,2,1,0:T(8,128)(2,1)S(1)}, u32[]{:S(2)}, u32[]{:S(2)}) collective-permute-start(bf16[4,2,128,128]{3,2,1,0:T(8,128)(2,1)S(1)} %pad_maximum_fusion.2), channel_id=1, source_target_pairs={{0,2},{1,3},{2,0},{3,1},{4,6},{5,7},{6,4},{7,5},{8,10},{9,11},{10,... | collective-permute-start | bytes 786440 | tf_op jit(solution)/shard_map/ppermute | solution.py:162
  77.8 5.0 %collective-permute-start.22 = (bf16[2,2,128,128]{3,2,1,0:T(8,128)(2,1)S(1)}, bf16[2,2,128,128]{3,2,1,0:T(8,128)(2,1)S(1)}, u32[]{:S(2)}, u32[]{:S(2)}) collective-permute-start(bf16[2,2,128,128]{3,2,1,0:T(8,128)(2,1)S(1)} %get-tuple-element.31), channel_id=1, source_target_pairs={{0,4},{4,0},{8,12},{12,8},{16,20},{20,16},{24,28},{28,24},{1,5},{5... | collective-permute-start | bytes 393224 | tf_op jit(solution)/shard_map/ppermute | solution.py:162
  78.8 5.0 %collective-permute-start.23 = (bf16[2,2,128,128]{3,2,1,0:T(8,128)(2,1)S(1)}, bf16[2,2,128,128]{3,2,1,0:T(8,128)(2,1)S(1)}, u32[]{:S(2)}, u32[]{:S(2)}) collective-permute-start(bf16[2,2,128,128]{3,2,1,0:T(8,128)(2,1)S(1)} %get-tuple-element.31), channel_id=1, source_target_pairs={{0,8},{4,12},{8,0},{12,4},{16,24},{20,28},{24,16},{28,20},{1,9},{5... | collective-permute-start | bytes 393224 | tf_op jit(solution)/shard_map/ppermute | solution.py:162
  80.8 5.9 %collective-permute-start.24 = (bf16[2,2,128,128]{3,2,1,0:T(8,128)(2,1)S(1)}, bf16[2,2,128,128]{3,2,1,0:T(8,128)(2,1)S(1)}, u32[]{:S(2)}, u32[]{:S(2)}) collective-permute-start(bf16[2,2,128,128]{3,2,1,0:T(8,128)(2,1)S(1)} %get-tuple-element.31), channel_id=1, source_target_pairs={{0,12},{4,8},{8,4},{12,0},{16,28},{20,24},{24,20},{28,16},{1,13},{... | collective-permute-start | bytes 393224 | tf_op jit(solution)/shard_map/ppermute | solution.py:162
  86.7 2.0 %collective-permute-start.26 = (bf16[2048,128]{1,0:T(8,128)(2,1)S(1)}, bf16[2048,128]{1,0:T(8,128)(2,1)S(1)}, u32[]{:S(2)}, u32[]{:S(2)}) collective-permute-start(bf16[2048,128]{1,0:T(8,128)(2,1)S(1)} %bitcast.93), channel_id=1, source_target_pairs={{0,1},{1,0},{2,3},{3,2},{4,5},{5,4},{6,7},{7,6},{8,9},{9,8},{10,11... | collective-permute-start | bytes 1572872 | tf_op jit(solution)/shard_map/ppermute | solution.py:162
  86.9 2.6 %collective-permute-start.25 = (bf16[2048,128]{1,0:T(8,128)(2,1)S(1)}, bf16[2048,128]{1,0:T(8,128)(2,1)S(1)}, u32[]{:S(2)}, u32[]{:S(2)}) collective-permute-start(bf16[2048,128]{1,0:T(8,128)(2,1)S(1)} %bitcast.95), channel_id=1, source_target_pairs={{0,1},{1,0},{2,3},{3,2},{4,5},{5,4},{6,7},{7,6},{8,9},{9,8},{10,11... | collective-permute-start | bytes 1572872 | tf_op jit(solution)/shard_map/ppermute | solution.py:162
  90.1 4.9 %collective-permute-start.27 = (bf16[192,256]{1,0:T(8,128)(2,1)S(1)}, bf16[192,256]{1,0:T(8,128)(2,1)S(1)}, u32[]{:S(2)}, u32[]{:S(2)}) collective-permute-start(bf16[192,256]{1,0:T(8,128)(2,1)S(1)} %get-tuple-element.29), channel_id=1, source_target_pairs={{0,4},{4,0},{8,12},{12,8},{16,20},{20,16},{24,28},{28,24},{1,5},{5... | collective-permute-start | bytes 294920 | tf_op jit(solution)/shard_map/ppermute | solution.py:162
  90.3 4.8 %collective-permute-start.30 = (bf16[192,256]{1,0:T(8,128)(2,1)S(1)}, bf16[192,256]{1,0:T(8,128)(2,1)S(1)}, u32[]{:S(2)}, u32[]{:S(2)}) collective-permute-start(bf16[192,256]{1,0:T(8,128)(2,1)S(1)} %get-tuple-element.28), channel_id=1, source_target_pairs={{0,8},{4,12},{8,0},{12,4},{16,24},{20,28},{24,16},{28,20},{1,9},{5... | collective-permute-start | bytes 294920 | tf_op jit(solution)/shard_map/ppermute | solution.py:162
  95.2 7.2 %collective-permute-start.31 = (bf16[192,256]{1,0:T(8,128)(2,1)S(1)}, bf16[192,256]{1,0:T(8,128)(2,1)S(1)}, u32[]{:S(2)}, u32[]{:S(2)}) collective-permute-start(bf16[192,256]{1,0:T(8,128)(2,1)S(1)} %get-tuple-element.26), channel_id=1, source_target_pairs={{0,16},{4,20},{8,24},{12,28},{16,0},{20,4},{24,8},{28,12},{1,17},{... | collective-permute-start | bytes 294920 | tf_op jit(solution)/shard_map/ppermute | solution.py:162
  97.2 6.4 %collective-permute-start.28 = (bf16[192,256]{1,0:T(8,128)(2,1)S(1)}, bf16[192,256]{1,0:T(8,128)(2,1)S(1)}, u32[]{:S(2)}, u32[]{:S(2)}) collective-permute-start(bf16[192,256]{1,0:T(8,128)(2,1)S(1)} %get-tuple-element.27), channel_id=1, source_target_pairs={{0,8},{4,12},{8,0},{12,4},{16,24},{20,28},{24,16},{28,20},{1,9},{5... | collective-permute-start | bytes 294920 | tf_op jit(solution)/shard_map/ppermute | solution.py:162
  102.3 4.7 %collective-permute-start.32 = (bf16[192,256]{1,0:T(8,128)(2,1)S(1)}, bf16[192,256]{1,0:T(8,128)(2,1)S(1)}, u32[]{:S(2)}, u32[]{:S(2)}) collective-permute-start(bf16[192,256]{1,0:T(8,128)(2,1)S(1)} %add_convert_fusion), channel_id=1, source_target_pairs={{0,4},{4,0},{8,12},{12,8},{16,20},{20,16},{24,28},{28,24},{1,5},{5... | collective-permute-start | bytes 294920 | tf_op jit(solution)/shard_map/ppermute | solution.py:162
  103.6 6.0 %collective-permute-start.29 = (bf16[192,256]{1,0:T(8,128)(2,1)S(1)}, bf16[192,256]{1,0:T(8,128)(2,1)S(1)}, u32[]{:S(2)}, u32[]{:S(2)}) collective-permute-start(bf16[192,256]{1,0:T(8,128)(2,1)S(1)} %add_convert_fusion.2), channel_id=1, source_target_pairs={{0,16},{4,20},{8,24},{12,28},{16,0},{20,4},{24,8},{28,12},{1,17},{... | collective-permute-start | bytes 294920 | tf_op jit(solution)/shard_map/ppermute | solution.py:162

commit v7 on v6

--- a/solution.py
+++ b/solution.py
@@ -237,9 +237,10 @@
     weights = jnp.concatenate(
         [w_self, w_neighbor[128:], w_neighbor[:128]], axis=0
     )
-    came = [swap(parts[m], "wide", m) for m in range(1, 4)]
-    came, table = lax.optimization_barrier((came, table))
-    asked = jnp.stack([parts[0]] + came).reshape(4, wide_count // 4, 2 * capacity)
+    odd = swap(jnp.stack([parts[1], parts[3]]), "wide", 1)
+    odd, table = lax.optimization_barrier((odd, table))
+    high = swap(jnp.stack([parts[2], odd[1]]), "wide", 2)
+    asked = jnp.stack([parts[0], odd[0], high[0], high[1]]).reshape(4, wide_count // 4, 2 * capacity)
     for b in range(2, bits):
         split = asked.reshape(asked.shape[0], -1, 2, 2 * capacity)
         asked = jnp.concatenate([split[:, :, 0], swap(split[:, :, 1], "wide", 1 << b)], axis=0)

time: 111 us -> 114 us (1.027)
  waiting for transfers between devices: 35.1 us -> 38.9 us
  starting transfers between devices: 40.3 us -> 39 us
    ppermute x33 -> x32, waiting for transfers between devices: 35.1 us -> 38.9 us  [swap(): return lax.ppermute(value, axis, [(i, i ^ bit) for i in range(count)])]
    ppermute x33 -> x32, starting transfers between devices: 40.3 us -> 39 us  [swap(): return lax.ppermute(value, axis, [(i, i ^ bit) for i in range(count)])]
  transfers between devices with their start and end apart: 33 -> 32, of which waited for: 23 -> 23; matrix products, arithmetic and copies ran while one was open for 3% -> 3% of each run, Pallas kernels for 4% -> 4%
where the time goes in v7:
time: 114 us
  starting transfers between devices  39 us (34%)
  waiting for transfers between devices  38.9 us (34%)
  Pallas kernels  25.2 us (22%)
  other arithmetic  3.67 us (3%)
  matrix products  3.51 us (3%)
  local copies, waits for them, and re-layouts  2.34 us (2%)
    ppermute x32, starting transfers between devices, swap(): return lax.ppermute(value, axis, [(i, i ^ bit) for i in range(count)])  39 us
    ppermute x32, waiting for transfers between devices, swap(): return lax.ppermute(value, axis, [(i, i ^ bit) for i in range(count)])  38.9 us
    pallas_call x1, Pallas kernels, on_device(): pl.pallas_call(functools.partial(owner_kernel, tgt_bits), grid_spec=pltpu...  17.6 us
    pallas_call x1, Pallas kernels, on_device(): pl.pallas_call(functools.partial(list_kernel, wide_count, capacity, tgt_b...  3.18 us
    pallas_call x1, Pallas kernels, on_device(): pl.pallas_call(functools.partial(first_kernel, unroll), grid_spec=pltpu.P...  2.75 us
  transfers between devices with their start and end apart: 32, of which 23 were waited for; matrix products, arithmetic and copies ran while one was open for 3% of the time, Pallas kernels for 4%

profile of v7, /device:TPU:0, one launch (start us, length us, event | category | flops | bytes accessed | tf_op | source)
XLA Modules:
  0.0 113.6 jit_solution(12290183158730041204)
XLA Ops:
  0.6 3.2 %lists.1 = (s32[48,128]{1,0:T(8,128)}, s32[48,128]{1,0:T(8,128)}, s32[48,128]{1,0:T(8,128)}, s32[48,128]{1,0:T(8,128)}) custom-call(s32[16,1,512]{2,1,0:T(1,128)} %bitcast.109, s32[16,512]{1,0:T(8,128)} %bitcast.110), custom_call_target="tpu_custom_call" | custom-call | tf_op jit(solution)/shard_map/lists/pallas_call | solution.py:227
  3.8 0.8 pad_add_fusion.2
  4.6 3.0 %collective-permute-start = (s32[2,48,128]{2,1,0:T(8,128)S(1)}, s32[2,48,128]{2,1,0:T(8,128)S(1)}, u32[]{:S(2)}, u32[]{:S(2)}) collective-permute-start(s32[2,48,128]{2,1,0:T(8,128)S(1)} %pad_add_fusion.2), channel_id=1, source_target_pairs={{0,4},{4,0},{8,12},{12,8},{16,20},{20,16},{24,28},{28,24},{1,5},{5... | collective-permute-start | bytes 147464 | tf_op jit(solution)/shard_map/ppermute | solution.py:162
  7.5 1.9 %copy-done = bf16[192,8192]{1,0:T(8,128)(2,1)S(1)} copy-done((bf16[192,8192]{1,0:T(8,128)(2,1)S(1)}, bf16[192,8192]{1,0:T(8,128)(2,1)}, u32[]{:S(2)}) %copy-start) | copy-done | bytes 3145752
  9.5 1.6 %table.1.table_ref = f32[8192,2,128]{2,1,0:T(2,128)S(1)} custom-call(bf16[192,8192]{1,0:T(8,128)(2,1)S(1)} %copy-done), custom_call_target="tpu_custom_call" | custom-call | bytes 25165824 | tf_op jit(solution)/shard_map/table/pallas_call | solution.py:214
  11.1 1.6 %collective-permute-start.1 = (s32[2,48,128]{2,1,0:T(8,128)S(1)}, s32[2,48,128]{2,1,0:T(8,128)S(1)}, u32[]{:S(2)}, u32[]{:S(2)}) collective-permute-start(s32[2,48,128]{2,1,0:T(8,128)S(1)} %pad_add_fusion.3), channel_id=1, source_target_pairs={{0,8},{4,12},{8,0},{12,4},{16,24},{20,28},{24,16},{28,20},{1,9},{5... | collective-permute-start | bytes 147464 | tf_op jit(solution)/shard_map/ppermute | solution.py:162
  12.8 2.5 %collective-permute-done.1 = s32[2,48,128]{2,1,0:T(8,128)S(1)} collective-permute-done((s32[2,48,128]{2,1,0:T(8,128)S(1)}, s32[2,48,128]{2,1,0:T(8,128)S(1)}, u32[]{:S(2)}, u32[]{:S(2)}) %collective-permute-start.1) | collective-permute-done | bytes 49184 | tf_op jit(solution)/shard_map/ppermute | solution.py:162
  15.3 2.7 %collective-permute-start.2 = (s32[4,1,3072]{2,1,0:T(1,128)S(1)}, s32[4,1,3072]{2,1,0:T(1,128)S(1)}, u32[]{:S(2)}, u32[]{:S(2)}) collective-permute-start(s32[4,1,3072]{2,1,0:T(1,128)S(1)} %get-tuple-element.31), channel_id=1, source_target_pairs={{0,16},{4,20},{8,24},{12,28},{16,0},{20,4},{24,8},{28,12},{1,17},{... | collective-permute-start | bytes 147464 | tf_op jit(solution)/shard_map/ppermute | solution.py:162
  18.0 2.7 %first.1.first_ref = bf16[1536,256]{1,0:T(8,128)(2,1)S(1)} custom-call(s32[6144]{0:T(1024)S(1)} %bitcast.87, f32[8192,2,128]{2,1,0:T(2,128)S(1)} %table.1.table_ref), custom_call_target="tpu_custom_call" | custom-call | bytes 4194304 | tf_op jit(solution)/shard_map/first/pallas_call | solution.py:250
  20.8 17.6 %owner.1 = (bf16[2,8,128,384]{3,2,1,0:T(8,128)(2,1)S(1)}, bf16[2,8,128,384]{3,2,1,0:T(8,128)(2,1)S(1)}) custom-call(s32[24576]{0:T(1024)S(1)} %bitcast.85, s32[8,1,3072]{2,1,0:T(1,128)S(1)} %pad_add_fusion.1.key_ref, f32[8192,2,128]{2,1,0:T(2,128)S(1)} %table.1.table_ref, bf16[1536,256]{1,0:T(8,128)(2,1)S(1)} %first.1.first_ref), custom_call_target="tpu_custom_call" | custom-call | tf_op jit(solution)/shard_map/owner/pallas_call | solution.py:265
  41.7 1.6 %collective-permute-start.4 = (bf16[8,128,128]{2,1,0:T(8,128)(2,1)S(1)}, bf16[8,128,128]{2,1,0:T(8,128)(2,1)S(1)}, u32[]{:S(2)}, u32[]{:S(2)}) collective-permute-start(bf16[8,128,128]{2,1,0:T(8,128)(2,1)S(1)} %bitcast.99), channel_id=1, source_target_pairs={{0,2},{1,3},{2,0},{3,1},{4,6},{5,7},{6,4},{7,5},{8,10},{9,11},{10,... | collective-permute-start | bytes 786440 | tf_op jit(solution)/shard_map/ppermute | solution.py:162
  43.6 1.6 %collective-permute-start.10 = (bf16[4,128,128]{2,1,0:T(8,128)(2,1)S(1)}, bf16[4,128,128]{2,1,0:T(8,128)(2,1)S(1)}, u32[]{:S(2)}, u32[]{:S(2)}) collective-permute-start(bf16[4,128,128]{2,1,0:T(8,128)(2,1)S(1)} %get-tuple-element.21), channel_id=1, source_target_pairs={{0,8},{4,12},{8,0},{12,4},{16,24},{20,28},{24,16},{28,20},{1,9},{5... | collective-permute-start | bytes 393224 | tf_op jit(solution)/shard_map/ppermute | solution.py:162
  45.7 1.5 %collective-permute-start.9 = (bf16[4,128,128]{2,1,0:T(8,128)(2,1)S(1)}, bf16[4,128,128]{2,1,0:T(8,128)(2,1)S(1)}, u32[]{:S(2)}, u32[]{:S(2)}) collective-permute-start(bf16[4,128,128]{2,1,0:T(8,128)(2,1)S(1)} %get-tuple-element.19), channel_id=1, source_target_pairs={{0,4},{4,0},{8,12},{12,8},{16,20},{20,16},{24,28},{28,24},{1,5},{5... | collective-permute-start | bytes 393224 | tf_op jit(solution)/shard_map/ppermute | solution.py:162
  47.2 2.9 %collective-permute-done.4 = bf16[8,128,128]{2,1,0:T(8,128)(2,1)S(1)} collective-permute-done((bf16[8,128,128]{2,1,0:T(8,128)(2,1)S(1)}, bf16[8,128,128]{2,1,0:T(8,128)(2,1)S(1)}, u32[]{:S(2)}, u32[]{:S(2)}) %collective-permute-start.4) | collective-permute-done | bytes 262176 | tf_op jit(solution)/shard_map/ppermute | solution.py:162
  50.8 1.0 collective-permute-done.11
  51.8 2.3 %collective-permute-done.9 = bf16[4,128,128]{2,1,0:T(8,128)(2,1)S(1)} collective-permute-done((bf16[4,128,128]{2,1,0:T(8,128)(2,1)S(1)}, bf16[4,128,128]{2,1,0:T(8,128)(2,1)S(1)}, u32[]{:S(2)}, u32[]{:S(2)}) %collective-permute-start.9) | collective-permute-done | bytes 131104 | tf_op jit(solution)/shard_map/ppermute | solution.py:162
  54.3 1.6 %collective-permute-done.5 = bf16[4,128,128]{2,1,0:T(8,128)(2,1)S(1)} collective-permute-done((bf16[4,128,128]{2,1,0:T(8,128)(2,1)S(1)}, bf16[4,128,128]{2,1,0:T(8,128)(2,1)S(1)}, u32[]{:S(2)}, u32[]{:S(2)}) %collective-permute-start.5) | collective-permute-done | bytes 131104 | tf_op jit(solution)/shard_map/ppermute | solution.py:162
  56.0 1.7 %collective-permute-start.6 = (bf16[2,128,128]{2,1,0:T(8,128)(2,1)S(1)}, bf16[2,128,128]{2,1,0:T(8,128)(2,1)S(1)}, u32[]{:S(2)}, u32[]{:S(2)}) collective-permute-start(bf16[2,128,128]{2,1,0:T(8,128)(2,1)S(1)} %slice.214), channel_id=1, source_target_pairs={{0,8},{4,12},{8,0},{12,4},{16,24},{20,28},{24,16},{28,20},{1,9},{5... | collective-permute-start | bytes 196616 | tf_op jit(solution)/shard_map/ppermute | solution.py:162
  57.7 0.8 collective-permute-done.12
  58.5 2.9 %collective-permute-start.13 = (bf16[1,128,128]{2,1,0:T(8,128)(2,1)S(1)}, bf16[1,128,128]{2,1,0:T(8,128)(2,1)S(1)}, u32[]{:S(2)}, u32[]{:S(2)}) collective-permute-start(bf16[1,128,128]{2,1,0:T(8,128)(2,1)S(1)} %slice.215), channel_id=1, source_target_pairs={{0,16},{4,20},{8,24},{12,28},{16,0},{20,4},{24,8},{28,12},{1,17},{... | collective-permute-start | bytes 98312 | tf_op jit(solution)/shard_map/ppermute | solution.py:162
  61.4 1.5 %collective-permute-start.7 = (bf16[1,128,128]{2,1,0:T(8,128)(2,1)S(1)}, bf16[1,128,128]{2,1,0:T(8,128)(2,1)S(1)}, u32[]{:S(2)}, u32[]{:S(2)}) collective-permute-start(bf16[1,128,128]{2,1,0:T(8,128)(2,1)S(1)} %slice.216), channel_id=1, source_target_pairs={{0,16},{4,20},{8,24},{12,28},{16,0},{20,4},{24,8},{28,12},{1,17},{... | collective-permute-start | bytes 98312 | tf_op jit(solution)/shard_map/ppermute | solution.py:162
  62.9 0.8 collective-permute-done.13
  63.8 2.5 %collective-permute-done.7 = bf16[1,128,128]{2,1,0:T(8,128)(2,1)S(1)} collective-permute-done((bf16[1,128,128]{2,1,0:T(8,128)(2,1)S(1)}, bf16[1,128,128]{2,1,0:T(8,128)(2,1)S(1)}, u32[]{:S(2)}, u32[]{:S(2)}) %collective-permute-start.7) | collective-permute-done | bytes 32800 | tf_op jit(solution)/shard_map/ppermute | solution.py:162
  66.3 0.7 fusion.13
  67.1 1.5 %collective-permute-start.14 = (bf16[128,128]{1,0:T(8,128)(2,1)S(1)}, bf16[128,128]{1,0:T(8,128)(2,1)S(1)}, u32[]{:S(2)}, u32[]{:S(2)}) collective-permute-start(bf16[128,128]{1,0:T(8,128)(2,1)S(1)} %get-tuple-element.37), channel_id=1, source_target_pairs={{0,16},{4,20},{8,24},{12,28},{16,0},{20,4},{24,8},{28,12},{1,17},{... | collective-permute-start | bytes 98312 | tf_op jit(solution)/shard_map/ppermute | solution.py:162
  68.6 1.5 %collective-permute-start.19 = (bf16[128,128]{1,0:T(8,128)(2,1)S(1)}, bf16[128,128]{1,0:T(8,128)(2,1)S(1)}, u32[]{:S(2)}, u32[]{:S(2)}) collective-permute-start(bf16[128,128]{1,0:T(8,128)(2,1)S(1)} %get-tuple-element.36), channel_id=1, source_target_pairs={{0,16},{4,20},{8,24},{12,28},{16,0},{20,4},{24,8},{28,12},{1,17},{... | collective-permute-start | bytes 98312 | tf_op jit(solution)/shard_map/ppermute | solution.py:162
  70.1 2.0 %collective-permute-done.14 = bf16[128,128]{1,0:T(8,128)(2,1)S(1)} collective-permute-done((bf16[128,128]{1,0:T(8,128)(2,1)S(1)}, bf16[128,128]{1,0:T(8,128)(2,1)S(1)}, u32[]{:S(2)}, u32[]{:S(2)}) %collective-permute-start.14) | collective-permute-done | bytes 32800 | tf_op jit(solution)/shard_map/ppermute | solution.py:162
  72.1 1.2 %collective-permute-start.15 = (bf16[2,128,128]{2,1,0:T(8,128)(2,1)S(1)}, bf16[2,128,128]{2,1,0:T(8,128)(2,1)S(1)}, u32[]{:S(2)}, u32[]{:S(2)}) collective-permute-start(bf16[2,128,128]{2,1,0:T(8,128)(2,1)S(1)} %get-tuple-element.33), channel_id=1, source_target_pairs={{0,4},{4,0},{8,12},{12,8},{16,20},{20,16},{24,28},{28,24},{1,5},{5... | collective-permute-start | bytes 196616 | tf_op jit(solution)/shard_map/ppermute | solution.py:162
  73.3 2.0 %collective-permute-start.16 = (bf16[2,128,128]{2,1,0:T(8,128)(2,1)S(1)}, bf16[2,128,128]{2,1,0:T(8,128)(2,1)S(1)}, u32[]{:S(2)}, u32[]{:S(2)}) collective-permute-start(bf16[2,128,128]{2,1,0:T(8,128)(2,1)S(1)} %get-tuple-element.33), channel_id=1, source_target_pairs={{0,8},{4,12},{8,0},{12,4},{16,24},{20,28},{24,16},{28,20},{1,9},{5... | collective-permute-start | bytes 196616 | tf_op jit(solution)/shard_map/ppermute | solution.py:162
  76.4 1.4 %collective-permute-done.16 = bf16[2,128,128]{2,1,0:T(8,128)(2,1)S(1)} collective-permute-done((bf16[2,128,128]{2,1,0:T(8,128)(2,1)S(1)}, bf16[2,128,128]{2,1,0:T(8,128)(2,1)S(1)}, u32[]{:S(2)}, u32[]{:S(2)}) %collective-permute-start.16) | collective-permute-done | bytes 65568 | tf_op jit(solution)/shard_map/ppermute | solution.py:162
  77.8 3.5 %collective-permute-done.17 = bf16[2,128,128]{2,1,0:T(8,128)(2,1)S(1)} collective-permute-done((bf16[2,128,128]{2,1,0:T(8,128)(2,1)S(1)}, bf16[2,128,128]{2,1,0:T(8,128)(2,1)S(1)}, u32[]{:S(2)}, u32[]{:S(2)}) %collective-permute-start.17) | collective-permute-done | bytes 65568 | tf_op jit(solution)/shard_map/ppermute | solution.py:162
  81.3 0.7 collective-permute-start.18
  82.1 1.8 %collective-permute-start.22 = (bf16[2,2,128,128]{3,2,1,0:T(8,128)(2,1)S(1)}, bf16[2,2,128,128]{3,2,1,0:T(8,128)(2,1)S(1)}, u32[]{:S(2)}, u32[]{:S(2)}) collective-permute-start(bf16[2,2,128,128]{3,2,1,0:T(8,128)(2,1)S(1)} %get-tuple-element.27), channel_id=1, source_target_pairs={{0,8},{4,12},{8,0},{12,4},{16,24},{20,28},{24,16},{28,20},{1,9},{5... | collective-permute-start | bytes 393224 | tf_op jit(solution)/shard_map/ppermute | solution.py:162
  84.0 1.7 %collective-permute-start.23 = (bf16[2,2,128,128]{3,2,1,0:T(8,128)(2,1)S(1)}, bf16[2,2,128,128]{3,2,1,0:T(8,128)(2,1)S(1)}, u32[]{:S(2)}, u32[]{:S(2)}) collective-permute-start(bf16[2,2,128,128]{3,2,1,0:T(8,128)(2,1)S(1)} %get-tuple-element.27), channel_id=1, source_target_pairs={{0,12},{4,8},{8,4},{12,0},{16,28},{20,24},{24,20},{28,16},{1,13},{... | collective-permute-start | bytes 393224 | tf_op jit(solution)/shard_map/ppermute | solution.py:162
  85.6 1.5 %collective-permute-done.21 = bf16[2,2,128,128]{3,2,1,0:T(8,128)(2,1)S(1)} collective-permute-done((bf16[2,2,128,128]{3,2,1,0:T(8,128)(2,1)S(1)}, bf16[2,2,128,128]{3,2,1,0:T(8,128)(2,1)S(1)}, u32[]{:S(2)}, u32[]{:S(2)}) %collective-permute-start.21) | collective-permute-done | bytes 131104 | tf_op jit(solution)/shard_map/ppermute | solution.py:162
  87.2 2.8 %collective-permute-done.23 = bf16[2,2,128,128]{3,2,1,0:T(8,128)(2,1)S(1)} collective-permute-done((bf16[2,2,128,128]{3,2,1,0:T(8,128)(2,1)S(1)}, bf16[2,2,128,128]{3,2,1,0:T(8,128)(2,1)S(1)}, u32[]{:S(2)}, u32[]{:S(2)}) %collective-permute-start.23) | collective-permute-done | bytes 131104 | tf_op jit(solution)/shard_map/ppermute | solution.py:162
  91.4 0.6 collective-permute-done.25
  92.1 0.7 collective-permute-done.24
  93.6 2.0 %collective-permute-start.29 = (bf16[192,256]{1,0:T(8,128)(2,1)S(1)}, bf16[192,256]{1,0:T(8,128)(2,1)S(1)}, u32[]{:S(2)}, u32[]{:S(2)}) collective-permute-start(bf16[192,256]{1,0:T(8,128)(2,1)S(1)} %get-tuple-element.24), channel_id=1, source_target_pairs={{0,8},{4,12},{8,0},{12,4},{16,24},{20,28},{24,16},{28,20},{1,9},{5... | collective-permute-start | bytes 294920 | tf_op jit(solution)/shard_map/ppermute | solution.py:162
  95.6 2.8 %collective-permute-done.26 = bf16[192,256]{1,0:T(8,128)(2,1)S(1)} collective-permute-done((bf16[192,256]{1,0:T(8,128)(2,1)S(1)}, bf16[192,256]{1,0:T(8,128)(2,1)S(1)}, u32[]{:S(2)}, u32[]{:S(2)}) %collective-permute-start.26) | collective-permute-done | bytes 98336 | tf_op jit(solution)/shard_map/ppermute | solution.py:162
  98.5 1.7 %collective-permute-start.30 = (bf16[192,256]{1,0:T(8,128)(2,1)S(1)}, bf16[192,256]{1,0:T(8,128)(2,1)S(1)}, u32[]{:S(2)}, u32[]{:S(2)}) collective-permute-start(bf16[192,256]{1,0:T(8,128)(2,1)S(1)} %get-tuple-element.22), channel_id=1, source_target_pairs={{0,16},{4,20},{8,24},{12,28},{16,0},{20,4},{24,8},{28,12},{1,17},{... | collective-permute-start | bytes 294920 | tf_op jit(solution)/shard_map/ppermute | solution.py:162
  100.2 1.6 %collective-permute-start.27 = (bf16[192,256]{1,0:T(8,128)(2,1)S(1)}, bf16[192,256]{1,0:T(8,128)(2,1)S(1)}, u32[]{:S(2)}, u32[]{:S(2)}) collective-permute-start(bf16[192,256]{1,0:T(8,128)(2,1)S(1)} %get-tuple-element.23), channel_id=1, source_target_pairs={{0,8},{4,12},{8,0},{12,4},{16,24},{20,28},{24,16},{28,20},{1,9},{5... | collective-permute-start | bytes 294920 | tf_op jit(solution)/shard_map/ppermute | solution.py:162
  101.8 3.8 %collective-permute-done.30 = bf16[192,256]{1,0:T(8,128)(2,1)S(1)} collective-permute-done((bf16[192,256]{1,0:T(8,128)(2,1)S(1)}, bf16[192,256]{1,0:T(8,128)(2,1)S(1)}, u32[]{:S(2)}, u32[]{:S(2)}) %collective-permute-start.30) | collective-permute-done | bytes 98336 | tf_op jit(solution)/shard_map/ppermute | solution.py:162
  105.6 1.4 %collective-permute-start.31 = (bf16[192,256]{1,0:T(8,128)(2,1)S(1)}, bf16[192,256]{1,0:T(8,128)(2,1)S(1)}, u32[]{:S(2)}, u32[]{:S(2)}) collective-permute-start(bf16[192,256]{1,0:T(8,128)(2,1)S(1)} %add_convert_fusion), channel_id=1, source_target_pairs={{0,4},{4,0},{8,12},{12,8},{16,20},{20,16},{24,28},{28,24},{1,5},{5... | collective-permute-start | bytes 294920 | tf_op jit(solution)/shard_map/ppermute | solution.py:162
  107.5 2.7 %collective-permute-done.31 = bf16[192,256]{1,0:T(8,128)(2,1)S(1)} collective-permute-done((bf16[192,256]{1,0:T(8,128)(2,1)S(1)}, bf16[192,256]{1,0:T(8,128)(2,1)S(1)}, u32[]{:S(2)}, u32[]{:S(2)}) %collective-permute-start.31) | collective-permute-done | bytes 98336 | tf_op jit(solution)/shard_map/ppermute | solution.py:162
  110.3 0.7 pad_maximum_fusion.4
  111.0 1.9 %collective-permute-done.28 = bf16[192,256]{1,0:T(8,128)(2,1)S(1)} collective-permute-done((bf16[192,256]{1,0:T(8,128)(2,1)S(1)}, bf16[192,256]{1,0:T(8,128)(2,1)S(1)}, u32[]{:S(2)}, u32[]{:S(2)}) %collective-permute-start.28) | collective-permute-done | bytes 98336 | tf_op jit(solution)/shard_map/ppermute | solution.py:162
  112.9 0.7 convert_add_fusion.3
  (88 shorter events, 9.3 us)
Async XLA Ops:
  4.6 6.5 %collective-permute-start = (s32[2,48,128]{2,1,0:T(8,128)S(1)}, s32[2,48,128]{2,1,0:T(8,128)S(1)}, u32[]{:S(2)}, u32[]{:S(2)}) collective-permute-start(s32[2,48,128]{2,1,0:T(8,128)S(1)} %pad_add_fusion.2), channel_id=1, source_target_pairs={{0,4},{4,0},{8,12},{12,8},{16,20},{20,16},{24,28},{28,24},{1,5},{5... | collective-permute-start | bytes 147464 | tf_op jit(solution)/shard_map/ppermute | solution.py:162
  7.5 1.9 %copy-start = (bf16[192,8192]{1,0:T(8,128)(2,1)S(1)}, bf16[192,8192]{1,0:T(8,128)(2,1)}, u32[]{:S(2)}) copy-start(bf16[192,8192]{1,0:T(8,128)(2,1)} %feature_ref.1) | copy-start | bytes 9437188
  9.4 1.7 %copy-start.4 = (s32[48,128]{1,0:T(8,128)S(1)}, s32[48,128]{1,0:T(8,128)}, u32[]{:S(2)}) copy-start(s32[48,128]{1,0:T(8,128)} %get-tuple-element.15) | copy-start | bytes 73732
  9.4 5.9 %copy-start.1 = (s32[48,128]{1,0:T(8,128)S(1)}, s32[48,128]{1,0:T(8,128)}, u32[]{:S(2)}) copy-start(s32[48,128]{1,0:T(8,128)} %get-tuple-element.11) | copy-start | bytes 73732
  9.4 8.6 %slice-start = ((bf16[192,256]{1,0:T(8,128)(2,1)}), bf16[128,256]{1,0:T(8,128)(2,1)S(1)}, s32[]{:S(2)}) async-start(bf16[192,256]{1,0:T(8,128)(2,1)} %param.10), calls=%async_computation | async-start | bytes 131072 | tf_op jit(solution)/shard_map/slice | solution.py:238
  9.4 8.6 %slice-start.1 = ((bf16[192,256]{1,0:T(8,128)(2,1)}), bf16[64,256]{1,0:T(8,128)(2,1)S(1)}, s32[]{:S(2)}) async-start(bf16[192,256]{1,0:T(8,128)(2,1)} %param.10), calls=%async_computation.1 | async-start | bytes 65536 | tf_op jit(solution)/shard_map/slice | solution.py:238
  9.4 8.6 %copy-start.2 = (bf16[192,256]{1,0:T(8,128)(2,1)S(1)}, bf16[192,256]{1,0:T(8,128)(2,1)}, u32[]{:S(2)}) copy-start(bf16[192,256]{1,0:T(8,128)(2,1)} %param.9) | copy-start | bytes 294916
  11.1 4.2 %collective-permute-start.1 = (s32[2,48,128]{2,1,0:T(8,128)S(1)}, s32[2,48,128]{2,1,0:T(8,128)S(1)}, u32[]{:S(2)}, u32[]{:S(2)}) collective-permute-start(s32[2,48,128]{2,1,0:T(8,128)S(1)} %pad_add_fusion.3), channel_id=1, source_target_pairs={{0,8},{4,12},{8,0},{12,4},{16,24},{20,28},{24,16},{28,20},{1,9},{5... | collective-permute-start | bytes 147464 | tf_op jit(solution)/shard_map/ppermute | solution.py:162
  15.3 5.4 %collective-permute-start.2 = (s32[4,1,3072]{2,1,0:T(1,128)S(1)}, s32[4,1,3072]{2,1,0:T(1,128)S(1)}, u32[]{:S(2)}, u32[]{:S(2)}) collective-permute-start(s32[4,1,3072]{2,1,0:T(1,128)S(1)} %get-tuple-element.31), channel_id=1, source_target_pairs={{0,16},{4,20},{8,24},{12,28},{16,0},{20,4},{24,8},{28,12},{1,17},{... | collective-permute-start | bytes 147464 | tf_op jit(solution)/shard_map/ppermute | solution.py:162
  39.6 2.0 %collective-permute-start.3 = (bf16[2048,128]{1,0:T(8,128)(2,1)S(1)}, bf16[2048,128]{1,0:T(8,128)(2,1)S(1)}, u32[]{:S(2)}, u32[]{:S(2)}) collective-permute-start(bf16[2048,128]{1,0:T(8,128)(2,1)S(1)} %convolution_convert_fusion.1), channel_id=1, source_target_pairs={{0,1},{1,0},{2,3},{3,2},{4,5},{5,4},{6,7},{7,6},{8,9},{9,8},{10,11... | collective-permute-start | bytes 1572872 | tf_op jit(solution)/shard_map/ppermute | solution.py:162
  39.6 3.6 %collective-permute-start.8 = (bf16[2048,128]{1,0:T(8,128)(2,1)S(1)}, bf16[2048,128]{1,0:T(8,128)(2,1)S(1)}, u32[]{:S(2)}, u32[]{:S(2)}) collective-permute-start(bf16[2048,128]{1,0:T(8,128)(2,1)S(1)} %convolution_convert_fusion), channel_id=1, source_target_pairs={{0,1},{1,0},{2,3},{3,2},{4,5},{5,4},{6,7},{7,6},{8,9},{9,8},{10,11... | collective-permute-start | bytes 1572872 | tf_op jit(solution)/shard_map/ppermute | solution.py:162
  41.7 8.4 %collective-permute-start.4 = (bf16[8,128,128]{2,1,0:T(8,128)(2,1)S(1)}, bf16[8,128,128]{2,1,0:T(8,128)(2,1)S(1)}, u32[]{:S(2)}, u32[]{:S(2)}) collective-permute-start(bf16[8,128,128]{2,1,0:T(8,128)(2,1)S(1)} %bitcast.99), channel_id=1, source_target_pairs={{0,2},{1,3},{2,0},{3,1},{4,6},{5,7},{6,4},{7,5},{8,10},{9,11},{10,... | collective-permute-start | bytes 786440 | tf_op jit(solution)/shard_map/ppermute | solution.py:162
  43.6 7.1 %collective-permute-start.10 = (bf16[4,128,128]{2,1,0:T(8,128)(2,1)S(1)}, bf16[4,128,128]{2,1,0:T(8,128)(2,1)S(1)}, u32[]{:S(2)}, u32[]{:S(2)}) collective-permute-start(bf16[4,128,128]{2,1,0:T(8,128)(2,1)S(1)} %get-tuple-element.21), channel_id=1, source_target_pairs={{0,8},{4,12},{8,0},{12,4},{16,24},{20,28},{24,16},{28,20},{1,9},{5... | collective-permute-start | bytes 393224 | tf_op jit(solution)/shard_map/ppermute | solution.py:162
  45.2 6.6 %collective-permute-start.11 = (bf16[4,128,128]{2,1,0:T(8,128)(2,1)S(1)}, bf16[4,128,128]{2,1,0:T(8,128)(2,1)S(1)}, u32[]{:S(2)}, u32[]{:S(2)}) collective-permute-start(bf16[4,128,128]{2,1,0:T(8,128)(2,1)S(1)} %get-tuple-element.20), channel_id=1, source_target_pairs={{0,12},{4,8},{8,4},{12,0},{16,28},{20,24},{24,20},{28,16},{1,13},{... | collective-permute-start | bytes 393224 | tf_op jit(solution)/shard_map/ppermute | solution.py:162
  45.7 8.4 %collective-permute-start.9 = (bf16[4,128,128]{2,1,0:T(8,128)(2,1)S(1)}, bf16[4,128,128]{2,1,0:T(8,128)(2,1)S(1)}, u32[]{:S(2)}, u32[]{:S(2)}) collective-permute-start(bf16[4,128,128]{2,1,0:T(8,128)(2,1)S(1)} %get-tuple-element.19), channel_id=1, source_target_pairs={{0,4},{4,0},{8,12},{12,8},{16,20},{20,16},{24,28},{28,24},{1,5},{5... | collective-permute-start | bytes 393224 | tf_op jit(solution)/shard_map/ppermute | solution.py:162
  50.2 16.2 %copy-start.3 = (bf16[128,256]{1,0:T(8,128)(2,1)S(1)}, bf16[128,256]{1,0:T(8,128)(2,1)}, u32[]{:S(2)}) copy-start(bf16[128,256]{1,0:T(8,128)(2,1)} %param.11) | copy-start | bytes 196612
  50.2 5.8 %collective-permute-start.5 = (bf16[4,128,128]{2,1,0:T(8,128)(2,1)S(1)}, bf16[4,128,128]{2,1,0:T(8,128)(2,1)S(1)}, u32[]{:S(2)}, u32[]{:S(2)}) collective-permute-start(bf16[4,128,128]{2,1,0:T(8,128)(2,1)S(1)} %slice.212), channel_id=1, source_target_pairs={{0,4},{4,0},{8,12},{12,8},{16,20},{20,16},{24,28},{28,24},{1,5},{5... | collective-permute-start | bytes 393224 | tf_op jit(solution)/shard_map/ppermute | solution.py:162
  54.2 4.3 %collective-permute-start.12 = (bf16[2,128,128]{2,1,0:T(8,128)(2,1)S(1)}, bf16[2,128,128]{2,1,0:T(8,128)(2,1)S(1)}, u32[]{:S(2)}, u32[]{:S(2)}) collective-permute-start(bf16[2,128,128]{2,1,0:T(8,128)(2,1)S(1)} %slice.213), channel_id=1, source_target_pairs={{0,2},{1,3},{2,0},{3,1},{4,6},{5,7},{6,4},{7,5},{8,10},{9,11},{10,... | collective-permute-start | bytes 196616 | tf_op jit(solution)/shard_map/ppermute | solution.py:162
  56.0 5.4 %collective-permute-start.6 = (bf16[2,128,128]{2,1,0:T(8,128)(2,1)S(1)}, bf16[2,128,128]{2,1,0:T(8,128)(2,1)S(1)}, u32[]{:S(2)}, u32[]{:S(2)}) collective-permute-start(bf16[2,128,128]{2,1,0:T(8,128)(2,1)S(1)} %slice.214), channel_id=1, source_target_pairs={{0,8},{4,12},{8,0},{12,4},{16,24},{20,28},{24,16},{28,20},{1,9},{5... | collective-permute-start | bytes 196616 | tf_op jit(solution)/shard_map/ppermute | solution.py:162
  58.5 5.2 %collective-permute-start.13 = (bf16[1,128,128]{2,1,0:T(8,128)(2,1)S(1)}, bf16[1,128,128]{2,1,0:T(8,128)(2,1)S(1)}, u32[]{:S(2)}, u32[]{:S(2)}) collective-permute-start(bf16[1,128,128]{2,1,0:T(8,128)(2,1)S(1)} %slice.215), channel_id=1, source_target_pairs={{0,16},{4,20},{8,24},{12,28},{16,0},{20,4},{24,8},{28,12},{1,17},{... | collective-permute-start | bytes 98312 | tf_op jit(solution)/shard_map/ppermute | solution.py:162
  61.4 4.9 %collective-permute-start.7 = (bf16[1,128,128]{2,1,0:T(8,128)(2,1)S(1)}, bf16[1,128,128]{2,1,0:T(8,128)(2,1)S(1)}, u32[]{:S(2)}, u32[]{:S(2)}) collective-permute-start(bf16[1,128,128]{2,1,0:T(8,128)(2,1)S(1)} %slice.216), channel_id=1, source_target_pairs={{0,16},{4,20},{8,24},{12,28},{16,0},{20,4},{24,8},{28,12},{1,17},{... | collective-permute-start | bytes 98312 | tf_op jit(solution)/shard_map/ppermute | solution.py:162
  67.1 5.0 %collective-permute-start.14 = (bf16[128,128]{1,0:T(8,128)(2,1)S(1)}, bf16[128,128]{1,0:T(8,128)(2,1)S(1)}, u32[]{:S(2)}, u32[]{:S(2)}) collective-permute-start(bf16[128,128]{1,0:T(8,128)(2,1)S(1)} %get-tuple-element.37), channel_id=1, source_target_pairs={{0,16},{4,20},{8,24},{12,28},{16,0},{20,4},{24,8},{28,12},{1,17},{... | collective-permute-start | bytes 98312 | tf_op jit(solution)/shard_map/ppermute | solution.py:162
  68.6 7.1 %collective-permute-start.19 = (bf16[128,128]{1,0:T(8,128)(2,1)S(1)}, bf16[128,128]{1,0:T(8,128)(2,1)S(1)}, u32[]{:S(2)}, u32[]{:S(2)}) collective-permute-start(bf16[128,128]{1,0:T(8,128)(2,1)S(1)} %get-tuple-element.36), channel_id=1, source_target_pairs={{0,16},{4,20},{8,24},{12,28},{16,0},{20,4},{24,8},{28,12},{1,17},{... | collective-permute-start | bytes 98312 | tf_op jit(solution)/shard_map/ppermute | solution.py:162
  72.1 4.3 %collective-permute-start.15 = (bf16[2,128,128]{2,1,0:T(8,128)(2,1)S(1)}, bf16[2,128,128]{2,1,0:T(8,128)(2,1)S(1)}, u32[]{:S(2)}, u32[]{:S(2)}) collective-permute-start(bf16[2,128,128]{2,1,0:T(8,128)(2,1)S(1)} %get-tuple-element.33), channel_id=1, source_target_pairs={{0,4},{4,0},{8,12},{12,8},{16,20},{20,16},{24,28},{28,24},{1,5},{5... | collective-permute-start | bytes 196616 | tf_op jit(solution)/shard_map/ppermute | solution.py:162
  73.3 4.5 %collective-permute-start.16 = (bf16[2,128,128]{2,1,0:T(8,128)(2,1)S(1)}, bf16[2,128,128]{2,1,0:T(8,128)(2,1)S(1)}, u32[]{:S(2)}, u32[]{:S(2)}) collective-permute-start(bf16[2,128,128]{2,1,0:T(8,128)(2,1)S(1)} %get-tuple-element.33), channel_id=1, source_target_pairs={{0,8},{4,12},{8,0},{12,4},{16,24},{20,28},{24,16},{28,20},{1,9},{5... | collective-permute-start | bytes 196616 | tf_op jit(solution)/shard_map/ppermute | solution.py:162
  75.3 6.0 %collective-permute-start.17 = (bf16[2,128,128]{2,1,0:T(8,128)(2,1)S(1)}, bf16[2,128,128]{2,1,0:T(8,128)(2,1)S(1)}, u32[]{:S(2)}, u32[]{:S(2)}) collective-permute-start(bf16[2,128,128]{2,1,0:T(8,128)(2,1)S(1)} %get-tuple-element.33), channel_id=1, source_target_pairs={{0,12},{4,8},{8,4},{12,0},{16,28},{20,24},{24,20},{28,16},{1,13},{... | collective-permute-start | bytes 196616 | tf_op jit(solution)/shard_map/ppermute | solution.py:162
  75.7 6.4 %collective-permute-start.20 = (bf16[2,128,128]{2,1,0:T(8,128)(2,1)S(1)}, bf16[2,128,128]{2,1,0:T(8,128)(2,1)S(1)}, u32[]{:S(2)}, u32[]{:S(2)}) collective-permute-start(bf16[2,128,128]{2,1,0:T(8,128)(2,1)S(1)} %get-tuple-element.39), channel_id=1, source_target_pairs={{0,2},{1,3},{2,0},{3,1},{4,6},{5,7},{6,4},{7,5},{8,10},{9,11},{10,... | collective-permute-start | bytes 196616 | tf_op jit(solution)/shard_map/ppermute | solution.py:162
  81.3 8.8 %collective-permute-start.18 = (bf16[4,2,128,128]{3,2,1,0:T(8,128)(2,1)S(1)}, bf16[4,2,128,128]{3,2,1,0:T(8,128)(2,1)S(1)}, u32[]{:S(2)}, u32[]{:S(2)}) collective-permute-start(bf16[4,2,128,128]{3,2,1,0:T(8,128)(2,1)S(1)} %pad_maximum_fusion.2), channel_id=1, source_target_pairs={{0,2},{1,3},{2,0},{3,1},{4,6},{5,7},{6,4},{7,5},{8,10},{9,11},{10,... | collective-permute-start | bytes 786440 | tf_op jit(solution)/shard_map/ppermute | solution.py:162
  82.1 5.0 %collective-permute-start.21 = (bf16[2,2,128,128]{3,2,1,0:T(8,128)(2,1)S(1)}, bf16[2,2,128,128]{3,2,1,0:T(8,128)(2,1)S(1)}, u32[]{:S(2)}, u32[]{:S(2)}) collective-permute-start(bf16[2,2,128,128]{3,2,1,0:T(8,128)(2,1)S(1)} %get-tuple-element.27), channel_id=1, source_target_pairs={{0,4},{4,0},{8,12},{12,8},{16,20},{20,16},{24,28},{28,24},{1,5},{5... | collective-permute-start | bytes 393224 | tf_op jit(solution)/shard_map/ppermute | solution.py:162
  82.1 5.0 %collective-permute-start.22 = (bf16[2,2,128,128]{3,2,1,0:T(8,128)(2,1)S(1)}, bf16[2,2,128,128]{3,2,1,0:T(8,128)(2,1)S(1)}, u32[]{:S(2)}, u32[]{:S(2)}) collective-permute-start(bf16[2,2,128,128]{3,2,1,0:T(8,128)(2,1)S(1)} %get-tuple-element.27), channel_id=1, source_target_pairs={{0,8},{4,12},{8,0},{12,4},{16,24},{20,28},{24,16},{28,20},{1,9},{5... | collective-permute-start | bytes 393224 | tf_op jit(solution)/shard_map/ppermute | solution.py:162
  84.0 6.0 %collective-permute-start.23 = (bf16[2,2,128,128]{3,2,1,0:T(8,128)(2,1)S(1)}, bf16[2,2,128,128]{3,2,1,0:T(8,128)(2,1)S(1)}, u32[]{:S(2)}, u32[]{:S(2)}) collective-permute-start(bf16[2,2,128,128]{3,2,1,0:T(8,128)(2,1)S(1)} %get-tuple-element.27), channel_id=1, source_target_pairs={{0,12},{4,8},{8,4},{12,0},{16,28},{20,24},{24,20},{28,16},{1,13},{... | collective-permute-start | bytes 393224 | tf_op jit(solution)/shard_map/ppermute | solution.py:162
  90.1 2.0 %collective-permute-start.25 = (bf16[2048,128]{1,0:T(8,128)(2,1)S(1)}, bf16[2048,128]{1,0:T(8,128)(2,1)S(1)}, u32[]{:S(2)}, u32[]{:S(2)}) collective-permute-start(bf16[2048,128]{1,0:T(8,128)(2,1)S(1)} %bitcast.95), channel_id=1, source_target_pairs={{0,1},{1,0},{2,3},{3,2},{4,5},{5,4},{6,7},{7,6},{8,9},{9,8},{10,11... | collective-permute-start | bytes 1572872 | tf_op jit(solution)/shard_map/ppermute | solution.py:162
  90.3 2.6 %collective-permute-start.24 = (bf16[2048,128]{1,0:T(8,128)(2,1)S(1)}, bf16[2048,128]{1,0:T(8,128)(2,1)S(1)}, u32[]{:S(2)}, u32[]{:S(2)}) collective-permute-start(bf16[2048,128]{1,0:T(8,128)(2,1)S(1)} %bitcast.97), channel_id=1, source_target_pairs={{0,1},{1,0},{2,3},{3,2},{4,5},{5,4},{6,7},{7,6},{8,9},{9,8},{10,11... | collective-permute-start | bytes 1572872 | tf_op jit(solution)/shard_map/ppermute | solution.py:162
  93.5 4.9 %collective-permute-start.26 = (bf16[192,256]{1,0:T(8,128)(2,1)S(1)}, bf16[192,256]{1,0:T(8,128)(2,1)S(1)}, u32[]{:S(2)}, u32[]{:S(2)}) collective-permute-start(bf16[192,256]{1,0:T(8,128)(2,1)S(1)} %get-tuple-element.25), channel_id=1, source_target_pairs={{0,4},{4,0},{8,12},{12,8},{16,20},{20,16},{24,28},{28,24},{1,5},{5... | collective-permute-start | bytes 294920 | tf_op jit(solution)/shard_map/ppermute | solution.py:162
  93.6 4.8 %collective-permute-start.29 = (bf16[192,256]{1,0:T(8,128)(2,1)S(1)}, bf16[192,256]{1,0:T(8,128)(2,1)S(1)}, u32[]{:S(2)}, u32[]{:S(2)}) collective-permute-start(bf16[192,256]{1,0:T(8,128)(2,1)S(1)} %get-tuple-element.24), channel_id=1, source_target_pairs={{0,8},{4,12},{8,0},{12,4},{16,24},{20,28},{24,16},{28,20},{1,9},{5... | collective-permute-start | bytes 294920 | tf_op jit(solution)/shard_map/ppermute | solution.py:162
  98.5 7.1 %collective-permute-start.30 = (bf16[192,256]{1,0:T(8,128)(2,1)S(1)}, bf16[192,256]{1,0:T(8,128)(2,1)S(1)}, u32[]{:S(2)}, u32[]{:S(2)}) collective-permute-start(bf16[192,256]{1,0:T(8,128)(2,1)S(1)} %get-tuple-element.22), channel_id=1, source_target_pairs={{0,16},{4,20},{8,24},{12,28},{16,0},{20,4},{24,8},{28,12},{1,17},{... | collective-permute-start | bytes 294920 | tf_op jit(solution)/shard_map/ppermute | solution.py:162
  100.2 6.8 %collective-permute-start.27 = (bf16[192,256]{1,0:T(8,128)(2,1)S(1)}, bf16[192,256]{1,0:T(8,128)(2,1)S(1)}, u32[]{:S(2)}, u32[]{:S(2)}) collective-permute-start(bf16[192,256]{1,0:T(8,128)(2,1)S(1)} %get-tuple-element.23), channel_id=1, source_target_pairs={{0,8},{4,12},{8,0},{12,4},{16,24},{20,28},{24,16},{28,20},{1,9},{5... | collective-permute-start | bytes 294920 | tf_op jit(solution)/shard_map/ppermute | solution.py:162
  105.6 4.7 %collective-permute-start.31 = (bf16[192,256]{1,0:T(8,128)(2,1)S(1)}, bf16[192,256]{1,0:T(8,128)(2,1)S(1)}, u32[]{:S(2)}, u32[]{:S(2)}) collective-permute-start(bf16[192,256]{1,0:T(8,128)(2,1)S(1)} %add_convert_fusion), channel_id=1, source_target_pairs={{0,4},{4,0},{8,12},{12,8},{16,20},{20,16},{24,28},{28,24},{1,5},{5... | collective-permute-start | bytes 294920 | tf_op jit(solution)/shard_map/ppermute | solution.py:162
  107.0 5.9 %collective-permute-start.28 = (bf16[192,256]{1,0:T(8,128)(2,1)S(1)}, bf16[192,256]{1,0:T(8,128)(2,1)S(1)}, u32[]{:S(2)}, u32[]{:S(2)}) collective-permute-start(bf16[192,256]{1,0:T(8,128)(2,1)S(1)} %add_convert_fusion.2), channel_id=1, source_target_pairs={{0,16},{4,20},{8,24},{12,28},{16,0},{20,4},{24,8},{28,12},{1,17},{... | collective-permute-start | bytes 294920 | tf_op jit(solution)/shard_map/ppermute | solution.py:162
